TPU v7x, 128 devices: a whole 4x4x4 slice. The times are simulated.
128 devices in a mesh: seq: 4 (over z), mem: 32 (over x, y, core).
Axes of the slice: x: 4, y: 4, z: 4, core: 2. Of those that a mesh axis runs over, the one named last changes fastest.
Arguments:
- queries: bfloat16 [32, 512, 1024], P('mem', 'seq'), may hold values from -24 to 24
- keys: bfloat16 [32, 512, 1024], P('mem', 'seq'), may hold values from -8 to 8
- values: bfloat16 [32, 512, 1024], P('mem', 'seq'), may hold values from -6 to 6
- mem_keys: bfloat16 [65536, 1024], P(('seq', 'mem')), may hold values from -8 to 8
- mem_values: bfloat16 [65536, 1024], P(('seq', 'mem')), may hold values from -6 to 6
- knn_index: int32 [32, 512, 8, 32], P('mem', 'seq'), may hold values from 0 to 65535, as said below
- block_slot: int32 [1024], replicated, may hold values from 0 to 1023, as said below
- gate_bias: float32 [8], replicated, may hold values from -2 to 2
- w_out: bfloat16 [1024, 2048], replicated, may hold values from -0.1875 to 0.1875
Outputs:
- mixed: bfloat16 [32, 512, 2048], P('mem', 'seq')
Inputs may be any that keep to these rules, and one draw needn't show every extreme that they name: `block_slot`: A permutation of the 1024 blocks. Storage row q lies on device q // 512 of seq+mem (seq slowest). `knn_index`: counting the lookups of one device (its tokens, all heads and ranks) by the device that stores the row, no device gets more than 384; some device gets exactly 384 from every device. Rows of one list may repeat.
All inputs are finite; a program needn't handle non-finite values.
Results may differ from a plain program's by a relative error of at most 0.011.
Values may be sent and summed in bfloat16 or wider, within the bound.
No kernel may reach another device: no remote copies, remote signals or barrier semaphores. Data moves between devices by JAX's collectives and lax.ppermute only.
A program may use at most 128 MiB of HBM per device.

v0:
```python
import jax
import jax.numpy as jnp
from jax import lax
from jax.sharding import PartitionSpec as P

BLK_DEV = 8


def shards(queries, keys, values, mem_keys, mem_values, knn_index, block_slot, gate_bias, w_out):
    tok = queries.shape[1]
    width = queries.shape[2]
    heads = gate_bias.shape[0]
    head = width // heads
    topk = knn_index.shape[3]
    mem_dev = mem_keys.shape[0]
    seq_count = lax.axis_size("seq")
    mem_count = lax.axis_size("mem")
    devices = seq_count * mem_count
    block = mem_dev // BLK_DEV
    capacity = 3 * (tok * heads * topk // devices) // 2
    scale = head ** (-0.5)
    whole_keys, whole_values = (
        lax.all_gather(keys, "seq", axis=1, tiled=True),
        lax.all_gather(values, "seq", axis=1, tiled=True),
    )
    query = queries[0].reshape(tok, heads, head)
    span = whole_keys.shape[1]
    key_rows = whole_keys[0].reshape(span, heads, head)
    value_rows = whole_values[0].reshape(span, heads, head)
    scores = jnp.einsum("qhd,khd->hqk", query, key_rows, preferred_element_type=jnp.float32) * scale
    query_pos = lax.axis_index("seq") * tok + jnp.arange(tok, dtype=jnp.int32)
    key_pos = jnp.arange(span, dtype=jnp.int32)
    scores = jnp.where(key_pos[None, None, :] <= query_pos[None, :, None], scores, -jnp.inf)
    probs = jax.nn.softmax(scores, axis=-1).astype(jnp.bfloat16)
    local_out = jnp.einsum("hqk,khd->qhd", probs, value_rows, preferred_element_type=jnp.float32)
    total = tok * heads * topk
    lookups = knn_index[0].reshape(total)
    head_of = jnp.arange(total, dtype=jnp.int32) // topk % heads
    storage = jnp.take(block_slot, lookups // block) * block + lookups % block
    owner = storage // mem_dev
    code = storage % mem_dev * heads + head_of
    one_hot = (owner[:, None] == jnp.arange(devices, dtype=jnp.int32)[None, :]).astype(jnp.int32)
    running = jnp.cumsum(one_hot, axis=0)
    rank = jnp.sum(one_hot * running, axis=1) - 1
    slot_of = owner * capacity + rank
    requests = jnp.zeros((devices * capacity,), jnp.int32).at[slot_of].set(code)
    requests = requests.reshape(devices, capacity)
    table = jnp.concatenate(
        [mem_keys.reshape(mem_dev * heads, head), mem_values.reshape(mem_dev * heads, head)], axis=1
    )
    replies = lax.all_to_all(
        jnp.take(
            table,
            lax.all_to_all(requests, ("seq", "mem"), split_axis=0, concat_axis=0, tiled=True),
            axis=0,
        ),
        ("seq", "mem"),
        split_axis=0,
        concat_axis=0,
        tiled=True,
    )
    fetched = jnp.take(replies.reshape(devices * capacity, 2 * head), slot_of, axis=0)
    fetched = fetched.reshape(tok, heads, topk, 2 * head)
    mem_k = fetched[..., :head]
    mem_v = fetched[..., head:]
    mem_scores = (
        jnp.einsum("thd,thkd->thk", query, mem_k, preferred_element_type=jnp.float32) * scale
    )
    mem_probs = jax.nn.softmax(mem_scores, axis=-1).astype(jnp.bfloat16)
    mem_out = jnp.einsum("thk,thkd->thd", mem_probs, mem_v, preferred_element_type=jnp.float32)
    gate = jax.nn.sigmoid(gate_bias)[None, :, None]
    combined = (gate * mem_out + (1.0 - gate) * local_out).astype(jnp.bfloat16).reshape(tok, width)
    mixed = jnp.dot(combined, w_out, preferred_element_type=jnp.float32).astype(jnp.bfloat16)
    return mixed[None]


def solution(mesh):
    return jax.shard_map(
        shards,
        mesh=mesh,
        in_specs=(
            P("mem", "seq", None),
            P("mem", "seq", None),
            P("mem", "seq", None),
            P(("seq", "mem"), None),
            P(("seq", "mem"), None),
            P("mem", "seq", None, None),
            P(),
            P(),
            P(),
        ),
        out_specs=P("mem", "seq", None),
        check_vma=False,
    )
```

profile of v0, /device:TPU:1, one launch (start us, length us, event | category | flops | bytes accessed | tf_op | source)
XLA Modules:
  0.0 1069.2 jit_solution(14462346384990772915)
XLA Ops:
  9.0 130.0 %gather_fusion = s32[32768]{0:T(1024)S(1)} fusion(s32[1024]{0:T(1024)S(1)} %copy-done, s32[32768]{0:T(1024)S(1)} %broadcast_clamp_fusion.2), kind=kCustom, calls=%fused_computation | custom fusion | bytes 393216 | tf_op jit(solution)/shard_map/jit(_take)/gather | solution.py:39
  139.4 7.4 fusion.4
  148.3 12.3 %broadcast_add_fusion = s32[128,256,128]{1,0,2:T(8,128)} fusion(s32[128,256,128]{1,0,2:T(8,128)} %fusion.4, s32[128,256]{1,0:T(8,128)S(1)} %copy.47), kind=kLoop, calls=%fused_computation.18 | loop fusion | flops 4194304 | bytes 33685504 | tf_op jit(solution)/shard_map/reduce_window_sum
  160.6 18.0 %copy.48 = s32[128,256,128]{0,2,1:T(8,128)} copy(s32[128,256,128]{1,0,2:T(8,128)} %broadcast_add_fusion) | data formatting | bytes 33554432 | tf_op jit(solution)/shard_map/reduce_window_sum
  178.9 11.8 %fusion.3 = s32[32768]{0:T(1024)S(1)} fusion(s32[128,256,128]{0,2,1:T(8,128)} %copy.48, s32[32768]{0:T(1024)S(1)} %add_select_fusion.9), kind=kLoop, calls=%fused_computation.9 | loop fusion | flops 12550144 | bytes 17039360 | tf_op jit(solution)/shard_map/reduce_sum | solution.py:44
  191.3 1.9 compare_select_fusion.3
  193.3 120.8 %scatter_custom_fusion = s32[49152]{0:T(1024)} fusion(s32[32768]{0:T(1024)S(1)} %bitcast.101, s32[32768]{0:T(1024)S(1)} %get-tuple-element.7, s32[]{:T(128)} %constant.125.clone.1), kind=kCustom, calls=%fused_computation.131 | custom fusion | bytes 196612 | tf_op jit(solution)/shard_map/scatter | solution.py:46
  314.0 11.5 %all-to-all-start = ((s32[128,1,384]{2,1,0:T(1,128)}), s32[128,1,384]{2,1,0:T(1,128)S(1)}, u32[]{:S(2)}, u32[]{:S(2)}) async-start(s32[128,1,384]{2,1,0:T(1,128)} %bitcast.10), calls=%async_computation | async-start | bytes 393216 | tf_op jit(solution)/shard_map/all_to_all | solution.py:54
  326.1 2.3 reshape.374
  328.4 1.6 pad_maximum_fusion
  330.0 6.1 all-to-all-done
  336.3 192.5 %gather_fusion.1 = bf16[49152,256]{1,0:T(8,128)(2,1)} fusion(bf16[4096,256]{1,0:T(8,128)(2,1)S(1)} %pad_maximum_fusion, s32[49152]{0:T(1024)S(1)} %broadcast_clamp_fusion), kind=kCustom, calls=%fused_computation.1 | custom fusion | bytes 50528256 | tf_op jit(solution)/shard_map/jit(_take)/gather | solution.py:52
  528.9 17.2 %broadcast_select_fusion = bf16[128,384,256]{2,1,0:T(8,128)(2,1)} fusion(bf16[128,384,256]{2,1,0:T(8,128)(2,1)} %bitcast.90, pred[128,384]{1,0:T(8,128)(4,1)S(1)} %compare_and_fusion.1), kind=kLoop, calls=%fused_computation.7 | loop fusion | flops 12582912 | bytes 50380800 | tf_op jit(solution)/shard_map/jit(_take)/select_n | solution.py:52
  546.2 5.6 all-to-all-start.1
  555.4 148.0 %all-gather.5.cloned.1.call-done = bf16[1,512,1024]{2,1,0:T(8,128)(2,1)} async-done(((bf16[1,128,1024]{2,1,0:T(8,128)(2,1)}), bf16[1,512,1024]{2,1,0:T(8,128)(2,1)}) %all-gather.5.cloned.1.call-update) | async-done | bytes 1048592 | tf_op jit(solution)/shard_map/all_gather | solution.py:24
  705.0 128.8 %all-gather.3.cloned.1.call-done = bf16[1,512,1024]{1,2,0:T(8,128)(2,1)} async-done(((bf16[1,128,1024]{1,2,0:T(8,128)(2,1)}), bf16[1,512,1024]{1,2,0:T(8,128)(2,1)}) %all-gather.3.cloned.1.call-update) | async-done | bytes 1048592 | tf_op jit(solution)/shard_map/all_gather | solution.py:23
  833.8 3.4 fusion.64
  837.1 59.6 %all-to-all-done.1 = bf16[128,384,256]{2,1,0:T(8,128)(2,1)} async-done(((bf16[128,384,256]{2,1,0:T(8,128)(2,1)}), bf16[128,384,256]{2,1,0:T(8,128)(2,1)}, u32[]{:S(2)}, u32[]{:S(2)}) %all-to-all-start.1) | async-done | bytes 25165856 | tf_op jit(solution)/shard_map/all_to_all | solution.py:51
  896.7 132.1 %gather_fusion.2 = bf16[32768,256]{1,0:T(8,128)(2,1)} fusion(bf16[49152,256]{1,0:T(8,128)(2,1)} %bitcast.14, s32[32768]{0:T(1024)S(1)} %broadcast_clamp_fusion.1), kind=kCustom, calls=%fused_computation.2 | custom fusion | bytes 33685504 | tf_op jit(solution)/shard_map/jit(_take)/gather | solution.py:62
  1028.8 11.9 %broadcast_select_fusion.1 = bf16[128,8,32,256]{3,2,1,0:T(8,128)(2,1)} fusion(bf16[128,8,32,256]{3,2,1,0:T(8,128)(2,1)} %bitcast.91, pred[128,8,32]{2,1,0:T(8,128)(4,1)S(1)} %compare_and_fusion), kind=kLoop, calls=%fused_computation.15 | loop fusion | flops 8388608 | bytes 33587200 | tf_op jit(solution)/shard_map/jit(_take)/select_n | solution.py:62
  1040.7 7.8 fusion.6
  1049.2 7.1 multiply_reduce_fusion
  1056.5 2.2 fusion.13
  1058.7 3.7 fusion.9
  (70 shorter events, 11.8 us)
Async XLA Ops:
  6.5 2.5 copy-start
  7.7 131.4 %copy-start.2 = (s32[1,128,8,32]{3,2,1,0:T(8,128)}, s32[1,128,8,32]{3,2,1,0:T(8,128)S(1)}, u32[]{:S(2)}) copy-start(s32[1,128,8,32]{3,2,1,0:T(8,128)S(1)} %copy.40) | copy-start | bytes 393220
  178.6 147.0 %copy-start.7 = (bf16[512,1024]{1,0:T(8,128)(2,1)S(1)}, bf16[512,1024]{1,0:T(8,128)(2,1)}, u32[]{:S(2)}) copy-start(bf16[512,1024]{1,0:T(8,128)(2,1)} %param.12) | copy-start | bytes 3145732
  190.7 0.7 copy-start.4
  193.3 132.8 %copy-start.8 = (s32[32768,1]{0,1:T(1,128)}, s32[32768,1]{0,1:T(1,128)S(1)}, u32[]{:S(2)}) copy-start(s32[32768,1]{0,1:T(1,128)S(1)} %compare_select_fusion.3) | copy-start | bytes 393220
  314.0 22.0 %all-to-all-start = ((s32[128,1,384]{2,1,0:T(1,128)}), s32[128,1,384]{2,1,0:T(1,128)S(1)}, u32[]{:S(2)}, u32[]{:S(2)}) async-start(s32[128,1,384]{2,1,0:T(1,128)} %bitcast.10), calls=%async_computation | async-start | bytes 393216 | tf_op jit(solution)/shard_map/all_to_all | solution.py:54
  546.1 6.5 copy-start.10
  546.1 7.3 copy-start.5
  546.1 7.7 copy-start.6
  546.1 8.0 copy-start.11
  546.1 8.1 copy-start.3
  546.2 9.2 copy-start.9
  546.2 350.5 %all-to-all-start.1 = ((bf16[128,384,256]{2,1,0:T(8,128)(2,1)}), bf16[128,384,256]{2,1,0:T(8,128)(2,1)}, u32[]{:S(2)}, u32[]{:S(2)}) async-start(bf16[128,384,256]{2,1,0:T(8,128)(2,1)} %broadcast_select_fusion), calls=%async_computation.1 | async-start | bytes 50331648 | tf_op jit(solution)/shard_map/all_to_all | solution.py:51
  551.8 151.7 %all-gather.5.cloned.1.call-start = ((), (), s32[]{:S(2)}) async-start(), calls=%async_computation.3 | async-start | bytes 1310720 | tf_op jit(solution)/shard_map/all_gather | solution.py:24
  552.5 281.3 %all-gather.3.cloned.1.call-start = ((), (), s32[]{:S(2)}) async-start(), calls=%async_computation.2 | async-start | bytes 1310720 | tf_op jit(solution)/shard_map/all_gather | solution.py:23
  1028.8 33.6 %copy-start.1 = (s32[1024]{0:T(1024)S(1)}, s32[1024]{0:T(1024)}, u32[]{:S(2)}) copy-start(s32[1024]{0:T(1024)} %param.15) | copy-start | bytes 12292
Sparse Core Ops, SparseCore 0:
  554.3 149.1 all-gather.4
  705.1 128.6 all-gather.2
where the time goes:
time: 1080 us; the launch traced here: 1070 us
  local copies, waits for them, and re-layouts  604 us (56%)
  waiting for transfers between devices  343 us (32%)
  other arithmetic  74.2 us (7%)
  starting transfers between devices  17.2 us (2%)
  matrix products  17 us (2%)
  between operations  13.9 us (1%)
    gather x1, local copies, waits for them, and re-layouts, shards(): jnp.take(table, lax.all_to_all(requests, ('seq', 'mem'), split_axis=0, co...  193 us
    all_gather x1, waiting for transfers between devices, shards(): lax.all_gather(values, 'seq', axis=1, tiled=True)  148 us
    gather x1, local copies, waits for them, and re-layouts, shards(): jnp.take(replies.reshape(devices * capacity, 2 * head), slot_of, axis=0)  132 us
    gather x2, local copies, waits for them, and re-layouts, shards(): storage = jnp.take(block_slot, lookups // block) * block + lookups % block  130 us
    all_gather x1, waiting for transfers between devices, shards(): lax.all_gather(keys, 'seq', axis=1, tiled=True)  129 us
    scatter x1, local copies, waits for them, and re-layouts, shards(): requests = jnp.zeros((devices * capacity,), jnp.int32).at[slot_of].set(code)  121 us
    all_to_all x1, waiting for transfers between devices, shards(): lax.all_to_all(jnp.take(table, lax.all_to_all(requests, ('seq', 'mem'), s...  59.6 us
  transfers between devices with their start and end apart: 4, of which 4 were waited for; matrix products, arithmetic and copies ran while one was open for 1% of the time, Pallas kernels for 0%

commit v1 on v0

v1 whole, which is shorter than its diff:
```python
import functools

import jax
import jax.numpy as jnp
from jax import lax
from jax.experimental import pallas as pl
from jax.experimental.pallas import tpu as pltpu
from jax.sharding import PartitionSpec as P

DEVS = 128
TOK = 128
HEADS = 8
HEAD = 128
TOPK = 32
MEM_DEV = 512
BLOCK = 64
CAP = 384
PART = 128
PARTS = CAP // PART
GROUP = 8
BATCH = 8
ROWS = 256
NT = (((1,), (1,)), ((), ()))


def one_hot(mask):
    return jnp.where(mask, 1.0, 0.0).astype(jnp.bfloat16)


def route_kernel(look_ref, slot_ref, req_ref, store, total, slots, parts):
    table = [jnp.broadcast_to(slot_ref[r : r + 1, :], (8, 128)) for r in range(8)]

    def translate(i, carry):
        base = pl.multiple_of(i * 8, 8)
        for half in range(ROWS // 128):
            look = look_ref[pl.ds(base, 8), half * 128 : (half + 1) * 128]
            blk = look >> 6
            low = blk & 127
            high = blk >> 7
            place = jnp.zeros((8, 128), jnp.int32)
            for r in range(8):
                place = jnp.where(high == r, jnp.take_along_axis(table[r], low, axis=1), place)
            store[pl.ds(base, 8), half * 128 : (half + 1) * 128] = place * BLOCK + (look & (BLOCK - 1))
        return carry

    lax.fori_loop(0, look_ref.shape[0] // 8, translate, 0)
    total[...] = jnp.zeros_like(total)
    upper = one_hot(
        lax.broadcasted_iota(jnp.int32, (ROWS, ROWS), 0) <= lax.broadcasted_iota(jnp.int32, (ROWS, ROWS), 1)
    )
    owners = lax.broadcasted_iota(jnp.int32, (DEVS, ROWS), 0)
    ranks = lax.broadcasted_iota(jnp.int32, (CAP, ROWS), 0)
    lane = lax.broadcasted_iota(jnp.int32, (1, ROWS), 1)
    batch = BATCH
    per_head = TOK * TOPK // ROWS

    def place(i, run):
        base = pl.multiple_of(i * batch, batch)
        rows = store[pl.ds(base, batch), :]
        for b in range(batch):
            row = base + b
            head = row // per_head
            tok = (row % per_head) * (ROWS // TOPK) + lane // TOPK
            here = rows[b : b + 1, :]
            mine = jnp.where(owners == here // MEM_DEV, 1.0, 0.0)
            count = jnp.dot(mine.astype(jnp.bfloat16), upper, preferred_element_type=jnp.float32) + run
            rank = jnp.sum(mine * count, axis=0, keepdims=True).astype(jnp.int32) - 1
            run = jnp.broadcast_to(count[:, ROWS - 1 :], (DEVS, ROWS))
            span = slice(b * ROWS, (b + 1) * ROWS)
            slots[:, span] = one_hot(ranks == rank)
            local = here & (MEM_DEV - 1)
            first = (local & 255).astype(jnp.float32)
            second = ((local >> 8) + 2 * tok).astype(jnp.float32)
            parts[0:DEVS, span] = (mine * first).astype(jnp.bfloat16)
            parts[DEVS : 2 * DEVS, span] = (mine * second).astype(jnp.bfloat16)
            parts[2 * DEVS :, span] = (mine * (head + 1).astype(jnp.float32)).astype(jnp.bfloat16)
        total[...] += lax.dot_general(parts[...], slots[...], NT, preferred_element_type=jnp.float32)
        return run

    lax.fori_loop(0, look_ref.shape[0] // batch, place, jnp.zeros((DEVS, ROWS), jnp.float32))
    first = total[0:DEVS, :].astype(jnp.int32)
    second = total[DEVS : 2 * DEVS, :].astype(jnp.int32)
    third = total[2 * DEVS :, :].astype(jnp.int32)
    local = first + (second & 1) * 256
    query = (third - 1) * TOK + (second >> 1)
    req_ref[...] = jnp.where(third > 0, query * MEM_DEV + local, -1)


def route(lookups, block_slot):
    return pl.pallas_call(
        route_kernel,
        out_shape=jax.ShapeDtypeStruct((DEVS, CAP), jnp.int32),
        scratch_shapes=[
            pltpu.VMEM((TOK * HEADS * TOPK // ROWS, ROWS), jnp.int32),
            pltpu.VMEM((3 * DEVS, CAP), jnp.float32),
            pltpu.VMEM((CAP, BATCH * ROWS), jnp.bfloat16),
            pltpu.VMEM((3 * DEVS, BATCH * ROWS), jnp.bfloat16),
        ],
        compiler_params=pltpu.CompilerParams(vmem_limit_bytes=32 * 1024 * 1024),
        name="route",
    )(lookups, block_slot.reshape(8, 128))


def pick_kernel(code_ref, mem_ref, out_ref, hot, head_of):
    code = jnp.transpose(code_ref[...])
    row_ids = lax.broadcasted_iota(jnp.int32, (PART, MEM_DEV), 1)
    for i in range(GROUP):
        col = code[:, i : i + 1]
        span = slice(i * PART, (i + 1) * PART)
        hot[span, :] = one_hot((col & (MEM_DEV - 1)) == row_ids)
        head_of[span, :] = jnp.broadcast_to(col >> 16, (PART, HEAD))
    for i in range(GROUP // 2):
        span = slice(i * 2 * PART, (i + 1) * 2 * PART)
        out = jnp.zeros((2 * PART, HEAD), jnp.float32)
        which = head_of[span, :]
        for pair in range(HEADS // 2):
            both = jnp.dot(
                hot[span, :], mem_ref[:, pair * 256 : (pair + 1) * 256], preferred_element_type=jnp.float32
            )
            out = jnp.where(which == 2 * pair, both[:, :HEAD], out)
            out = jnp.where(which == 2 * pair + 1, both[:, HEAD:], out)
        out_ref[2 * i : 2 * i + 2] = out.astype(jnp.bfloat16).reshape(2, PART, HEAD)


def pick(codes, mem, part):
    return pl.pallas_call(
        pick_kernel,
        grid=(DEVS // GROUP,),
        in_specs=[
            pl.BlockSpec((GROUP, PART), lambda g: (g, part)),
            pl.BlockSpec((MEM_DEV, HEADS * HEAD), lambda g: (0, 0)),
        ],
        out_specs=pl.BlockSpec((GROUP, PART, HEAD), lambda g: (g, 0, 0)),
        out_shape=jax.ShapeDtypeStruct((DEVS, PART, HEAD), jnp.bfloat16),
        scratch_shapes=[
            pltpu.VMEM((GROUP * PART, MEM_DEV), jnp.bfloat16),
            pltpu.VMEM((GROUP * PART, HEAD), jnp.int32),
        ],
        compiler_params=pltpu.CompilerParams(vmem_limit_bytes=32 * 1024 * 1024),
        name="pick",
    )(codes, mem)


def score_kernel(code_ref, query_ref, *refs):
    keys, out_ref = refs[:PARTS], refs[PARTS]
    step = pl.program_id(0)

    @pl.when(step == 0)
    def _():
        out_ref[...] = jnp.zeros_like(out_ref)

    tok_ids = lax.broadcasted_iota(jnp.int32, (PART, TOK), 1)
    lane = lax.broadcasted_iota(jnp.int32, (PART, DEVS), 1)
    for part in range(PARTS):
        code = jnp.transpose(code_ref[:, part * PART : (part + 1) * PART])
        acc = out_ref[part * PART : (part + 1) * PART, :]
        for i in range(GROUP):
            col = code[:, i : i + 1]
            which = jnp.broadcast_to(col >> 16, (PART, HEAD))
            hot = one_hot(((col >> 9) & (TOK - 1)) == tok_ids)
            query = jnp.zeros((PART, HEAD), jnp.float32)
            for pair in range(HEADS // 2):
                both = jnp.dot(
                    hot,
                    query_ref[i * TOK : (i + 1) * TOK, pair * 256 : (pair + 1) * 256],
                    preferred_element_type=jnp.float32,
                )
                query = jnp.where(which == 2 * pair, both[:, :HEAD], query)
                query = jnp.where(which == 2 * pair + 1, both[:, HEAD:], query)
            score = jnp.sum(query * keys[part][i].astype(jnp.float32), axis=1, keepdims=True)
            acc = jnp.where(lane == step * GROUP + i, score * HEAD ** (-0.5), acc)
        out_ref[part * PART : (part + 1) * PART, :] = acc


def score(codes, queries, keys):
    return pl.pallas_call(
        score_kernel,
        grid=(DEVS // GROUP,),
        in_specs=[
            pl.BlockSpec((GROUP, CAP), lambda g: (g, 0)),
            pl.BlockSpec((GROUP * TOK, HEADS * HEAD), lambda g: (g, 0)),
        ]
        + [pl.BlockSpec((GROUP, PART, HEAD), lambda g: (g, 0, 0))] * PARTS,
        out_specs=pl.BlockSpec((CAP, DEVS), lambda g: (0, 0)),
        out_shape=jax.ShapeDtypeStruct((CAP, DEVS), jnp.float32),
        compiler_params=pltpu.CompilerParams(vmem_limit_bytes=48 * 1024 * 1024),
        name="score",
    )(codes, queries, *keys)


def weigh_kernel(code_ref, score_ref, out_ref, top):
    step = 128
    tiles = HEADS * TOK // step

    def best(h, carry):
        base = pl.multiple_of(h * step, step)
        ids = lax.broadcasted_iota(jnp.int32, (step, PART), 0) + h * step

        def look(g, acc):
            rows = pl.ds(pl.multiple_of(g * GROUP, GROUP), GROUP)
            for part in range(PARTS):
                span = slice(part * PART, (part + 1) * PART)
                query = code_ref[rows, span] >> 9
                score = score_ref[rows, span]
                for i in range(GROUP):
                    acc = jnp.maximum(acc, jnp.where(ids == query[i : i + 1], score[i : i + 1], -jnp.inf))
            return acc

        acc = lax.fori_loop(0, DEVS // GROUP, look, jnp.full((step, PART), -jnp.inf, jnp.float32))
        top[pl.ds(base, step), :] = jnp.broadcast_to(jnp.max(acc, axis=1, keepdims=True), (step, PART))
        return carry

    lax.fori_loop(0, tiles, best, 0)

    def shift(g, carry):
        rows = pl.ds(pl.multiple_of(g * GROUP, GROUP), GROUP)
        for part in range(PARTS):
            span = slice(part * PART, (part + 1) * PART)
            query = code_ref[rows, span] >> 9
            highs = []
            for i in range(GROUP):
                found = jnp.zeros((step, PART), jnp.float32)
                for h in range(tiles):
                    ids = lax.broadcasted_iota(jnp.int32, (step, PART), 0) + h * step
                    found = jnp.where(ids == query[i : i + 1], top[h * step : (h + 1) * step, :], found)
                highs.append(jnp.sum(found, axis=0, keepdims=True))
            high = jnp.concatenate(highs, axis=0)
            out_ref[rows, span] = jnp.where(query >= 0, jnp.exp(score_ref[rows, span] - high), 0.0)
        return carry

    lax.fori_loop(0, DEVS // GROUP, shift, 0)


def weigh(codes, scores):
    return pl.pallas_call(
        weigh_kernel,
        out_shape=jax.ShapeDtypeStruct((DEVS, CAP), jnp.float32),
        scratch_shapes=[pltpu.VMEM((HEADS * TOK, PART), jnp.float32)],
        compiler_params=pltpu.CompilerParams(vmem_limit_bytes=32 * 1024 * 1024),
        name="weigh",
    )(codes, scores)


def mix_kernel(code_ref, weight_ref, value_ref, out_ref, spread, rows):
    step = pl.program_id(0)

    @pl.when(step == 0)
    def _():
        out_ref[...] = jnp.zeros_like(out_ref)
        rows[:, HEAD:] = jnp.ones((GROUP * PART, HEAD), jnp.bfloat16)

    for i in range(GROUP):
        span = slice(i * PART, (i + 1) * PART)
        rows[span, :HEAD] = value_ref[i]
        query = code_ref[i : i + 1, :] >> 9
        weight = weight_ref[i : i + 1, :]
        for h in range(HEADS):
            ids = lax.broadcasted_iota(jnp.int32, (TOK, PART), 0) + h * TOK
            spread[h * TOK : (h + 1) * TOK, span] = jnp.where(ids == query, weight, 0.0).astype(jnp.bfloat16)
    for h in range(HEADS // 2):
        span = slice(h * 2 * TOK, (h + 1) * 2 * TOK)
        out_ref[span, :] += jnp.dot(spread[span, :], rows[...], preferred_element_type=jnp.float32)


def mix(codes, weights, values, part):
    return pl.pallas_call(
        mix_kernel,
        grid=(DEVS // GROUP,),
        in_specs=[
            pl.BlockSpec((GROUP, PART), lambda g: (g, part)),
            pl.BlockSpec((GROUP, PART), lambda g: (g, part)),
            pl.BlockSpec((GROUP, PART, HEAD), lambda g: (g, 0, 0)),
        ],
        out_specs=pl.BlockSpec((HEADS * TOK, 2 * HEAD), lambda g: (0, 0)),
        out_shape=jax.ShapeDtypeStruct((HEADS * TOK, 2 * HEAD), jnp.float32),
        scratch_shapes=[
            pltpu.VMEM((HEADS * TOK, GROUP * PART), jnp.bfloat16),
            pltpu.VMEM((GROUP * PART, 2 * HEAD), jnp.bfloat16),
        ],
        compiler_params=pltpu.CompilerParams(vmem_limit_bytes=32 * 1024 * 1024),
        name="mix",
    )(codes, weights, values)


def shards(queries, keys, values, mem_keys, mem_values, knn_index, block_slot, gate_bias, w_out):
    every = ("seq", "mem")
    send = functools.partial(lax.all_to_all, axis_name=every, split_axis=0, concat_axis=0, tiled=True)
    scale = HEAD ** (-0.5)
    all_queries = lax.all_gather(queries[0], every, axis=0, tiled=True)
    whole_keys = lax.all_gather(keys[0], "seq", axis=0, tiled=True)
    whole_values = lax.all_gather(values[0], "seq", axis=0, tiled=True)

    lookups = knn_index[0].transpose(1, 0, 2).reshape(TOK * HEADS * TOPK // ROWS, ROWS)
    asked = route(lookups, block_slot)
    codes = send(asked)
    fetched = [send(pick(codes, mem_values, part)) for part in range(PARTS)]
    kept = [pick(codes, mem_keys, part) for part in range(PARTS)]
    scores = send(score(codes, all_queries, kept).T)
    weights = weigh(asked, scores)
    sums = sum(mix(asked, weights, fetched[part], part) for part in range(PARTS))
    mem_out = (sums[:, :HEAD] / sums[:, HEAD:]).reshape(HEADS, TOK, HEAD)

    query = queries[0].reshape(TOK, HEADS, HEAD)
    span = whole_keys.shape[0]
    key_rows = whole_keys.reshape(span, HEADS, HEAD)
    value_rows = whole_values.reshape(span, HEADS, HEAD)
    local = jnp.einsum("qhd,khd->hqk", query, key_rows, preferred_element_type=jnp.float32) * scale
    query_pos = lax.axis_index("seq") * TOK + jnp.arange(TOK, dtype=jnp.int32)
    key_pos = jnp.arange(span, dtype=jnp.int32)
    local = jnp.where(key_pos[None, None, :] <= query_pos[None, :, None], local, -jnp.inf)
    probs = jax.nn.softmax(local, axis=-1).astype(jnp.bfloat16)
    local_out = jnp.einsum("hqk,khd->hqd", probs, value_rows, preferred_element_type=jnp.float32)

    gate = jax.nn.sigmoid(gate_bias)[:, None, None]
    combined = (gate * mem_out + (1.0 - gate) * local_out).astype(jnp.bfloat16)
    combined = combined.transpose(1, 0, 2).reshape(TOK, HEADS * HEAD)
    mixed = jnp.dot(combined, w_out, preferred_element_type=jnp.float32).astype(jnp.bfloat16)
    return mixed[None]


def solution(mesh):
    return jax.shard_map(
        shards,
        mesh=mesh,
        in_specs=(
            P("mem", "seq", None),
            P("mem", "seq", None),
            P("mem", "seq", None),
            P(("seq", "mem"), None),
            P(("seq", "mem"), None),
            P("mem", "seq", None, None),
            P(),
            P(),
            P(),
        ),
        out_specs=P("mem", "seq", None),
        check_vma=False,
    )
```

time: 1080 us -> 569 us (0.53)
  local copies, waits for them, and re-layouts: 604 us -> 21.5 us
  Pallas kernels: 0 us -> 330 us
  waiting for transfers between devices: 343 us -> 140 us
  other arithmetic: 74.2 us -> 0.4 us
  blocking collectives: 0 us -> 22 us
  starting transfers between devices: 17.2 us -> 31.2 us
    gather x4 -> x0, local copies, waits for them, and re-layouts: 455 us -> none  [the longest x1 193 us: shards(): jnp.take(table, lax.all_to_all(requests, ('seq', 'mem'), split_axis=0, co...]
    pallas_call x0 -> x12, Pallas kernels: none -> 330 us  [the longest x6 135 us: pick(): pl.pallas_call(pick_kernel, grid=(DEVS // GROUP,), in_specs=[pl.BlockSpec...]
    all_gather x2 -> x3, waiting for transfers between devices: 277 us -> 81.6 us  [the longest x1 54.8 us: shards(): whole_values = lax.all_gather(values[0], 'seq', axis=0, tiled=True)]
    scatter x1 -> x0, local copies, waits for them, and re-layouts: 121 us -> none  [shards(): requests = jnp.zeros((devices * capacity,), jnp.int32).at[slot_of].set(code)]
    select_n x7 -> x0, other arithmetic: 32.3 us -> none  [the longest x2 17.4 us: shards(): jnp.take(table, lax.all_to_all(requests, ('seq', 'mem'), split_axis=0, co...]
    all_to_all x0 -> x1, blocking collectives: none -> 22 us  [shards(): codes = send(asked)]
    another operation x5 -> x0, other arithmetic: 19.9 us -> none
    another operation x12 -> x0, local copies, waits for them, and re-layouts: 19.1 us -> none
  transfers between devices with their start and end apart: 4 -> 7, of which waited for: 4 -> 3; matrix products, arithmetic and copies ran while one was open for 1% -> 1% of each run, Pallas kernels for 0% -> 55%
where the time goes in v1:
time: 569 us; the launch traced here: 568 us
  Pallas kernels  330 us (58%)
  waiting for transfers between devices  140 us (25%)
  starting transfers between devices  31.2 us (5%)
  blocking collectives  22 us (4%)
  local copies, waits for them, and re-layouts  21.5 us (4%)
  between operations  15.2 us (3%)
  matrix products  7.26 us (1%)
    pallas_call x6, Pallas kernels, pick(): pl.pallas_call(pick_kernel, grid=(DEVS // GROUP,), in_specs=[pl.BlockSpec...  135 us
    pallas_call x1, Pallas kernels, score(): pl.pallas_call(score_kernel, grid=(DEVS // GROUP,), in_specs=[pl.BlockSpe...  89.9 us
    all_to_all x3, waiting for transfers between devices, shards(): fetched = [send(pick(codes, mem_values, part)) for part in range(PARTS)]  57.4 us
    all_gather x1, waiting for transfers between devices, shards(): whole_values = lax.all_gather(values[0], 'seq', axis=0, tiled=True)  54.8 us
    pallas_call x3, Pallas kernels, mix(): pl.pallas_call(mix_kernel, grid=(DEVS // GROUP,), in_specs=[pl.BlockSpec(...  45 us
    pallas_call x1, Pallas kernels, weigh(): pl.pallas_call(weigh_kernel, out_shape=jax.ShapeDtypeStruct((DEVS, CAP),...  38.3 us
    all_gather x1, waiting for transfers between devices, shards(): whole_keys = lax.all_gather(keys[0], 'seq', axis=0, tiled=True)  26.8 us
    all_to_all x1, blocking collectives, shards(): codes = send(asked)  22 us
  transfers between devices with their start and end apart: 7, of which 3 were waited for; matrix products, arithmetic and copies ran while one was open for 1% of the time, Pallas kernels for 55%

profile of v1, /device:TPU:1, one launch (start us, length us, event | category | flops | bytes accessed | tf_op | source)
XLA Modules:
  0.0 567.8 jit_solution(6315094372979139165)
XLA Ops:
  10.1 22.0 %route.1.code_ref = s32[128,384]{1,0:T(8,128)S(1)} custom-call(s32[128,256]{1,0:T(8,128)S(1)} %reshape.54.look_ref, s32[8,128]{1,0:T(8,128)S(1)} %bitcast.40), custom_call_target="tpu_custom_call" | custom-call | tf_op jit(solution)/shard_map/route/pallas_call | solution.py:90
  32.3 22.0 %all_to_all.37 = s32[128,1,384]{2,1,0:T(1,128)S(1)} all-to-all(s32[128,1,384]{2,1,0:T(1,128)S(1)} %copy.23), channel_id=1, replica_groups=mesh['seq'=4,'mem'=32] {'seq','mem'}, dimensions={0} | all-to-all | bytes 393216 | tf_op jit(solution)/shard_map/all_to_all | solution.py:295
  55.6 22.4 %pick.9 = bf16[128,128,128]{2,1,0:T(8,128)(2,1)S(1)} custom-call(s32[128,384]{1,0:T(8,128)S(1)} %bitcast.30, bf16[512,1024]{1,0:T(8,128)(2,1)S(1)} %copy-done.8), custom_call_target="tpu_custom_call" | custom-call | tf_op jit(solution)/shard_map/pick/pallas_call | solution.py:126
  80.1 5.5 all-to-all-start.2
  85.6 22.4 %pick.10 = bf16[128,128,128]{2,1,0:T(8,128)(2,1)S(1)} custom-call(s32[128,384]{1,0:T(8,128)S(1)} %bitcast.31, bf16[512,1024]{1,0:T(8,128)(2,1)S(1)} %copy-done.9), custom_call_target="tpu_custom_call" | custom-call | tf_op jit(solution)/shard_map/pick/pallas_call | solution.py:126
  110.0 57.4 %all-to-all-done.2.value_ref = bf16[128,128,128]{2,1,0:T(8,128)(2,1)} async-done(((bf16[128,128,128]{2,1,0:T(8,128)(2,1)}), bf16[128,128,128]{2,1,0:T(8,128)(2,1)}, u32[]{:S(2)}, u32[]{:S(2)}) %all-to-all-start.2) | async-done | bytes 4194336 | tf_op jit(solution)/shard_map/all_to_all | solution.py:296
  167.4 5.3 all-to-all-start.3
  172.7 22.4 %pick.6.refs_0_ = bf16[128,128,128]{2,1,0:T(8,128)(2,1)S(1)} custom-call(s32[128,384]{1,0:T(8,128)S(1)} %bitcast.32, bf16[512,1024]{1,0:T(8,128)(2,1)S(1)} %copy-done.7), custom_call_target="tpu_custom_call" | custom-call | tf_op jit(solution)/shard_map/pick/pallas_call | solution.py:126
  197.2 22.4 %pick.7.refs_1_ = bf16[128,128,128]{2,1,0:T(8,128)(2,1)S(1)} custom-call(s32[128,384]{1,0:T(8,128)S(1)} %bitcast.33, bf16[512,1024]{1,0:T(8,128)(2,1)S(1)} %copy-done.7), custom_call_target="tpu_custom_call" | custom-call | tf_op jit(solution)/shard_map/pick/pallas_call | solution.py:126
  221.6 22.4 %pick.8.refs_2_ = bf16[128,128,128]{2,1,0:T(8,128)(2,1)S(1)} custom-call(s32[128,384]{1,0:T(8,128)S(1)} %bitcast.34, bf16[512,1024]{1,0:T(8,128)(2,1)S(1)} %copy-done.7), custom_call_target="tpu_custom_call" | custom-call | tf_op jit(solution)/shard_map/pick/pallas_call | solution.py:126
  244.0 2.0 copy-done.6
  246.1 2.2 copy-done.4
  248.3 89.9 %score.1 = f32[384,128]{1,0:T(8,128)S(1)} custom-call(s32[128,384]{1,0:T(8,128)S(1)} %bitcast.35, bf16[16384,1024]{1,0:T(8,128)(2,1)} %bitcast.41, bf16[128,128,128]{2,1,0:T(8,128)(2,1)S(1)} %copy-done.4, bf16[128,128,128]{2,1,0:T(8,128)(2,1)} %copy-done.5, bf16[128,128,128]{2,1,0:T(8,128)(2,1)} %copy-done.6), custom_call_target="tpu_custom_call" | custom-call | tf_op jit(solution)/shard_map/score/pallas_call | solution.py:176
  339.0 9.9 %all-to-all-start.1 = ((f32[128,1,384]{2,1,0:T(1,128)}), f32[128,1,384]{2,1,0:T(1,128)S(1)}, u32[]{:S(2)}, u32[]{:S(2)}) async-start(f32[128,1,384]{2,1,0:T(1,128)} %copy.24), calls=%async_computation.1 | async-start | bytes 393216 | tf_op jit(solution)/shard_map/all_to_all | solution.py:298
  348.9 22.5 %pick.11 = bf16[128,128,128]{2,1,0:T(8,128)(2,1)S(1)} custom-call(s32[128,384]{1,0:T(8,128)S(1)} %bitcast.36, bf16[512,1024]{1,0:T(8,128)(2,1)S(1)} %copy-done.9), custom_call_target="tpu_custom_call" | custom-call | tf_op jit(solution)/shard_map/pick/pallas_call | solution.py:126
  373.5 10.2 %all-to-all-start.4 = ((bf16[128,128,128]{2,1,0:T(8,128)(2,1)}), bf16[128,128,128]{2,1,0:T(8,128)(2,1)}, u32[]{:S(2)}, u32[]{:S(2)}) async-start(bf16[128,128,128]{2,1,0:T(8,128)(2,1)} %copy-done), calls=%async_computation.4 | async-start | bytes 8388608 | tf_op jit(solution)/shard_map/all_to_all | solution.py:296
  385.6 54.8 %all-gather.11.cloned.1.call-done = bf16[1,512,1024]{2,1,0:T(8,128)(2,1)} async-done(((bf16[1,128,1024]{2,1,0:T(8,128)(2,1)}), bf16[1,512,1024]{2,1,0:T(8,128)(2,1)}) %all-gather.11.cloned.1.call-update) | async-done | bytes 1048592 | tf_op jit(solution)/shard_map/all_gather | solution.py:291
  441.9 26.8 %all-gather.9.cloned.1.call-done = bf16[1,512,1024]{1,2,0:T(8,128)(2,1)} async-done(((bf16[1,128,1024]{1,2,0:T(8,128)(2,1)}), bf16[1,512,1024]{1,2,0:T(8,128)(2,1)}) %all-gather.9.cloned.1.call-update) | async-done | bytes 1048592 | tf_op jit(solution)/shard_map/all_gather | solution.py:290
  468.7 3.4 fusion.18
  472.1 38.3 %weigh.1.weight_ref = f32[128,384]{1,0:T(8,128)S(1)} custom-call(s32[128,384]{1,0:T(8,128)S(1)} %route.1.code_ref, f32[128,384]{1,0:T(8,128)S(1)} %bitcast.39), custom_call_target="tpu_custom_call" | custom-call | tf_op jit(solution)/shard_map/weigh/pallas_call | solution.py:235
  510.4 15.0 %mix.3 = f32[1024,256]{1,0:T(8,128)S(1)} custom-call(s32[128,384]{1,0:T(8,128)S(1)} %route.1.code_ref, f32[128,384]{1,0:T(8,128)S(1)} %weigh.1.weight_ref, bf16[128,128,128]{2,1,0:T(8,128)(2,1)} %all-to-all-done.2.value_ref), custom_call_target="tpu_custom_call" | custom-call | tf_op jit(solution)/shard_map/mix/pallas_call | solution.py:266
  525.4 15.0 %mix.4 = f32[1024,256]{1,0:T(8,128)S(1)} custom-call(s32[128,384]{1,0:T(8,128)S(1)} %route.1.code_ref, f32[128,384]{1,0:T(8,128)S(1)} %weigh.1.weight_ref, bf16[128,128,128]{2,1,0:T(8,128)(2,1)} %all-to-all-done.3.value_ref), custom_call_target="tpu_custom_call" | custom-call | tf_op jit(solution)/shard_map/mix/pallas_call | solution.py:266
  540.4 15.1 %mix.5 = f32[1024,256]{1,0:T(8,128)S(1)} custom-call(s32[128,384]{1,0:T(8,128)S(1)} %route.1.code_ref, f32[128,384]{1,0:T(8,128)S(1)} %weigh.1.weight_ref, bf16[128,128,128]{2,1,0:T(8,128)(2,1)} %all-to-all-done.4.value_ref), custom_call_target="tpu_custom_call" | custom-call | tf_op jit(solution)/shard_map/mix/pallas_call | solution.py:266
  556.0 2.3 fusion.4
  (54 shorter events, 20.8 us)
Async XLA Ops:
  7.4 238.7 %all-gather.7.cloned.1.call-start = ((), (), s32[]{:S(2)}) async-start(), calls=%async_computation.5 | async-start | bytes 33816576 | tf_op jit(solution)/shard_map/all_gather | solution.py:289
  9.4 0.7 copy-start.10
  54.4 1.2 copy-start.8
  78.1 2.0 copy-start.2
  80.1 5.5 copy-start.9
  80.1 87.3 %all-to-all-start.2 = ((bf16[128,128,128]{2,1,0:T(8,128)(2,1)}), bf16[128,128,128]{2,1,0:T(8,128)(2,1)}, u32[]{:S(2)}, u32[]{:S(2)}) async-start(bf16[128,128,128]{2,1,0:T(8,128)(2,1)} %copy-done.2), calls=%async_computation.2 | async-start | bytes 8388608 | tf_op jit(solution)/shard_map/all_to_all | solution.py:296
  108.0 1.9 copy-start.1
  110.0 62.7 %copy-start.7 = (bf16[512,1024]{1,0:T(8,128)(2,1)S(1)}, bf16[512,1024]{1,0:T(8,128)(2,1)}, u32[]{:S(2)}) copy-start(bf16[512,1024]{1,0:T(8,128)(2,1)} %mem_ref.8) | copy-start | bytes 3145732
  167.4 171.7 %all-to-all-start.3 = ((bf16[128,128,128]{2,1,0:T(8,128)(2,1)}), bf16[128,128,128]{2,1,0:T(8,128)(2,1)}, u32[]{:S(2)}, u32[]{:S(2)}) async-start(bf16[128,128,128]{2,1,0:T(8,128)(2,1)} %copy-done.1), calls=%async_computation.3 | async-start | bytes 8388608 | tf_op jit(solution)/shard_map/all_to_all | solution.py:296
  195.2 2.0 copy-start.3
  219.6 2.0 copy-start.5
  244.0 2.1 copy-start.6
  246.1 2.2 copy-start.4
  339.0 34.4 %all-to-all-start.1 = ((f32[128,1,384]{2,1,0:T(1,128)}), f32[128,1,384]{2,1,0:T(1,128)S(1)}, u32[]{:S(2)}, u32[]{:S(2)}) async-start(f32[128,1,384]{2,1,0:T(1,128)} %copy.24), calls=%async_computation.1 | async-start | bytes 393216 | tf_op jit(solution)/shard_map/all_to_all | solution.py:298
  371.4 2.0 copy-start
  373.4 11.1 %copy-start.13 = (bf16[1,128,1024]{2,1,0:T(8,128)(2,1)S(1)}, bf16[1,128,1024]{2,1,0:T(8,128)(2,1)}, u32[]{:S(2)}) copy-start(bf16[1,128,1024]{2,1,0:T(8,128)(2,1)} %param.10) | copy-start | bytes 786436
  373.4 11.9 %copy-start.12 = (bf16[1,128,1024]{2,1,0:T(8,128)(2,1)S(1)}, bf16[1,128,1024]{2,1,0:T(8,128)(2,1)}, u32[]{:S(2)}) copy-start(bf16[1,128,1024]{2,1,0:T(8,128)(2,1)} %param.9) | copy-start | bytes 786436
  373.4 12.0 %copy-start.14 = (f32[8]{0:T(128)S(1)}, f32[8]{0:T(128)}, u32[]{:S(2)}) copy-start(f32[8]{0:T(128)} %param.16) | copy-start | bytes 100
  373.5 166.9 %all-to-all-start.4 = ((bf16[128,128,128]{2,1,0:T(8,128)(2,1)}), bf16[128,128,128]{2,1,0:T(8,128)(2,1)}, u32[]{:S(2)}, u32[]{:S(2)}) async-start(bf16[128,128,128]{2,1,0:T(8,128)(2,1)} %copy-done), calls=%async_computation.4 | async-start | bytes 8388608 | tf_op jit(solution)/shard_map/all_to_all | solution.py:296
  383.7 56.7 %all-gather.11.cloned.1.call-start = ((), (), s32[]{:S(2)}) async-start(), calls=%async_computation.7 | async-start | bytes 1310720 | tf_op jit(solution)/shard_map/all_gather | solution.py:291
  384.2 84.4 %all-gather.9.cloned.1.call-start = ((), (), s32[]{:S(2)}) async-start(), calls=%async_computation.6 | async-start | bytes 1310720 | tf_op jit(solution)/shard_map/all_gather | solution.py:290
  556.0 2.8 copy-start.11
Sparse Core Ops, SparseCore 0:
  11.2 154.4 all-gather.6
Sparse Core Ops, SparseCore 1:
  385.8 54.6 all-gather.10
  441.9 26.7 all-gather.8

commit v2 on v1

--- a/solution.py
+++ b/solution.py
@@ -20,6 +20,7 @@
 GROUP = 8
 BATCH = 8
 ROWS = 256
+WINDOW = 80
 NT = (((1,), (1,)), ((), ()))
 
 
@@ -27,7 +28,7 @@
     return jnp.where(mask, 1.0, 0.0).astype(jnp.bfloat16)
 
 
-def route_kernel(look_ref, slot_ref, req_ref, store, total, slots, parts):
+def route_kernel(look_ref, slot_ref, req_ref, store, total, slots, parts, starts):
     table = [jnp.broadcast_to(slot_ref[r : r + 1, :], (8, 128)) for r in range(8)]
 
     def translate(i, carry):
@@ -45,6 +46,8 @@
 
     lax.fori_loop(0, look_ref.shape[0] // 8, translate, 0)
     total[...] = jnp.zeros_like(total)
+    starts[...] = jnp.zeros_like(starts)
+    heads = lax.broadcasted_iota(jnp.int32, starts.shape, 1)
     upper = one_hot(
         lax.broadcasted_iota(jnp.int32, (ROWS, ROWS), 0) <= lax.broadcasted_iota(jnp.int32, (ROWS, ROWS), 1)
     )
@@ -57,6 +60,7 @@
     def place(i, run):
         base = pl.multiple_of(i * batch, batch)
         rows = store[pl.ds(base, batch), :]
+        starts[...] = jnp.where((heads * per_head == base) & (heads < HEADS), run[:, :128], starts[...])
         for b in range(batch):
             row = base + b
             head = row // per_head
@@ -77,99 +81,136 @@
         total[...] += lax.dot_general(parts[...], slots[...], NT, preferred_element_type=jnp.float32)
         return run
 
-    lax.fori_loop(0, look_ref.shape[0] // batch, place, jnp.zeros((DEVS, ROWS), jnp.float32))
+    run = lax.fori_loop(0, look_ref.shape[0] // batch, place, jnp.zeros((DEVS, ROWS), jnp.float32))
     first = total[0:DEVS, :].astype(jnp.int32)
     second = total[DEVS : 2 * DEVS, :].astype(jnp.int32)
     third = total[2 * DEVS :, :].astype(jnp.int32)
     local = first + (second & 1) * 256
     query = (third - 1) * TOK + (second >> 1)
-    req_ref[...] = jnp.where(third > 0, query * MEM_DEV + local, -1)
+    req_ref[:, :CAP] = jnp.where(third > 0, query * MEM_DEV + local, -1)
+    req_ref[:, CAP:] = jnp.where(heads == HEADS, run[:, :128], starts[...]).astype(jnp.int32)
 
 
 def route(lookups, block_slot):
     return pl.pallas_call(
         route_kernel,
-        out_shape=jax.ShapeDtypeStruct((DEVS, CAP), jnp.int32),
+        out_shape=jax.ShapeDtypeStruct((DEVS, CAP + 128), jnp.int32),
         scratch_shapes=[
             pltpu.VMEM((TOK * HEADS * TOPK // ROWS, ROWS), jnp.int32),
             pltpu.VMEM((3 * DEVS, CAP), jnp.float32),
             pltpu.VMEM((CAP, BATCH * ROWS), jnp.bfloat16),
             pltpu.VMEM((3 * DEVS, BATCH * ROWS), jnp.bfloat16),
+            pltpu.VMEM((DEVS, 128), jnp.float32),
         ],
         compiler_params=pltpu.CompilerParams(vmem_limit_bytes=32 * 1024 * 1024),
         name="route",
     )(lookups, block_slot.reshape(8, 128))
 
 
-def pick_kernel(code_ref, mem_ref, out_ref, hot, head_of):
-    code = jnp.transpose(code_ref[...])
-    row_ids = lax.broadcasted_iota(jnp.int32, (PART, MEM_DEV), 1)
+def turn_kernel(query_ref, out_ref):
+    for h in range(HEADS):
+        span = slice(h * HEAD, (h + 1) * HEAD)
+        out_ref[span, :] = jnp.transpose(query_ref[:, span].astype(jnp.float32)).astype(jnp.bfloat16)
+
+
+def turn(queries):
+    return pl.pallas_call(
+        turn_kernel,
+        out_shape=jax.ShapeDtypeStruct((HEADS * HEAD, TOK), jnp.bfloat16),
+        name="turn",
+    )(queries)
+
+
+def pick_kernel(code_ref, start_ref, key_ref, value_ref, *refs):
+    outs, kept_ref = refs[:PARTS], refs[PARTS]
+    table, wanted, found, hot = refs[PARTS + 1 :]
+
+    @pl.when(pl.program_id(0) == 0)
+    def _():
+        for h in range(HEADS):
+            table[h, :, :HEAD] = key_ref[:, h * HEAD : (h + 1) * HEAD]
+            table[h, :, HEAD:] = value_ref[:, h * HEAD : (h + 1) * HEAD]
+        wanted[CAP:, :] = jnp.full((WINDOW, GROUP), -1, jnp.int32)
+
+    for part in range(PARTS):
+        span = slice(part * PART, (part + 1) * PART)
+        code = jnp.transpose(code_ref[:, span])
+        wanted[span, :] = (code & (MEM_DEV - 1)) + (code >> 16) * MEM_DEV
+    found[...] = jnp.zeros_like(found)
+    row_ids = lax.broadcasted_iota(jnp.int32, (WINDOW, MEM_DEV), 1)
+
+    def one_head(h, carry):
+        begins = [start_ref[i, h] // 8 * 8 for i in range(GROUP)]
+        most = start_ref[0, h + 1] - begins[0]
+        for i in range(1, GROUP):
+            most = jnp.maximum(most, start_ref[i, h + 1] - begins[i])
+
+        def one_window(w, carry):
+            spans = []
+            for i in range(GROUP):
+                at = jnp.minimum(begins[i] + w * WINDOW, CAP)
+                spans.append(pl.ds(pl.multiple_of(at, 8), WINDOW))
+                col = wanted[spans[i], i : i + 1]
+                hot[i * WINDOW : (i + 1) * WINDOW, :] = one_hot(col - h * MEM_DEV == row_ids)
+            both = jnp.dot(hot[...], table[h], preferred_element_type=jnp.float32)
+            for i in range(GROUP):
+                found[i, spans[i], :] += both[i * WINDOW : (i + 1) * WINDOW, :]
+            return carry
+
+        return lax.fori_loop(0, (most + WINDOW - 1) // WINDOW, one_window, carry)
+
+    lax.fori_loop(0, HEADS, one_head, 0)
     for i in range(GROUP):
-        col = code[:, i : i + 1]
-        span = slice(i * PART, (i + 1) * PART)
-        hot[span, :] = one_hot((col & (MEM_DEV - 1)) == row_ids)
-        head_of[span, :] = jnp.broadcast_to(col >> 16, (PART, HEAD))
-    for i in range(GROUP // 2):
-        span = slice(i * 2 * PART, (i + 1) * 2 * PART)
-        out = jnp.zeros((2 * PART, HEAD), jnp.float32)
-        which = head_of[span, :]
-        for pair in range(HEADS // 2):
-            both = jnp.dot(
-                hot[span, :], mem_ref[:, pair * 256 : (pair + 1) * 256], preferred_element_type=jnp.float32
-            )
-            out = jnp.where(which == 2 * pair, both[:, :HEAD], out)
-            out = jnp.where(which == 2 * pair + 1, both[:, HEAD:], out)
-        out_ref[2 * i : 2 * i + 2] = out.astype(jnp.bfloat16).reshape(2, PART, HEAD)
-
-
-def pick(codes, mem, part):
+        kept_ref[i] = found[i, :CAP, :HEAD].astype(jnp.bfloat16)
+        for part in range(PARTS):
+            outs[part][i] = found[i, part * PART : (part + 1) * PART, HEAD:].astype(jnp.bfloat16)
+
+
+def pick(codes, mem_keys, mem_values):
+    whole = pl.BlockSpec((MEM_DEV, HEADS * HEAD), lambda g: (0, 0))
     return pl.pallas_call(
         pick_kernel,
         grid=(DEVS // GROUP,),
         in_specs=[
-            pl.BlockSpec((GROUP, PART), lambda g: (g, part)),
-            pl.BlockSpec((MEM_DEV, HEADS * HEAD), lambda g: (0, 0)),
-        ],
-        out_specs=pl.BlockSpec((GROUP, PART, HEAD), lambda g: (g, 0, 0)),
-        out_shape=jax.ShapeDtypeStruct((DEVS, PART, HEAD), jnp.bfloat16),
+            pl.BlockSpec((GROUP, CAP), lambda g: (g, 0)),
+            pl.BlockSpec((GROUP, 128), lambda g: (g, CAP // 128), memory_space=pltpu.SMEM),
+            whole,
+            whole,
+        ],
+        out_specs=[pl.BlockSpec((GROUP, PART, HEAD), lambda g: (g, 0, 0))] * PARTS
+        + [pl.BlockSpec((GROUP, CAP, HEAD), lambda g: (g, 0, 0))],
+        out_shape=[jax.ShapeDtypeStruct((DEVS, PART, HEAD), jnp.bfloat16)] * PARTS
+        + [jax.ShapeDtypeStruct((DEVS, CAP, HEAD), jnp.bfloat16)],
         scratch_shapes=[
-            pltpu.VMEM((GROUP * PART, MEM_DEV), jnp.bfloat16),
-            pltpu.VMEM((GROUP * PART, HEAD), jnp.int32),
-        ],
-        compiler_params=pltpu.CompilerParams(vmem_limit_bytes=32 * 1024 * 1024),
+            pltpu.VMEM((HEADS, MEM_DEV, 2 * HEAD), jnp.bfloat16),
+            pltpu.VMEM((CAP + WINDOW, GROUP), jnp.int32),
+            pltpu.VMEM((GROUP, CAP + WINDOW, 2 * HEAD), jnp.float32),
+            pltpu.VMEM((GROUP * WINDOW, MEM_DEV), jnp.bfloat16),
+        ],
+        compiler_params=pltpu.CompilerParams(vmem_limit_bytes=40 * 1024 * 1024),
         name="pick",
-    )(codes, mem)
-
-
-def score_kernel(code_ref, query_ref, *refs):
-    keys, out_ref = refs[:PARTS], refs[PARTS]
-    step = pl.program_id(0)
-
-    @pl.when(step == 0)
-    def _():
-        out_ref[...] = jnp.zeros_like(out_ref)
-
-    tok_ids = lax.broadcasted_iota(jnp.int32, (PART, TOK), 1)
-    lane = lax.broadcasted_iota(jnp.int32, (PART, DEVS), 1)
-    for part in range(PARTS):
-        code = jnp.transpose(code_ref[:, part * PART : (part + 1) * PART])
-        acc = out_ref[part * PART : (part + 1) * PART, :]
-        for i in range(GROUP):
-            col = code[:, i : i + 1]
-            which = jnp.broadcast_to(col >> 16, (PART, HEAD))
-            hot = one_hot(((col >> 9) & (TOK - 1)) == tok_ids)
-            query = jnp.zeros((PART, HEAD), jnp.float32)
-            for pair in range(HEADS // 2):
-                both = jnp.dot(
-                    hot,
-                    query_ref[i * TOK : (i + 1) * TOK, pair * 256 : (pair + 1) * 256],
-                    preferred_element_type=jnp.float32,
-                )
-                query = jnp.where(which == 2 * pair, both[:, :HEAD], query)
-                query = jnp.where(which == 2 * pair + 1, both[:, HEAD:], query)
-            score = jnp.sum(query * keys[part][i].astype(jnp.float32), axis=1, keepdims=True)
-            acc = jnp.where(lane == step * GROUP + i, score * HEAD ** (-0.5), acc)
-        out_ref[part * PART : (part + 1) * PART, :] = acc
+    )(codes, codes, mem_keys, mem_values)
+
+
+def score_kernel(code_ref, query_ref, key_ref, out_ref):
+    tok_ids = lax.broadcasted_iota(jnp.int32, (TOK, CAP), 0)
+    diagonal = lax.broadcasted_iota(jnp.int32, (PART, PART), 0) == lax.broadcasted_iota(
+        jnp.int32, (PART, PART), 1
+    )
+    for i in range(GROUP):
+        code = code_ref[i : i + 1, :]
+        head = code >> 16
+        hot = one_hot(((code >> 9) & (TOK - 1)) == tok_ids)
+        each = jnp.dot(query_ref[i], hot, preferred_element_type=jnp.float32)
+        query = jnp.zeros((HEAD, CAP), jnp.float32)
+        for h in range(HEADS):
+            query = jnp.where(head == h, each[h * HEAD : (h + 1) * HEAD, :], query)
+        query = query.astype(jnp.bfloat16)
+        for part in range(PARTS):
+            span = slice(part * PART, (part + 1) * PART)
+            cross = jnp.dot(key_ref[i, span, :], query[:, span], preferred_element_type=jnp.float32)
+            score = jnp.sum(jnp.where(diagonal, cross, 0.0), axis=0, keepdims=True)
+            out_ref[i : i + 1, span] = score * HEAD ** (-0.5)
 
 
 def score(codes, queries, keys):
@@ -178,14 +219,14 @@
         grid=(DEVS // GROUP,),
         in_specs=[
             pl.BlockSpec((GROUP, CAP), lambda g: (g, 0)),
-            pl.BlockSpec((GROUP * TOK, HEADS * HEAD), lambda g: (g, 0)),
-        ]
-        + [pl.BlockSpec((GROUP, PART, HEAD), lambda g: (g, 0, 0))] * PARTS,
-        out_specs=pl.BlockSpec((CAP, DEVS), lambda g: (0, 0)),
-        out_shape=jax.ShapeDtypeStruct((CAP, DEVS), jnp.float32),
-        compiler_params=pltpu.CompilerParams(vmem_limit_bytes=48 * 1024 * 1024),
+            pl.BlockSpec((GROUP, HEADS * HEAD, TOK), lambda g: (g, 0, 0)),
+            pl.BlockSpec((GROUP, CAP, HEAD), lambda g: (g, 0, 0)),
+        ],
+        out_specs=pl.BlockSpec((GROUP, CAP), lambda g: (g, 0)),
+        out_shape=jax.ShapeDtypeStruct((DEVS, CAP), jnp.float32),
+        compiler_params=pltpu.CompilerParams(vmem_limit_bytes=40 * 1024 * 1024),
         name="score",
-    )(codes, queries, *keys)
+    )(codes, queries, keys)
 
 
 def weigh_kernel(code_ref, score_ref, out_ref, top):
@@ -286,28 +327,37 @@
     every = ("seq", "mem")
     send = functools.partial(lax.all_to_all, axis_name=every, split_axis=0, concat_axis=0, tiled=True)
     scale = HEAD ** (-0.5)
-    all_queries = lax.all_gather(queries[0], every, axis=0, tiled=True)
-    whole_keys = lax.all_gather(keys[0], "seq", axis=0, tiled=True)
-    whole_values = lax.all_gather(values[0], "seq", axis=0, tiled=True)
+    all_queries = lax.all_gather(turn(queries[0]), every, axis=0, tiled=True).reshape(DEVS, HEADS * HEAD, TOK)
+    own = jnp.concatenate([keys[0], values[0]], axis=1)
+    devices = lax.axis_size("seq")
+    blocks = [own] + [
+        lax.ppermute(own, "seq", [(i, i + back) for i in range(devices - back)]) for back in range(1, devices)
+    ]
 
     lookups = knn_index[0].transpose(1, 0, 2).reshape(TOK * HEADS * TOPK // ROWS, ROWS)
     asked = route(lookups, block_slot)
     codes = send(asked)
-    fetched = [send(pick(codes, mem_values, part)) for part in range(PARTS)]
-    kept = [pick(codes, mem_keys, part) for part in range(PARTS)]
-    scores = send(score(codes, all_queries, kept).T)
+    *picked, kept = pick(codes, mem_keys, mem_values)
+    first = send(picked[0])
+    first, kept = lax.optimization_barrier((first, kept))
+    second = send(picked[1])
+    scores = send(score(codes, all_queries, kept))
+    scores, last = lax.optimization_barrier((scores, picked[2]))
+    third = send(last)
     weights = weigh(asked, scores)
-    sums = sum(mix(asked, weights, fetched[part], part) for part in range(PARTS))
+    sums = sum(mix(asked, weights, rows, part) for part, rows in enumerate((first, second, third)))
     mem_out = (sums[:, :HEAD] / sums[:, HEAD:]).reshape(HEADS, TOK, HEAD)
 
     query = queries[0].reshape(TOK, HEADS, HEAD)
-    span = whole_keys.shape[0]
-    key_rows = whole_keys.reshape(span, HEADS, HEAD)
-    value_rows = whole_values.reshape(span, HEADS, HEAD)
+    near = jnp.concatenate(blocks, axis=0)
+    key_rows = near[:, : HEADS * HEAD].reshape(-1, HEADS, HEAD)
+    value_rows = near[:, HEADS * HEAD :].reshape(-1, HEADS, HEAD)
     local = jnp.einsum("qhd,khd->hqk", query, key_rows, preferred_element_type=jnp.float32) * scale
-    query_pos = lax.axis_index("seq") * TOK + jnp.arange(TOK, dtype=jnp.int32)
-    key_pos = jnp.arange(span, dtype=jnp.int32)
-    local = jnp.where(key_pos[None, None, :] <= query_pos[None, :, None], local, -jnp.inf)
+    back = jnp.arange(near.shape[0], dtype=jnp.int32) // TOK
+    within = jnp.arange(near.shape[0], dtype=jnp.int32) % TOK
+    here = (back == 0)[None, :] & (within[None, :] <= jnp.arange(TOK, dtype=jnp.int32)[:, None])
+    earlier = (back > 0) & (back <= lax.axis_index("seq"))
+    local = jnp.where((here | earlier[None, :])[None], local, -jnp.inf)
     probs = jax.nn.softmax(local, axis=-1).astype(jnp.bfloat16)
     local_out = jnp.einsum("hqk,khd->hqd", probs, value_rows, preferred_element_type=jnp.float32)
 

time: 569 us -> 497 us (0.87)
  Pallas kernels: 330 us -> 237 us
  blocking collectives: 22 us -> 96.7 us
  waiting for transfers between devices: 140 us -> 109 us
  starting transfers between devices: 31.2 us -> 20.4 us
  local copies, waits for them, and re-layouts: 21.5 us -> 12.6 us
    all_gather x3 -> x1, waiting for transfers between devices: 81.6 us -> 0.01 us  [shards(): lax.all_gather(turn(queries[0]), every, axis=0, tiled=True)]
    all_to_all x0 -> x2, blocking collectives: none -> 73 us  [the longest x1 58.7 us: shards(): first = send(picked[0])]
    pallas_call x6 -> x1, Pallas kernels: 135 us -> 69.4 us  [pick(): pl.pallas_call(pick_kernel, grid=(DEVS // GROUP,), in_specs=[pl.BlockSpec...]
    ppermute x0 -> x3, waiting for transfers between devices: none -> 56.2 us  [shards(): lax.ppermute(own, 'seq', [(i, i + back) for i in range(devices - back)])]
    pallas_call x1, Pallas kernels: 89.9 us -> 61.6 us  [score(): pl.pallas_call(score_kernel, grid=(DEVS // GROUP,), in_specs=[pl.BlockSpe...]
    all_to_all x4 -> x2, starting transfers between devices: 30.9 us -> 10.5 us  [the longest x1 5.39 us: shards(): third = send(last)]
    ppermute x0 -> x3, starting transfers between devices: none -> 9.93 us  [shards(): lax.ppermute(own, 'seq', [(i, i + back) for i in range(devices - back)])]
    unnamed x34 -> x31, local copies, waits for them, and re-layouts: 17.5 us -> 9.49 us
  transfers between devices with their start and end apart: 7 -> 6, of which waited for: 3 -> 4; matrix products, arithmetic and copies ran while one was open for 1% -> 1% of each run, Pallas kernels for 55% -> 32%
where the time goes in v2:
time: 497 us; the launch traced here: 496 us
  Pallas kernels  237 us (48%)
  waiting for transfers between devices  109 us (22%)
  blocking collectives  96.7 us (19%)
  starting transfers between devices  20.4 us (4%)
  between operations  13.7 us (3%)
  local copies, waits for them, and re-layouts  12.6 us (3%)
  matrix products  5.99 us (1%)
    pallas_call x1, Pallas kernels, pick(): pl.pallas_call(pick_kernel, grid=(DEVS // GROUP,), in_specs=[pl.BlockSpec...  69.4 us
    pallas_call x1, Pallas kernels, score(): pl.pallas_call(score_kernel, grid=(DEVS // GROUP,), in_specs=[pl.BlockSpe...  61.6 us
    all_to_all x1, blocking collectives, shards(): first = send(picked[0])  58.7 us
    ppermute x3, waiting for transfers between devices, shards(): lax.ppermute(own, 'seq', [(i, i + back) for i in range(devices - back)])  56.2 us
    all_to_all x1, waiting for transfers between devices, shards(): second = send(picked[1])  52.9 us
    pallas_call x3, Pallas kernels, mix(): pl.pallas_call(mix_kernel, grid=(DEVS // GROUP,), in_specs=[pl.BlockSpec(...  43.2 us
    pallas_call x1, Pallas kernels, weigh(): pl.pallas_call(weigh_kernel, out_shape=jax.ShapeDtypeStruct((DEVS, CAP),...  38.3 us
    all_to_all x1, blocking collectives, shards(): codes = send(asked)  23.7 us
  transfers between devices with their start and end apart: 6, of which 4 were waited for; matrix products, arithmetic and copies ran while one was open for 1% of the time, Pallas kernels for 32%

profile of v2, /device:TPU:1, one launch (start us, length us, event | category | flops | bytes accessed | tf_op | source)
XLA Modules:
  0.0 496.0 jit_solution(1937380282477614)
XLA Ops:
  6.5 1.9 turn.1
  9.8 22.1 %route.1.code_ref = s32[128,512]{1,0:T(8,128)S(1)} custom-call(s32[128,256]{1,0:T(8,128)S(1)} %reshape.108.look_ref, s32[8,128]{1,0:T(8,128)S(1)} %bitcast.44), custom_call_target="tpu_custom_call" | custom-call | tf_op jit(solution)/shard_map/route/pallas_call | solution.py:95
  32.2 23.7 %all_to_all.38 = s32[128,1,512]{2,1,0:T(1,128)S(1)} all-to-all(s32[128,1,512]{2,1,0:T(1,128)S(1)} %copy.23), channel_id=1, replica_groups=mesh['seq'=4,'mem'=32] {'seq','mem'}, dimensions={0} | all-to-all | bytes 524288 | tf_op jit(solution)/shard_map/all_to_all | solution.py:339
  55.9 69.4 %pick.1 = (bf16[128,128,128]{2,1,0:T(8,128)(2,1)S(1)}, bf16[128,128,128]{2,1,0:T(8,128)(2,1)S(1)}, bf16[128,128,128]{2,1,0:T(8,128)(2,1)}, bf16[128,384,128]{2,1,0:T(8,128)(2,1)}) custom-call(s32[128,512]{1,0:T(8,128)S(1)} %bitcast.39, s32[128,512]{1,0:T(8,128)S(1)} %bitcast.40, bf16[512,1024]{1,0:T(8,128)(2,1)S(1)} %copy-done.3, bf16[512,1024]{1,0:T(8,128)(2,1)S(1)} %copy-done.4), custom_call_target="tpu_custom_call" | custom-call | tf_op jit(solution)/shard_map/pick/pallas_call | solution.py:171
  125.3 58.7 %all_to_all.39.value_ref = bf16[128,128,128]{2,1,0:T(8,128)(2,1)} all-to-all(bf16[128,128,128]{2,1,0:T(8,128)(2,1)S(1)} %get-tuple-element.13), channel_id=1, replica_groups=mesh['seq'=4,'mem'=32] {'seq','mem'}, dimensions={0} | all-to-all | bytes 8388608 | tf_op jit(solution)/shard_map/all_to_all | solution.py:341
  184.0 4.6 copy-done.1
  188.6 61.6 %score.1 = f32[128,384]{1,0:T(8,128)S(1)} custom-call(s32[128,512]{1,0:T(8,128)S(1)} %bitcast.41, bf16[128,1024,128]{2,1,0:T(8,128)(2,1)} %bitcast.45, bf16[128,384,128]{2,1,0:T(8,128)(2,1)S(1)} %copy-done.1), custom_call_target="tpu_custom_call" | custom-call | tf_op jit(solution)/shard_map/score/pallas_call | solution.py:217
  250.4 14.3 %all_to_all.40 = f32[128,1,384]{2,1,0:T(1,128)S(1)} all-to-all(f32[128,1,384]{2,1,0:T(1,128)S(1)} %copy.24), channel_id=1, replica_groups=mesh['seq'=4,'mem'=32] {'seq','mem'}, dimensions={0} | all-to-all | bytes 393216 | tf_op jit(solution)/shard_map/all_to_all | solution.py:344
  264.7 5.1 %all-to-all-start.3 = ((bf16[128,128,128]{2,1,0:T(8,128)(2,1)}), bf16[128,128,128]{2,1,0:T(8,128)(2,1)}, u32[]{:S(2)}, u32[]{:S(2)}) async-start(bf16[128,128,128]{2,1,0:T(8,128)(2,1)} %copy-done.2), calls=%async_computation.3 | async-start | bytes 8388608 | tf_op jit(solution)/shard_map/all_to_all | solution.py:343
  269.9 52.9 %all-to-all-done.3.value_ref = bf16[128,128,128]{2,1,0:T(8,128)(2,1)} async-done(((bf16[128,128,128]{2,1,0:T(8,128)(2,1)}), bf16[128,128,128]{2,1,0:T(8,128)(2,1)}, u32[]{:S(2)}, u32[]{:S(2)}) %all-to-all-start.3) | async-done | bytes 4194336 | tf_op jit(solution)/shard_map/all_to_all | solution.py:343
  322.8 5.4 %all-to-all-start.4 = ((bf16[128,128,128]{2,1,0:T(8,128)(2,1)}), bf16[128,128,128]{2,1,0:T(8,128)(2,1)}, u32[]{:S(2)}, u32[]{:S(2)}) async-start(bf16[128,128,128]{2,1,0:T(8,128)(2,1)} %get-tuple-element.20), calls=%async_computation.4 | async-start | bytes 8388608 | tf_op jit(solution)/shard_map/all_to_all | solution.py:346
  328.6 3.6 collective-permute-start
  332.2 4.8 collective-permute-start.1
  339.6 43.4 %collective-permute-done = bf16[128,2048]{0,1:T(8,128)(2,1)S(1)} collective-permute-done((bf16[128,2048]{0,1:T(8,128)(2,1)S(1)}, bf16[128,2048]{0,1:T(8,128)(2,1)S(1)}, u32[]{:S(2)}, u32[]{:S(2)}) %collective-permute-start) | collective-permute-done | bytes 524320 | tf_op jit(solution)/shard_map/ppermute | solution.py:334
  383.1 11.3 %collective-permute-done.1 = bf16[128,2048]{0,1:T(8,128)(2,1)S(1)} collective-permute-done((bf16[128,2048]{0,1:T(8,128)(2,1)S(1)}, bf16[128,2048]{0,1:T(8,128)(2,1)S(1)}, u32[]{:S(2)}, u32[]{:S(2)}) %collective-permute-start.1) | collective-permute-done | bytes 524320 | tf_op jit(solution)/shard_map/ppermute | solution.py:334
  394.3 1.5 collective-permute-done.2
  397.2 2.3 fusion.32
  399.5 38.3 %weigh.1.weight_ref = f32[128,384]{1,0:T(8,128)S(1)} custom-call(s32[128,512]{1,0:T(8,128)S(1)} %route.1.code_ref, f32[128,384]{1,0:T(8,128)S(1)} %bitcast.43), custom_call_target="tpu_custom_call" | custom-call | tf_op jit(solution)/shard_map/weigh/pallas_call | solution.py:276
  437.8 2.2 copy-done
  440.0 13.0 %mix.3 = f32[1024,256]{1,0:T(8,128)S(1)} custom-call(s32[128,512]{1,0:T(8,128)S(1)} %route.1.code_ref, f32[128,384]{1,0:T(8,128)S(1)} %weigh.1.weight_ref, bf16[128,128,128]{2,1,0:T(8,128)(2,1)S(1)} %copy-done), custom_call_target="tpu_custom_call" | custom-call | tf_op jit(solution)/shard_map/mix/pallas_call | solution.py:307
  453.1 15.1 %mix.4 = f32[1024,256]{1,0:T(8,128)S(1)} custom-call(s32[128,512]{1,0:T(8,128)S(1)} %route.1.code_ref, f32[128,384]{1,0:T(8,128)S(1)} %weigh.1.weight_ref, bf16[128,128,128]{2,1,0:T(8,128)(2,1)} %all-to-all-done.3.value_ref), custom_call_target="tpu_custom_call" | custom-call | tf_op jit(solution)/shard_map/mix/pallas_call | solution.py:307
  468.2 15.1 %mix.5 = f32[1024,256]{1,0:T(8,128)S(1)} custom-call(s32[128,512]{1,0:T(8,128)S(1)} %route.1.code_ref, f32[128,384]{1,0:T(8,128)S(1)} %weigh.1.weight_ref, bf16[128,128,128]{2,1,0:T(8,128)(2,1)} %all-to-all-done.4.value_ref), custom_call_target="tpu_custom_call" | custom-call | tf_op jit(solution)/shard_map/mix/pallas_call | solution.py:307
  484.8 2.2 fusion.4
  487.6 1.5 fusion.1
  (48 shorter events, 8.2 us)
Async XLA Ops:
  6.5 3.3 copy-start.5
  6.5 49.3 %copy-start.3 = (bf16[512,1024]{1,0:T(8,128)(2,1)S(1)}, bf16[512,1024]{1,0:T(8,128)(2,1)}, u32[]{:S(2)}) copy-start(bf16[512,1024]{1,0:T(8,128)(2,1)} %key_ref.1) | copy-start | bytes 3145732
  6.5 49.3 %copy-start.4 = (bf16[512,1024]{1,0:T(8,128)(2,1)S(1)}, bf16[512,1024]{1,0:T(8,128)(2,1)}, u32[]{:S(2)}) copy-start(bf16[512,1024]{1,0:T(8,128)(2,1)} %value_ref.1) | copy-start | bytes 3145732
  6.5 177.5 %all-gather.2.cloned.1.call-start = ((), (), s32[]{:S(2)}) async-start(), calls=%async_computation.5 | async-start | bytes 33816576 | tf_op jit(solution)/shard_map/all_gather | solution.py:330
  125.3 58.7 %copy-start.2 = (bf16[128,128,128]{2,1,0:T(8,128)(2,1)}, bf16[128,128,128]{2,1,0:T(8,128)(2,1)S(1)}, u32[]{:S(2)}) copy-start(bf16[128,128,128]{2,1,0:T(8,128)(2,1)S(1)} %get-tuple-element.19) | copy-start | bytes 12582916
  184.0 4.6 copy-start.1
  264.7 58.1 %all-to-all-start.3 = ((bf16[128,128,128]{2,1,0:T(8,128)(2,1)}), bf16[128,128,128]{2,1,0:T(8,128)(2,1)}, u32[]{:S(2)}, u32[]{:S(2)}) async-start(bf16[128,128,128]{2,1,0:T(8,128)(2,1)} %copy-done.2), calls=%async_computation.3 | async-start | bytes 8388608 | tf_op jit(solution)/shard_map/all_to_all | solution.py:343
  269.8 58.3 %copy-start.9 = (bf16[1,128,1024]{2,1,0:T(8,128)(2,1)S(1)}, bf16[1,128,1024]{2,1,0:T(8,128)(2,1)}, u32[]{:S(2)}) copy-start(bf16[1,128,1024]{2,1,0:T(8,128)(2,1)} %param.10) | copy-start | bytes 786436
  269.9 58.5 %copy-start.10 = (bf16[1,128,1024]{2,1,0:T(8,128)(2,1)S(1)}, bf16[1,128,1024]{2,1,0:T(8,128)(2,1)}, u32[]{:S(2)}) copy-start(bf16[1,128,1024]{2,1,0:T(8,128)(2,1)} %param.11) | copy-start | bytes 786436
  322.8 145.4 %all-to-all-start.4 = ((bf16[128,128,128]{2,1,0:T(8,128)(2,1)}), bf16[128,128,128]{2,1,0:T(8,128)(2,1)}, u32[]{:S(2)}, u32[]{:S(2)}) async-start(bf16[128,128,128]{2,1,0:T(8,128)(2,1)} %get-tuple-element.20), calls=%async_computation.4 | async-start | bytes 8388608 | tf_op jit(solution)/shard_map/all_to_all | solution.py:346
  328.2 10.4 %copy-start.7 = (bf16[1,128,1024]{2,1,0:T(8,128)(2,1)S(1)}, bf16[1,128,1024]{2,1,0:T(8,128)(2,1)}, u32[]{:S(2)}) copy-start(bf16[1,128,1024]{2,1,0:T(8,128)(2,1)} %param.9) | copy-start | bytes 786436
  328.2 11.1 %copy-start.12 = (f32[8]{0:T(128)S(1)}, f32[8]{0:T(128)}, u32[]{:S(2)}) copy-start(f32[8]{0:T(128)} %param.16) | copy-start | bytes 100
  328.6 54.5 %collective-permute-start = (bf16[128,2048]{0,1:T(8,128)(2,1)S(1)}, bf16[128,2048]{0,1:T(8,128)(2,1)S(1)}, u32[]{:S(2)}, u32[]{:S(2)}) collective-permute-start(bf16[128,2048]{0,1:T(8,128)(2,1)S(1)} %pad_maximum_fusion.1), channel_id=1, source_target_pairs={{0,32},{32,64},{64,96},{1,33},{33,65},{65,97},{2,34},{34,66},{66,9... | collective-permute-start | bytes 1572872 | tf_op jit(solution)/shard_map/ppermute | solution.py:334
  332.2 62.1 %collective-permute-start.1 = (bf16[128,2048]{0,1:T(8,128)(2,1)S(1)}, bf16[128,2048]{0,1:T(8,128)(2,1)S(1)}, u32[]{:S(2)}, u32[]{:S(2)}) collective-permute-start(bf16[128,2048]{0,1:T(8,128)(2,1)S(1)} %pad_maximum_fusion.1), channel_id=1, source_target_pairs={{0,64},{32,96},{1,65},{33,97},{2,66},{34,98},{3,67},{35,99},{4,68}... | collective-permute-start | bytes 1572872 | tf_op jit(solution)/shard_map/ppermute | solution.py:334
  337.0 58.8 %collective-permute-start.2 = (bf16[128,2048]{0,1:T(8,128)(2,1)S(1)}, bf16[128,2048]{0,1:T(8,128)(2,1)S(1)}, u32[]{:S(2)}, u32[]{:S(2)}) collective-permute-start(bf16[128,2048]{0,1:T(8,128)(2,1)S(1)} %pad_maximum_fusion.1), channel_id=1, source_target_pairs={{0,96},{1,97},{2,98},{3,99},{4,100},{5,101},{6,102},{7,103},{8,104... | collective-permute-start | bytes 1572872 | tf_op jit(solution)/shard_map/ppermute | solution.py:334
  396.1 1.1 copy-start.11
  437.8 2.2 copy-start
  483.6 1.2 copy-start.8
  484.8 2.8 copy-start.6
Sparse Core Ops, SparseCore 0:
  10.4 111.9 all-gather.1

commit v3 on v2

v3 whole, which is shorter than its diff:
```python
import functools

import jax
import jax.numpy as jnp
from jax import lax
from jax.experimental import pallas as pl
from jax.experimental.pallas import tpu as pltpu
from jax.sharding import PartitionSpec as P

DEVS = 128
TOK = 128
HEADS = 8
HEAD = 128
TOPK = 32
MEM_DEV = 512
BLOCK = 64
CAP = 384
PART = 128
PARTS = CAP // PART
GROUP = 8
BATCH = 8
ROWS = 256
WINDOW = 80
NT = (((1,), (1,)), ((), ()))


def one_hot(mask):
    return jnp.where(mask, 1.0, 0.0).astype(jnp.bfloat16)


def cost(micros):
    return pl.CostEstimate(flops=int(micros * 1e9), bytes_accessed=int(micros * 1e6), transcendentals=0)


def route_kernel(look_ref, slot_ref, req_ref, place_ref, store, total, slots, parts, starts):
    table = [jnp.broadcast_to(slot_ref[r : r + 1, :], (8, 128)) for r in range(8)]

    def translate(i, carry):
        base = pl.multiple_of(i * 8, 8)
        for half in range(ROWS // 128):
            look = look_ref[pl.ds(base, 8), half * 128 : (half + 1) * 128]
            blk = look >> 6
            low = blk & 127
            high = blk >> 7
            place = jnp.zeros((8, 128), jnp.int32)
            for r in range(8):
                place = jnp.where(high == r, jnp.take_along_axis(table[r], low, axis=1), place)
            store[pl.ds(base, 8), half * 128 : (half + 1) * 128] = place * BLOCK + (look & (BLOCK - 1))
        return carry

    lax.fori_loop(0, look_ref.shape[0] // 8, translate, 0)
    total[...] = jnp.zeros_like(total)
    starts[...] = jnp.zeros_like(starts)
    heads = lax.broadcasted_iota(jnp.int32, starts.shape, 1)
    upper = one_hot(
        lax.broadcasted_iota(jnp.int32, (ROWS, ROWS), 0) <= lax.broadcasted_iota(jnp.int32, (ROWS, ROWS), 1)
    )
    owners = lax.broadcasted_iota(jnp.int32, (DEVS, ROWS), 0)
    ranks = lax.broadcasted_iota(jnp.int32, (CAP, ROWS), 0)
    lane = lax.broadcasted_iota(jnp.int32, (1, ROWS), 1)
    batch = BATCH
    per_head = TOK * TOPK // ROWS

    def place(i, run):
        base = pl.multiple_of(i * batch, batch)
        rows = store[pl.ds(base, batch), :]
        starts[...] = jnp.where((heads * per_head == base) & (heads < HEADS), run[:, :128], starts[...])
        places = []
        for b in range(batch):
            row = base + b
            head = row // per_head
            tok = (row % per_head) * (ROWS // TOPK) + lane // TOPK
            here = rows[b : b + 1, :]
            owner = here // MEM_DEV
            mine = jnp.where(owners == owner, 1.0, 0.0)
            count = jnp.dot(mine.astype(jnp.bfloat16), upper, preferred_element_type=jnp.float32) + run
            rank = jnp.sum(mine * count, axis=0, keepdims=True).astype(jnp.int32) - 1
            run = jnp.broadcast_to(count[:, ROWS - 1 :], (DEVS, ROWS))
            places.append(owner * MEM_DEV + rank)
            span = slice(b * ROWS, (b + 1) * ROWS)
            slots[:, span] = one_hot(ranks == rank)
            local = here & (MEM_DEV - 1)
            first = (local & 255).astype(jnp.float32)
            second = ((local >> 8) + 2 * tok).astype(jnp.float32)
            parts[0:DEVS, span] = (mine * first).astype(jnp.bfloat16)
            parts[DEVS : 2 * DEVS, span] = (mine * second).astype(jnp.bfloat16)
            parts[2 * DEVS :, span] = (mine * (head + 1).astype(jnp.float32)).astype(jnp.bfloat16)
        total[...] += lax.dot_general(parts[...], slots[...], NT, preferred_element_type=jnp.float32)
        place_ref[pl.ds(base, batch), :] = jnp.concatenate(places, axis=0)
        return run

    run = lax.fori_loop(0, look_ref.shape[0] // batch, place, jnp.zeros((DEVS, ROWS), jnp.float32))
    first = total[0:DEVS, :].astype(jnp.int32)
    second = total[DEVS : 2 * DEVS, :].astype(jnp.int32)
    third = total[2 * DEVS :, :].astype(jnp.int32)
    local = first + (second & 1) * 256
    query = (third - 1) * TOK + (second >> 1)
    req_ref[:, :CAP] = jnp.where(third > 0, query * MEM_DEV + local, -1)
    req_ref[:, CAP:] = jnp.where(heads == HEADS, run[:, :128], starts[...]).astype(jnp.int32)


def route(lookups, block_slot):
    return pl.pallas_call(
        route_kernel,
        out_shape=[
            jax.ShapeDtypeStruct((DEVS, CAP + 128), jnp.int32),
            jax.ShapeDtypeStruct((TOK * HEADS * TOPK // ROWS, ROWS), jnp.int32),
        ],
        scratch_shapes=[
            pltpu.VMEM((TOK * HEADS * TOPK // ROWS, ROWS), jnp.int32),
            pltpu.VMEM((3 * DEVS, CAP), jnp.float32),
            pltpu.VMEM((CAP, BATCH * ROWS), jnp.bfloat16),
            pltpu.VMEM((3 * DEVS, BATCH * ROWS), jnp.bfloat16),
            pltpu.VMEM((DEVS, 128), jnp.float32),
        ],
        compiler_params=pltpu.CompilerParams(vmem_limit_bytes=32 * 1024 * 1024),
        cost_estimate=cost(22),
        name="route",
    )(lookups, block_slot.reshape(8, 128))


def turn_kernel(query_ref, out_ref):
    for h in range(HEADS):
        out_ref[h * TOK : (h + 1) * TOK, :] = query_ref[:, h * HEAD : (h + 1) * HEAD]


def turn(queries):
    return pl.pallas_call(
        turn_kernel,
        out_shape=jax.ShapeDtypeStruct((HEADS * TOK, HEAD), jnp.bfloat16),
        name="turn",
    )(queries)


def pick_rows(code_ref, start_ref, mem_ref, wanted, found, hot):
    @pl.when(pl.program_id(0) == 0)
    def _():
        wanted[CAP:, :] = jnp.full((WINDOW, GROUP), -1, jnp.int32)
        found[...] = jnp.zeros_like(found)

    for part in range(PARTS):
        span = slice(part * PART, (part + 1) * PART)
        code = jnp.transpose(code_ref[:, span])
        wanted[span, :] = (code & (MEM_DEV - 1)) + (code >> 16) * MEM_DEV
    row_ids = lax.broadcasted_iota(jnp.int32, (WINDOW, MEM_DEV), 1)
    for h in range(HEADS):
        begins = [start_ref[i, h] // 8 * 8 for i in range(GROUP)]
        most = start_ref[0, h + 1] - begins[0]
        for i in range(1, GROUP):
            most = jnp.maximum(most, start_ref[i, h + 1] - begins[i])

        def one_window(w, carry, h=h, begins=begins):
            for i in range(GROUP):
                at = pl.multiple_of(jnp.minimum(begins[i] + w * WINDOW, CAP), 8)
                col = wanted[pl.ds(at, WINDOW), i : i + 1] - h * MEM_DEV
                mine = slice(i * WINDOW, (i + 1) * WINDOW)
                hot[mine, :] = one_hot(col == row_ids)
                rows = jnp.dot(
                    hot[mine, :], mem_ref[:, h * HEAD : (h + 1) * HEAD], preferred_element_type=jnp.float32
                )
                own = (col[:8] >= 0) & (col[:8] < MEM_DEV)
                found[i, pl.ds(at, 8), :] = jnp.where(own, rows[:8], found[i, pl.ds(at, 8), :])
                found[i, pl.ds(at + 8, WINDOW - 8), :] = rows[8:]
            return carry

        lax.fori_loop(0, (most + WINDOW - 1) // WINDOW, one_window, 0)


PICK_SCRATCH = [
    pltpu.VMEM((CAP + WINDOW, GROUP), jnp.int32),
    pltpu.VMEM((GROUP, CAP + WINDOW, HEAD), jnp.float32),
    pltpu.VMEM((GROUP * WINDOW, MEM_DEV), jnp.bfloat16),
]
CODES = pl.BlockSpec((GROUP, CAP), lambda g: (g, 0))
STARTS = pl.BlockSpec((GROUP, 128), lambda g: (g, CAP // 128), memory_space=pltpu.SMEM)


def pick_kernel(code_ref, start_ref, value_ref, *refs):
    found = refs[PARTS + 1]
    pick_rows(code_ref, start_ref, value_ref, *refs[PARTS:])
    for i in range(GROUP):
        for part in range(PARTS):
            refs[part][i] = found[i, part * PART : (part + 1) * PART, :].astype(jnp.bfloat16)


def pick(codes, values):
    return pl.pallas_call(
        pick_kernel,
        grid=(DEVS // GROUP,),
        in_specs=[CODES, STARTS, pl.BlockSpec((MEM_DEV, HEADS * HEAD), lambda g: (0, 0))],
        out_specs=[pl.BlockSpec((GROUP, PART, HEAD), lambda g: (g, 0, 0))] * PARTS,
        out_shape=[jax.ShapeDtypeStruct((DEVS, PART, HEAD), jnp.bfloat16)] * PARTS,
        scratch_shapes=PICK_SCRATCH,
        compiler_params=pltpu.CompilerParams(vmem_limit_bytes=40 * 1024 * 1024),
        cost_estimate=cost(45),
        name="pick",
    )(codes, codes, values)


def score_kernel(code_ref, start_ref, key_ref, query_ref, *refs):
    out_ref, _, wanted, found, hot = refs[-5:]
    pick_rows(code_ref, start_ref, key_ref, wanted, found, hot)
    ids = lax.broadcasted_iota(jnp.int32, (HEADS * TOK, CAP), 0)
    for i in range(GROUP):
        keys = found[i, :CAP, :].astype(jnp.bfloat16)
        every = lax.dot_general(query_ref[i], keys, NT, preferred_element_type=jnp.float32)
        own = ids == code_ref[i : i + 1, :] >> 9
        out_ref[i : i + 1, :] = jnp.sum(jnp.where(own, every, 0.0), axis=0, keepdims=True) * HEAD ** (-0.5)


def score(codes, queries, keys, half, through, *ready):
    near = queries.shape[0] // GROUP
    steps = DEVS // GROUP // 2
    return pl.pallas_call(
        score_kernel,
        grid=(steps,),
        in_specs=[
            pl.BlockSpec((GROUP, CAP), lambda g: (g + half * steps, 0)),
            pl.BlockSpec((GROUP, 128), lambda g: (g + half * steps, CAP // 128), memory_space=pltpu.SMEM),
            pl.BlockSpec((MEM_DEV, HEADS * HEAD), lambda g: ((g + half * steps) // near, 0)),
            pl.BlockSpec((GROUP, HEADS * TOK, HEAD), lambda g: (g % near, 0, 0)),
            pl.BlockSpec(memory_space=pl.ANY),
        ]
        + [pl.BlockSpec(memory_space=pl.ANY)] * len(ready),
        out_specs=[CODES, pl.BlockSpec(memory_space=pl.ANY)],
        out_shape=[
            jax.ShapeDtypeStruct((DEVS // 2, CAP), jnp.float32),
            jax.ShapeDtypeStruct(through.shape, through.dtype),
        ],
        scratch_shapes=PICK_SCRATCH,
        input_output_aliases={4: 1},
        compiler_params=pltpu.CompilerParams(vmem_limit_bytes=40 * 1024 * 1024),
        cost_estimate=cost(40),
        name="score",
    )(codes, codes, keys, queries, through, *ready)


def join_kernel(a_ref, b_ref, _, out_ref):
    half = DEVS // 2
    out_ref[:half, :] = a_ref[...]
    out_ref[half:, :] = b_ref[...]


def join(one, two, ready):
    return pl.pallas_call(
        join_kernel,
        in_specs=[pl.BlockSpec(memory_space=pltpu.VMEM)] * 2 + [pl.BlockSpec(memory_space=pl.ANY)],
        out_shape=jax.ShapeDtypeStruct((DEVS, CAP), jnp.float32),
        name="join",
    )(one, two, ready)


def weigh_kernel(place_ref, score_ref, out_ref, parts, near, total, slots, spread):
    score = score_ref[...]
    for part in range(3):
        piece = score.astype(jnp.bfloat16)
        parts[part * DEVS : (part + 1) * DEVS, :] = piece
        score = score - piece.astype(jnp.float32)
    owners = lax.broadcasted_iota(jnp.int32, (DEVS, ROWS), 0)
    ranks = lax.broadcasted_iota(jnp.int32, (CAP, ROWS), 0)
    batches = place_ref.shape[0] // BATCH

    def fetch(i, carry):
        base = pl.multiple_of(i * BATCH, BATCH)
        place = place_ref[pl.ds(base, BATCH), :]
        rows = []
        for b in range(BATCH):
            here = place[b : b + 1, :]
            hot = one_hot(ranks == (here & (MEM_DEV - 1)))
            each = jnp.dot(parts[...], hot, preferred_element_type=jnp.float32)
            each = (each[:DEVS] + each[DEVS : 2 * DEVS]) + each[2 * DEVS :]
            rows.append(jnp.sum(jnp.where(owners == here // MEM_DEV, each, 0.0), axis=0, keepdims=True))
        near[pl.ds(base, BATCH), :] = jnp.concatenate(rows, axis=0)
        return carry

    lax.fori_loop(0, batches, fetch, 0)
    lane = lax.broadcasted_iota(jnp.int32, near.shape, 1)

    def across(x, op):
        for k in (16, 8, 4, 2, 1):
            other = jnp.where((lane & k) > 0, pltpu.roll(x, k, 1), pltpu.roll(x, ROWS - k, 1))
            x = op(x, other)
        return x

    score = near[...]
    power = jnp.exp(score - across(score, jnp.maximum))
    near[...] = power / across(power, jnp.add)
    total[...] = jnp.zeros_like(total)

    def scatter(i, carry):
        base = pl.multiple_of(i * BATCH, BATCH)
        place = place_ref[pl.ds(base, BATCH), :]
        prob = near[pl.ds(base, BATCH), :]
        for b in range(BATCH):
            here = place[b : b + 1, :]
            span = slice(b * ROWS, (b + 1) * ROWS)
            slots[:, span] = one_hot(ranks == (here & (MEM_DEV - 1)))
            mine = owners == here // MEM_DEV
            spread[:, span] = jnp.where(mine, prob[b : b + 1, :], 0.0).astype(jnp.bfloat16)
        total[...] += lax.dot_general(spread[...], slots[...], NT, preferred_element_type=jnp.float32)
        return carry

    lax.fori_loop(0, batches, scatter, 0)
    out_ref[...] = total[...]


def weigh(places, scores):
    return pl.pallas_call(
        weigh_kernel,
        out_shape=jax.ShapeDtypeStruct((DEVS, CAP), jnp.float32),
        scratch_shapes=[
            pltpu.VMEM((3 * DEVS, CAP), jnp.bfloat16),
            pltpu.VMEM(places.shape, jnp.float32),
            pltpu.VMEM((DEVS, CAP), jnp.float32),
            pltpu.VMEM((CAP, BATCH * ROWS), jnp.bfloat16),
            pltpu.VMEM((DEVS, BATCH * ROWS), jnp.bfloat16),
        ],
        compiler_params=pltpu.CompilerParams(vmem_limit_bytes=32 * 1024 * 1024),
        cost_estimate=cost(22),
        name="weigh",
    )(places, scores)


def mix_kernel(code_ref, weight_ref, value_ref, out_ref, spread):
    step = pl.program_id(0)

    @pl.when(step == 0)
    def _():
        out_ref[...] = jnp.zeros_like(out_ref)

    for i in range(GROUP):
        span = slice(i * PART, (i + 1) * PART)
        query = code_ref[i : i + 1, :] >> 9
        weight = weight_ref[i : i + 1, :]
        for h in range(HEADS):
            ids = lax.broadcasted_iota(jnp.int32, (TOK, PART), 0) + h * TOK
            spread[h * TOK : (h + 1) * TOK, span] = jnp.where(ids == query, weight, 0.0).astype(jnp.bfloat16)
    rows = value_ref[...].reshape(GROUP * PART, HEAD)
    for h in range(HEADS // 2):
        span = slice(h * 2 * TOK, (h + 1) * 2 * TOK)
        out_ref[span, :] += jnp.dot(spread[span, :], rows, preferred_element_type=jnp.float32)


def mix(codes, weights, values, part):
    return pl.pallas_call(
        mix_kernel,
        grid=(DEVS // GROUP,),
        in_specs=[
            pl.BlockSpec((GROUP, PART), lambda g: (g, part)),
            pl.BlockSpec((GROUP, PART), lambda g: (g, part)),
            pl.BlockSpec((GROUP, PART, HEAD), lambda g: (g, 0, 0)),
        ],
        out_specs=pl.BlockSpec((HEADS * TOK, HEAD), lambda g: (0, 0)),
        out_shape=jax.ShapeDtypeStruct((HEADS * TOK, HEAD), jnp.float32),
        scratch_shapes=[pltpu.VMEM((HEADS * TOK, GROUP * PART), jnp.bfloat16)],
        compiler_params=pltpu.CompilerParams(vmem_limit_bytes=32 * 1024 * 1024),
        cost_estimate=cost(15),
        name="mix",
    )(codes, weights, values)


def shards(queries, keys, values, mem_keys, mem_values, knn_index, block_slot, gate_bias, w_out):
    send = functools.partial(
        lax.all_to_all, axis_name=("seq", "mem"), split_axis=0, concat_axis=0, tiled=True
    )
    planes = lax.axis_size("seq")
    near = lax.axis_size("mem")
    near_queries = lax.all_gather(turn(queries[0]), "mem", axis=0, tiled=True).reshape(near, HEADS * TOK, HEAD)
    line_keys = lax.all_gather(mem_keys, "seq", axis=0, tiled=True)
    own = jnp.concatenate([keys[0], values[0]], axis=1)
    blocks = [own] + [
        lax.ppermute(own, "seq", [(i, i + back) for i in range(planes - back)]) for back in range(1, planes)
    ]

    lookups = knn_index[0].transpose(1, 0, 2).reshape(TOK * HEADS * TOPK // ROWS, ROWS)
    asked, places = route(lookups, block_slot)
    wanted = lax.all_to_all(
        asked.reshape(planes, near, CAP + 128), "mem", split_axis=1, concat_axis=1, tiled=True
    )
    codes = lax.all_to_all(wanted, "seq", split_axis=0, concat_axis=0, tiled=True).reshape(DEVS, CAP + 128)
    wanted = wanted.reshape(DEVS, CAP + 128)

    query = queries[0].reshape(TOK, HEADS, HEAD)
    seen = jnp.concatenate(blocks, axis=0)
    key_rows = seen[:, : HEADS * HEAD].reshape(-1, HEADS, HEAD)
    value_rows = seen[:, HEADS * HEAD :].reshape(-1, HEADS, HEAD)
    local = jnp.einsum("qhd,khd->hqk", query, key_rows, preferred_element_type=jnp.float32) * HEAD ** (-0.5)
    back = jnp.arange(seen.shape[0], dtype=jnp.int32) // TOK
    within = jnp.arange(seen.shape[0], dtype=jnp.int32) % TOK
    here = (back == 0)[None, :] & (within[None, :] <= jnp.arange(TOK, dtype=jnp.int32)[:, None])
    earlier = (back > 0) & (back <= lax.axis_index("seq"))
    local = jnp.where((here | earlier[None, :])[None], local, -jnp.inf)
    probs = jax.nn.softmax(local, axis=-1).astype(jnp.bfloat16)
    local_out = jnp.einsum("hqk,khd->hqd", probs, value_rows, preferred_element_type=jnp.float32)
    codes, local_out = lax.optimization_barrier((codes, local_out))

    picked = pick(codes, mem_values)
    first = send(picked[0])
    score_one, later = score(wanted, near_queries, line_keys, 0, picked[1])
    second = send(later)
    score_two, last = score(wanted, near_queries, line_keys, 1, picked[2], first)
    scored = join(score_one, score_two, second).reshape(planes, near, CAP)
    scores = lax.all_to_all(scored, "mem", split_axis=1, concat_axis=1, tiled=True).reshape(DEVS, CAP)
    third = send(last)
    weights = weigh(places, scores)
    sums = sum(mix(asked, weights, rows, part) for part, rows in enumerate((first, second, third)))
    mem_out = sums.reshape(HEADS, TOK, HEAD)

    gate = jax.nn.sigmoid(gate_bias)[:, None, None]
    combined = (gate * mem_out + (1.0 - gate) * local_out).astype(jnp.bfloat16)
    combined = combined.transpose(1, 0, 2).reshape(TOK, HEADS * HEAD)
    mixed = jnp.dot(combined, w_out, preferred_element_type=jnp.float32).astype(jnp.bfloat16)
    return mixed[None]


def solution(mesh):
    return jax.shard_map(
        shards,
        mesh=mesh,
        in_specs=(
            P("mem", "seq", None),
            P("mem", "seq", None),
            P("mem", "seq", None),
            P(("seq", "mem"), None),
            P(("seq", "mem"), None),
            P("mem", "seq", None, None),
            P(),
            P(),
            P(),
        ),
        out_specs=P("mem", "seq", None),
        check_vma=False,
    )
```

time: 497 us -> 400 us (0.80)
  blocking collectives: 96.7 us -> 0 us
  waiting for transfers between devices: 109 us -> 16.6 us
  Pallas kernels: 237 us -> 275 us
  starting transfers between devices: 20.4 us -> 53.9 us
  local copies, waits for them, and re-layouts: 12.6 us -> 28.7 us
    all_to_all x3 -> x0, blocking collectives: 96.7 us -> none  [the longest x1 58.7 us: shards(): first = send(picked[0])]
    ppermute x3, waiting for transfers between devices: 56.2 us -> 0.01 us  [shards(): lax.ppermute(own, 'seq', [(i, i + back) for i in range(planes - back)])]
    pallas_call x4 -> x6, Pallas kernels: 155 us -> 194 us  [the longest x2 99.2 us: score(): pl.pallas_call(score_kernel, grid=(steps,), in_specs=[pl.BlockSpec((GROUP...]
    all_to_all x1 -> x5, waiting for transfers between devices: 52.9 us -> 15.8 us  [the longest x1 8.3 us: shards(): lax.all_to_all(scored, 'mem', split_axis=1, concat_axis=1, tiled=True)]
    all_to_all x1 -> x5, starting transfers between devices: 5.1 us -> 37 us  [the longest x1 10.2 us: shards(): second = send(later)]
    unnamed x31 -> x39, local copies, waits for them, and re-layouts: 9.49 us -> 23.7 us
    pallas_call x1, Pallas kernels: 38.3 us -> 28.7 us  [weigh(): pl.pallas_call(weigh_kernel, out_shape=jax.ShapeDtypeStruct((DEVS, CAP),...]
    pallas_call x3, Pallas kernels: 43.2 us -> 52 us  [mix(): pl.pallas_call(mix_kernel, grid=(DEVS // GROUP,), in_specs=[pl.BlockSpec(...]
  transfers between devices with their start and end apart: 6 -> 11, of which waited for: 4 -> 3; matrix products, arithmetic and copies ran while one was open for 1% -> 3% of each run, Pallas kernels for 32% -> 64%
where the time goes in v3:
time: 400 us; the launch traced here: 399 us
  Pallas kernels  275 us (69%)
  starting transfers between devices  53.9 us (13%)
  local copies, waits for them, and re-layouts  28.7 us (7%)
  waiting for transfers between devices  16.6 us (4%)
  between operations  13.8 us (3%)
  matrix products  9.89 us (2%)
    pallas_call x2, Pallas kernels, score(): pl.pallas_call(score_kernel, grid=(steps,), in_specs=[pl.BlockSpec((GROUP...  99.2 us
    pallas_call x1, Pallas kernels, pick(): pl.pallas_call(pick_kernel, grid=(DEVS // GROUP,), in_specs=[CODES, START...  69.3 us
    pallas_call x3, Pallas kernels, mix(): pl.pallas_call(mix_kernel, grid=(DEVS // GROUP,), in_specs=[pl.BlockSpec(...  52 us
    pallas_call x1, Pallas kernels, weigh(): pl.pallas_call(weigh_kernel, out_shape=jax.ShapeDtypeStruct((DEVS, CAP),...  28.7 us
    unnamed x39, local copies, waits for them, and re-layouts  23.7 us
    pallas_call x1, Pallas kernels, route(): pl.pallas_call(route_kernel, out_shape=[jax.ShapeDtypeStruct((DEVS, CAP +...  22.1 us
    ppermute x3, starting transfers between devices, shards(): lax.ppermute(own, 'seq', [(i, i + back) for i in range(planes - back)])  10.3 us
    all_to_all x1, starting transfers between devices, shards(): second = send(later)  10.2 us
  transfers between devices with their start and end apart: 11, of which 3 were waited for; matrix products, arithmetic and copies ran while one was open for 3% of the time, Pallas kernels for 64%

profile of v3, /device:TPU:1, one launch (start us, length us, event | category | flops | bytes accessed | tf_op | source)
XLA Modules:
  0.0 398.9 jit_solution(7362307547895418537)
XLA Ops:
  11.3 6.5 %collective-permute-start.2 = (bf16[128,2048]{0,1:T(8,128)(2,1)S(1)}, bf16[128,2048]{0,1:T(8,128)(2,1)S(1)}, u32[]{:S(2)}, u32[]{:S(2)}) collective-permute-start(bf16[128,2048]{0,1:T(8,128)(2,1)S(1)} %pad_maximum_fusion.1), channel_id=1, source_target_pairs={{0,96},{1,97},{2,98},{3,99},{4,100},{5,101},{6,102},{7,103},{8,104... | collective-permute-start | bytes 1572872 | tf_op jit(solution)/shard_map/ppermute | solution.py:372
  19.2 2.5 collective-permute-start
  23.0 22.1 %route.1 = (s32[128,512]{1,0:T(8,128)S(1)}, s32[128,256]{1,0:T(8,128)S(1)}) custom-call(s32[128,256]{1,0:T(8,128)S(1)} %reshape.119.look_ref, s32[8,128]{1,0:T(8,128)S(1)} %bitcast.39), custom_call_target="tpu_custom_call" | custom-call | flops 22000001024 | bytes 22000000 | tf_op jit(solution)/shard_map/route/pallas_call | solution.py:103
  46.7 8.3 %all-to-all-start = ((s32[4,32,512]{2,0,1:T(4,128)}), s32[4,32,512]{2,0,1:T(4,128)S(1)}, u32[]{:S(2)}, u32[]{:S(2)}) async-start(s32[4,32,512]{2,0,1:T(4,128)} %copy.37), calls=%async_computation | async-start | bytes 524288 | tf_op jit(solution)/shard_map/all_to_all | solution.py:377
  56.7 7.3 %all-to-all-done = s32[4,32,512]{2,0,1:T(4,128)S(1)} async-done(((s32[4,32,512]{2,0,1:T(4,128)}), s32[4,32,512]{2,0,1:T(4,128)S(1)}, u32[]{:S(2)}, u32[]{:S(2)}) %all-to-all-start) | async-done | bytes 262176 | tf_op jit(solution)/shard_map/all_to_all | solution.py:377
  64.8 3.4 all-to-all-start.1
  68.6 3.2 fusion.32
  71.8 3.0 fusion.5
  75.0 69.3 %pick.1 = (bf16[128,128,128]{2,1,0:T(8,128)(2,1)S(1)}, bf16[128,128,128]{2,1,0:T(8,128)(2,1)S(1)}, bf16[128,128,128]{2,1,0:T(8,128)(2,1)S(1)}) custom-call(s32[128,512]{1,0:T(8,128)S(1)} %bitcast.36, s32[128,512]{1,0:T(8,128)S(1)} %bitcast.37, bf16[512,1024]{1,0:T(8,128)(2,1)S(1)} %copy-done.13), custom_call_target="tpu_custom_call" | custom-call | flops 44999999488 | bytes 45000000 | tf_op jit(solution)/shard_map/pick/pallas_call | solution.py:187
  150.4 7.7 %all-to-all-start.2 = ((bf16[128,128,128]{2,1,0:T(8,128)(2,1)}), bf16[128,128,128]{2,1,0:T(8,128)(2,1)}, u32[]{:S(2)}, u32[]{:S(2)}) async-start(bf16[128,128,128]{2,1,0:T(8,128)(2,1)} %copy-done.6), calls=%async_computation.2 | async-start | bytes 8388608 | tf_op jit(solution)/shard_map/all_to_all | solution.py:398
  158.1 2.2 copy-done.4
  160.3 2.2 copy-done.11
  162.5 49.6 %score.2 = (f32[64,384]{1,0:T(8,128)S(1)}, bf16[128,128,128]{2,1,0:T(8,128)(2,1)S(1)}) custom-call(s32[128,512]{1,0:T(8,128)} %bitcast.4.code_ref.start_ref, s32[128,512]{1,0:T(8,128)} %bitcast.4.code_ref.start_ref, bf16[2048,1024]{1,0:T(8,128)(2,1)S(1)} %copy-done.11, bf16[32,1024,128]{2,1,0:T(8,128)(2,1)} %bitcast.53, ...), custom_call_target="tpu_custom_call", output_to_operand_aliasing={{1}: (4, {})} | custom-call | flops 40000000000 | bytes 40000000 | tf_op jit(solution)/shard_map/score/pallas_call | solution.py:214
  214.7 10.2 %all-to-all-start.3 = ((bf16[128,128,128]{2,1,0:T(8,128)(2,1)}), bf16[128,128,128]{2,1,0:T(8,128)(2,1)}, u32[]{:S(2)}, u32[]{:S(2)}) async-start(bf16[128,128,128]{2,1,0:T(8,128)(2,1)} %copy-done.5), calls=%async_computation.3 | async-start | bytes 8388608 | tf_op jit(solution)/shard_map/all_to_all | solution.py:400
  227.1 2.2 copy-done.12
  229.3 49.6 %score.3 = (f32[64,384]{1,0:T(8,128)S(1)}, bf16[128,128,128]{2,1,0:T(8,128)(2,1)S(1)}) custom-call(s32[128,512]{1,0:T(8,128)} %bitcast.4.code_ref.start_ref, s32[128,512]{1,0:T(8,128)} %bitcast.4.code_ref.start_ref, bf16[2048,1024]{1,0:T(8,128)(2,1)S(1)} %copy-done.12, bf16[32,1024,128]{2,1,0:T(8,128)(2,1)} %bitcast.54, ...), custom_call_target="tpu_custom_call", output_to_operand_aliasing={{1}: (4, {})} | custom-call | flops 40000000000 | bytes 40000000 | tf_op jit(solution)/shard_map/score/pallas_call | solution.py:214
  284.9 7.4 %all-to-all-start.4 = ((f32[4,32,384]{2,0,1:T(4,128)}), f32[4,32,384]{2,0,1:T(4,128)S(1)}, u32[]{:S(2)}, u32[]{:S(2)}) async-start(f32[4,32,384]{2,0,1:T(4,128)} %copy.46), calls=%async_computation.4 | async-start | bytes 393216 | tf_op jit(solution)/shard_map/all_to_all | solution.py:403
  292.3 8.3 %all-to-all-done.4 = f32[4,32,384]{2,0,1:T(4,128)S(1)} async-done(((f32[4,32,384]{2,0,1:T(4,128)}), f32[4,32,384]{2,0,1:T(4,128)S(1)}, u32[]{:S(2)}, u32[]{:S(2)}) %all-to-all-start.4) | async-done | bytes 196640 | tf_op jit(solution)/shard_map/all_to_all | solution.py:403
  300.6 6.6 %all-to-all-start.5 = ((bf16[128,128,128]{2,1,0:T(8,128)(2,1)}), bf16[128,128,128]{2,1,0:T(8,128)(2,1)}, u32[]{:S(2)}, u32[]{:S(2)}) async-start(bf16[128,128,128]{2,1,0:T(8,128)(2,1)} %copy-done.2), calls=%async_computation.5 | async-start | bytes 8388608 | tf_op jit(solution)/shard_map/all_to_all | solution.py:404
  307.2 28.7 %weigh.1.weight_ref = f32[128,384]{1,0:T(8,128)S(1)} custom-call(s32[128,256]{1,0:T(8,128)S(1)} %get-tuple-element.17.place_ref, f32[128,384]{1,0:T(8,128)S(1)} %bitcast.38), custom_call_target="tpu_custom_call" | custom-call | flops 22000001024 | bytes 22000000 | tf_op jit(solution)/shard_map/weigh/pallas_call | solution.py:308
  335.9 17.3 %mix.3 = f32[1024,128]{1,0:T(8,128)S(1)} custom-call(s32[128,512]{1,0:T(8,128)S(1)} %copy-done.8, f32[128,384]{1,0:T(8,128)S(1)} %weigh.1.weight_ref, bf16[128,128,128]{2,1,0:T(8,128)(2,1)} %all-to-all-done.2.refs_1_.value_ref), custom_call_target="tpu_custom_call" | custom-call | flops 15000000512 | bytes 15000000 | tf_op jit(solution)/shard_map/mix/pallas_call | solution.py:345
  353.2 17.3 %mix.4 = f32[1024,128]{1,0:T(8,128)S(1)} custom-call(s32[128,512]{1,0:T(8,128)S(1)} %copy-done.8, f32[128,384]{1,0:T(8,128)S(1)} %weigh.1.weight_ref, bf16[128,128,128]{2,1,0:T(8,128)(2,1)} %all-to-all-done.3._.value_ref), custom_call_target="tpu_custom_call" | custom-call | flops 15000000512 | bytes 15000000 | tf_op jit(solution)/shard_map/mix/pallas_call | solution.py:345
  370.5 17.4 %mix.5 = f32[1024,128]{1,0:T(8,128)S(1)} custom-call(s32[128,512]{1,0:T(8,128)S(1)} %copy-done.8, f32[128,384]{1,0:T(8,128)S(1)} %weigh.1.weight_ref, bf16[128,128,128]{2,1,0:T(8,128)(2,1)} %all-to-all-done.5.value_ref), custom_call_target="tpu_custom_call" | custom-call | flops 15000000512 | bytes 15000000 | tf_op jit(solution)/shard_map/mix/pallas_call | solution.py:345
  388.3 3.7 fusion.1
  (68 shorter events, 29.3 us)
Async XLA Ops:
  6.5 16.5 %copy-start.14 = (s32[1024]{0:T(1024)S(1)}, s32[1024]{0:T(1024)}, u32[]{:S(2)}) copy-start(s32[1024]{0:T(1024)} %param.15) | copy-start | bytes 12292
  6.5 151.5 %all-gather.3.cloned.1.call-start = ((), (), s32[]{:S(2)}) async-start(), calls=%async_computation.6 | async-start | bytes 5242880 | tf_op jit(solution)/shard_map/all_gather | solution.py:369
  7.3 150.8 %all-gather.5.cloned.1.call-start = ((), (), s32[]{:S(2)}) async-start(), calls=%async_computation.7 | async-start | bytes 8650752 | tf_op jit(solution)/shard_map/all_gather | solution.py:368
  11.3 56.9 %collective-permute-start.2 = (bf16[128,2048]{0,1:T(8,128)(2,1)S(1)}, bf16[128,2048]{0,1:T(8,128)(2,1)S(1)}, u32[]{:S(2)}, u32[]{:S(2)}) collective-permute-start(bf16[128,2048]{0,1:T(8,128)(2,1)S(1)} %pad_maximum_fusion.1), channel_id=1, source_target_pairs={{0,96},{1,97},{2,98},{3,99},{4,100},{5,101},{6,102},{7,103},{8,104... | collective-permute-start | bytes 1572872 | tf_op jit(solution)/shard_map/ppermute | solution.py:372
  17.9 50.4 %collective-permute-start.1 = (bf16[128,2048]{0,1:T(8,128)(2,1)S(1)}, bf16[128,2048]{0,1:T(8,128)(2,1)S(1)}, u32[]{:S(2)}, u32[]{:S(2)}) collective-permute-start(bf16[128,2048]{0,1:T(8,128)(2,1)S(1)} %pad_maximum_fusion.1), channel_id=1, source_target_pairs={{0,64},{32,96},{1,65},{33,97},{2,66},{34,98},{3,67},{35,99},{4,68}... | collective-permute-start | bytes 1572872 | tf_op jit(solution)/shard_map/ppermute | solution.py:372
  19.2 49.1 %collective-permute-start = (bf16[128,2048]{0,1:T(8,128)(2,1)S(1)}, bf16[128,2048]{0,1:T(8,128)(2,1)S(1)}, u32[]{:S(2)}, u32[]{:S(2)}) collective-permute-start(bf16[128,2048]{0,1:T(8,128)(2,1)S(1)} %pad_maximum_fusion.1), channel_id=1, source_target_pairs={{0,32},{32,64},{64,96},{1,33},{33,65},{65,97},{2,34},{34,66},{66,9... | collective-permute-start | bytes 1572872 | tf_op jit(solution)/shard_map/ppermute | solution.py:372
  23.0 32.1 %copy-start.15 = (bf16[1,128,1024]{2,1,0:T(8,128)(2,1)S(1)}, bf16[1,128,1024]{2,1,0:T(8,128)(2,1)}, u32[]{:S(2)}) copy-start(bf16[1,128,1024]{2,1,0:T(8,128)(2,1)} %param.9) | copy-start | bytes 786436
  46.7 17.3 %all-to-all-start = ((s32[4,32,512]{2,0,1:T(4,128)}), s32[4,32,512]{2,0,1:T(4,128)S(1)}, u32[]{:S(2)}, u32[]{:S(2)}) async-start(s32[4,32,512]{2,0,1:T(4,128)} %copy.37), calls=%async_computation | async-start | bytes 524288 | tf_op jit(solution)/shard_map/all_to_all | solution.py:377
  64.8 10.2 %all-to-all-start.1 = ((s32[4,32,512]{2,1,0:T(8,128)}), s32[4,32,512]{2,1,0:T(8,128)S(1)}, u32[]{:S(2)}, u32[]{:S(2)}) async-start(s32[4,32,512]{2,1,0:T(8,128)} %copy.38), calls=%async_computation.1 | async-start | bytes 524288 | tf_op jit(solution)/shard_map/all_to_all | solution.py:380
  71.8 3.2 copy-start.13
  144.3 2.0 copy-start
  146.4 2.0 copy-start.3
  150.4 64.3 %all-to-all-start.2 = ((bf16[128,128,128]{2,1,0:T(8,128)(2,1)}), bf16[128,128,128]{2,1,0:T(8,128)(2,1)}, u32[]{:S(2)}, u32[]{:S(2)}) async-start(bf16[128,128,128]{2,1,0:T(8,128)(2,1)} %copy-done.6), calls=%async_computation.2 | async-start | bytes 8388608 | tf_op jit(solution)/shard_map/all_to_all | solution.py:398
  158.1 2.2 copy-start.4
  160.3 2.2 copy-start.11
  212.0 2.0 copy-start.5
  214.7 66.8 %all-to-all-start.3 = ((bf16[128,128,128]{2,1,0:T(8,128)(2,1)}), bf16[128,128,128]{2,1,0:T(8,128)(2,1)}, u32[]{:S(2)}, u32[]{:S(2)}) async-start(bf16[128,128,128]{2,1,0:T(8,128)(2,1)} %copy-done.5), calls=%async_computation.3 | async-start | bytes 8388608 | tf_op jit(solution)/shard_map/all_to_all | solution.py:400
  224.9 2.2 copy-start.1
  227.1 2.2 copy-start.12
  281.5 10.7 %copy-start.17 = (f32[8]{0:T(128)S(1)}, f32[8]{0:T(128)}, u32[]{:S(2)}) copy-start(f32[8]{0:T(128)} %param.16) | copy-start | bytes 100
  284.9 15.7 %all-to-all-start.4 = ((f32[4,32,384]{2,0,1:T(4,128)}), f32[4,32,384]{2,0,1:T(4,128)S(1)}, u32[]{:S(2)}, u32[]{:S(2)}) async-start(f32[4,32,384]{2,0,1:T(4,128)} %copy.46), calls=%async_computation.4 | async-start | bytes 393216 | tf_op jit(solution)/shard_map/all_to_all | solution.py:403
  300.6 70.0 %all-to-all-start.5 = ((bf16[128,128,128]{2,1,0:T(8,128)(2,1)}), bf16[128,128,128]{2,1,0:T(8,128)(2,1)}, u32[]{:S(2)}, u32[]{:S(2)}) async-start(bf16[128,128,128]{2,1,0:T(8,128)(2,1)} %copy-done.2), calls=%async_computation.5 | async-start | bytes 8388608 | tf_op jit(solution)/shard_map/all_to_all | solution.py:404
  307.2 28.7 %copy-start.8 = (s32[128,512]{1,0:T(8,128)S(1)}, s32[128,512]{1,0:T(8,128)}, u32[]{:S(2)}) copy-start(s32[128,512]{1,0:T(8,128)} %copy-done.7) | copy-start | bytes 786436
  370.5 17.5 %copy-start.16 = (f32[8,128,128]{2,1,0:T(8,128)S(1)}, f32[8,128,128]{2,1,0:T(8,128)}, u32[]{:S(2)}) copy-start(f32[8,128,128]{2,1,0:T(8,128)} %fusion.5) | copy-start | bytes 1572868
  (5 other events, 5.9 us)
Sparse Core Ops, SparseCore 0:
  9.0 69.7 all-gather.2
  81.0 55.4 all-gather.4

commit v4 on v3

--- a/solution.py
+++ b/solution.py
@@ -18,6 +18,7 @@
 PART = 128
 PARTS = CAP // PART
 GROUP = 8
+PICK = 16
 BATCH = 8
 ROWS = 256
 WINDOW = 80
@@ -133,72 +134,97 @@
 
 
 def pick_rows(code_ref, start_ref, mem_ref, wanted, found, hot):
+    group = code_ref.shape[0]
+
     @pl.when(pl.program_id(0) == 0)
     def _():
-        wanted[CAP:, :] = jnp.full((WINDOW, GROUP), -1, jnp.int32)
+        wanted[CAP:, :] = jnp.full((WINDOW, group), -1.0, jnp.float32)
         found[...] = jnp.zeros_like(found)
 
     for part in range(PARTS):
         span = slice(part * PART, (part + 1) * PART)
         code = jnp.transpose(code_ref[:, span])
-        wanted[span, :] = (code & (MEM_DEV - 1)) + (code >> 16) * MEM_DEV
-    row_ids = lax.broadcasted_iota(jnp.int32, (WINDOW, MEM_DEV), 1)
+        wanted[span, :] = ((code & (MEM_DEV - 1)) + (code >> 16) * MEM_DEV).astype(jnp.float32)
+    lanes = lax.broadcasted_iota(jnp.int32, (WINDOW, 128), 1).astype(jnp.float32)
+    lane_ids = [lanes.astype(jnp.bfloat16), (lanes + 128).astype(jnp.bfloat16)]
+
+    def product(h, spots, hot):
+        for i, at in enumerate(spots):
+            col = jnp.broadcast_to(wanted[pl.ds(at, WINDOW), i : i + 1], (WINDOW, 128))
+            low = (col - h * MEM_DEV).astype(jnp.bfloat16)
+            high = (col - (h * MEM_DEV + 256)).astype(jnp.bfloat16)
+            for k, part in enumerate((low, low, high, high)):
+                hot[i * WINDOW : (i + 1) * WINDOW, k * 128 : (k + 1) * 128] = jnp.where(
+                    part == lane_ids[k % 2], jnp.bfloat16(1), jnp.bfloat16(0)
+                )
+        return jnp.dot(hot[...], mem_ref[:, h * HEAD : (h + 1) * HEAD], preferred_element_type=jnp.float32)
+
+    def keep(h, i, at, rows):
+        head = wanted[pl.ds(at, rows.shape[0]), i : i + 1]
+        own = (head >= h * MEM_DEV) & (head < (h + 1) * MEM_DEV)
+        found[i, pl.ds(at, rows.shape[0]), :] = jnp.where(own, rows, found[i, pl.ds(at, rows.shape[0]), :])
+
+    begins = [[start_ref[i, h] // 8 * 8 for i in range(group)] for h in range(HEADS)]
     for h in range(HEADS):
-        begins = [start_ref[i, h] // 8 * 8 for i in range(GROUP)]
-        most = start_ref[0, h + 1] - begins[0]
-        for i in range(1, GROUP):
-            most = jnp.maximum(most, start_ref[i, h + 1] - begins[i])
-
-        def one_window(w, carry, h=h, begins=begins):
-            for i in range(GROUP):
-                at = pl.multiple_of(jnp.minimum(begins[i] + w * WINDOW, CAP), 8)
-                col = wanted[pl.ds(at, WINDOW), i : i + 1] - h * MEM_DEV
-                mine = slice(i * WINDOW, (i + 1) * WINDOW)
-                hot[mine, :] = one_hot(col == row_ids)
-                rows = jnp.dot(
-                    hot[mine, :], mem_ref[:, h * HEAD : (h + 1) * HEAD], preferred_element_type=jnp.float32
-                )
-                own = (col[:8] >= 0) & (col[:8] < MEM_DEV)
-                found[i, pl.ds(at, 8), :] = jnp.where(own, rows[:8], found[i, pl.ds(at, 8), :])
-                found[i, pl.ds(at + 8, WINDOW - 8), :] = rows[8:]
+        spots = [pl.multiple_of(at, 8) for at in begins[h]]
+        rows = product(h, spots, hot.at[h % 2])
+        for i, at in enumerate(spots):
+            mine = rows[i * WINDOW : (i + 1) * WINDOW]
+            keep(h, i, at, mine[:8])
+            found[i, pl.ds(at + 8, WINDOW - 8), :] = mine[8:]
+
+    for h in range(HEADS):
+        most = start_ref[0, h + 1] - begins[h][0]
+        for i in range(1, group):
+            most = jnp.maximum(most, start_ref[i, h + 1] - begins[h][i])
+
+        def one_window(w, carry, h=h):
+            spots = [pl.multiple_of(jnp.minimum(at + w * WINDOW, CAP), 8) for at in begins[h]]
+            rows = product(h, spots, hot.at[0])
+            for i, at in enumerate(spots):
+                keep(h, i, at, rows[i * WINDOW : (i + 1) * WINDOW])
             return carry
 
-        lax.fori_loop(0, (most + WINDOW - 1) // WINDOW, one_window, 0)
-
-
-PICK_SCRATCH = [
-    pltpu.VMEM((CAP + WINDOW, GROUP), jnp.int32),
-    pltpu.VMEM((GROUP, CAP + WINDOW, HEAD), jnp.float32),
-    pltpu.VMEM((GROUP * WINDOW, MEM_DEV), jnp.bfloat16),
-]
-CODES = pl.BlockSpec((GROUP, CAP), lambda g: (g, 0))
-STARTS = pl.BlockSpec((GROUP, 128), lambda g: (g, CAP // 128), memory_space=pltpu.SMEM)
-
-
-def pick_kernel(code_ref, start_ref, value_ref, *refs):
-    found = refs[PARTS + 1]
-    pick_rows(code_ref, start_ref, value_ref, *refs[PARTS:])
-    for i in range(GROUP):
-        for part in range(PARTS):
-            refs[part][i] = found[i, part * PART : (part + 1) * PART, :].astype(jnp.bfloat16)
+        lax.fori_loop(1, (most + WINDOW - 1) // WINDOW, one_window, 0)
+
+
+def pick_specs(group):
+    specs = [
+        pl.BlockSpec((group, CAP), lambda g: (g, 0)),
+        pl.BlockSpec((group, 128), lambda g: (g, CAP // 128), memory_space=pltpu.SMEM),
+    ]
+    scratch = [
+        pltpu.VMEM((CAP + WINDOW, group), jnp.float32),
+        pltpu.VMEM((group, CAP + WINDOW, HEAD), jnp.float32),
+        pltpu.VMEM((2, group * WINDOW, MEM_DEV), jnp.bfloat16),
+    ]
+    return specs, scratch
+
+
+def pick_kernel(code_ref, start_ref, value_ref, first_ref, last_ref, wanted, found, hot):
+    pick_rows(code_ref, start_ref, value_ref, wanted, found, hot)
+    for i in range(code_ref.shape[0]):
+        first_ref[i] = found[i, : CAP - PART, :].astype(jnp.bfloat16)
+        last_ref[i] = found[i, CAP - PART : CAP, :].astype(jnp.bfloat16)
 
 
 def pick(codes, values):
+    specs, scratch = pick_specs(PICK)
+    sizes = (CAP - PART, PART)
     return pl.pallas_call(
         pick_kernel,
-        grid=(DEVS // GROUP,),
-        in_specs=[CODES, STARTS, pl.BlockSpec((MEM_DEV, HEADS * HEAD), lambda g: (0, 0))],
-        out_specs=[pl.BlockSpec((GROUP, PART, HEAD), lambda g: (g, 0, 0))] * PARTS,
-        out_shape=[jax.ShapeDtypeStruct((DEVS, PART, HEAD), jnp.bfloat16)] * PARTS,
-        scratch_shapes=PICK_SCRATCH,
+        grid=(DEVS // PICK,),
+        in_specs=specs + [pl.BlockSpec((MEM_DEV, HEADS * HEAD), lambda g: (0, 0))],
+        out_specs=[pl.BlockSpec((PICK, size, HEAD), lambda g: (g, 0, 0)) for size in sizes],
+        out_shape=[pltpu.HBM((DEVS, size, HEAD), jnp.bfloat16) for size in sizes],
+        scratch_shapes=scratch,
         compiler_params=pltpu.CompilerParams(vmem_limit_bytes=40 * 1024 * 1024),
-        cost_estimate=cost(45),
+        cost_estimate=cost(40),
         name="pick",
     )(codes, codes, values)
 
 
-def score_kernel(code_ref, start_ref, key_ref, query_ref, *refs):
-    out_ref, _, wanted, found, hot = refs[-5:]
+def score_kernel(code_ref, start_ref, key_ref, query_ref, _, out_ref, __, wanted, found, hot):
     pick_rows(code_ref, start_ref, key_ref, wanted, found, hot)
     ids = lax.broadcasted_iota(jnp.int32, (HEADS * TOK, CAP), 0)
     for i in range(GROUP):
@@ -208,46 +234,42 @@
         out_ref[i : i + 1, :] = jnp.sum(jnp.where(own, every, 0.0), axis=0, keepdims=True) * HEAD ** (-0.5)
 
 
-def score(codes, queries, keys, half, through, *ready):
+def score(codes, queries, keys, through):
     near = queries.shape[0] // GROUP
-    steps = DEVS // GROUP // 2
+    specs, scratch = pick_specs(GROUP)
     return pl.pallas_call(
         score_kernel,
-        grid=(steps,),
-        in_specs=[
-            pl.BlockSpec((GROUP, CAP), lambda g: (g + half * steps, 0)),
-            pl.BlockSpec((GROUP, 128), lambda g: (g + half * steps, CAP // 128), memory_space=pltpu.SMEM),
-            pl.BlockSpec((MEM_DEV, HEADS * HEAD), lambda g: ((g + half * steps) // near, 0)),
+        grid=(DEVS // GROUP,),
+        in_specs=specs
+        + [
+            pl.BlockSpec((MEM_DEV, HEADS * HEAD), lambda g: (g // near, 0)),
             pl.BlockSpec((GROUP, HEADS * TOK, HEAD), lambda g: (g % near, 0, 0)),
             pl.BlockSpec(memory_space=pl.ANY),
-        ]
-        + [pl.BlockSpec(memory_space=pl.ANY)] * len(ready),
-        out_specs=[CODES, pl.BlockSpec(memory_space=pl.ANY)],
+        ],
+        out_specs=[specs[0], pl.BlockSpec(memory_space=pl.ANY)],
         out_shape=[
-            jax.ShapeDtypeStruct((DEVS // 2, CAP), jnp.float32),
+            jax.ShapeDtypeStruct((DEVS, CAP), jnp.float32),
             jax.ShapeDtypeStruct(through.shape, through.dtype),
         ],
-        scratch_shapes=PICK_SCRATCH,
+        scratch_shapes=scratch,
         input_output_aliases={4: 1},
         compiler_params=pltpu.CompilerParams(vmem_limit_bytes=40 * 1024 * 1024),
-        cost_estimate=cost(40),
+        cost_estimate=cost(75),
         name="score",
-    )(codes, codes, keys, queries, through, *ready)
-
-
-def join_kernel(a_ref, b_ref, _, out_ref):
-    half = DEVS // 2
-    out_ref[:half, :] = a_ref[...]
-    out_ref[half:, :] = b_ref[...]
-
-
-def join(one, two, ready):
+    )(codes, codes, keys, queries, through)
+
+
+def join_kernel(a_ref, _, __, out_ref):
+    out_ref[...] = a_ref[...]
+
+
+def join(scores, *ready):
     return pl.pallas_call(
         join_kernel,
-        in_specs=[pl.BlockSpec(memory_space=pltpu.VMEM)] * 2 + [pl.BlockSpec(memory_space=pl.ANY)],
-        out_shape=jax.ShapeDtypeStruct((DEVS, CAP), jnp.float32),
+        in_specs=[pl.BlockSpec(memory_space=pltpu.VMEM)] + [pl.BlockSpec(memory_space=pl.ANY)] * len(ready),
+        out_shape=jax.ShapeDtypeStruct(scores.shape, scores.dtype),
         name="join",
-    )(one, two, ready)
+    )(scores, *ready)
 
 
 def weigh_kernel(place_ref, score_ref, out_ref, parts, near, total, slots, spread):
@@ -321,42 +343,51 @@
     )(places, scores)
 
 
-def mix_kernel(code_ref, weight_ref, value_ref, out_ref, spread):
-    step = pl.program_id(0)
-
-    @pl.when(step == 0)
+def mix_kernel(code_ref, start_ref, weight_ref, value_ref, out_ref, spread, rows, *, begin):
+    part = pl.program_id(1)
+    half = HEADS // 2
+
+    @pl.when((pl.program_id(0) == 0) & (part == 0))
     def _():
         out_ref[...] = jnp.zeros_like(out_ref)
 
+    slot = lax.broadcasted_iota(jnp.int32, (PART, HEAD), 0).astype(jnp.float32).astype(jnp.bfloat16)
     for i in range(GROUP):
         span = slice(i * PART, (i + 1) * PART)
-        query = code_ref[i : i + 1, :] >> 9
+        first = jnp.clip(start_ref[i, half] - (begin + part) * PART, 0, PART)
+        later = slot >= first.astype(jnp.float32).astype(jnp.bfloat16)
+        value = value_ref[i]
+        rows[span, :HEAD] = jnp.where(later, jnp.bfloat16(0), value)
+        rows[span, HEAD:] = jnp.where(later, value, jnp.bfloat16(0))
+        query = (code_ref[i : i + 1, :] >> 9) & (half * TOK - 1)
         weight = weight_ref[i : i + 1, :]
-        for h in range(HEADS):
+        for h in range(half):
             ids = lax.broadcasted_iota(jnp.int32, (TOK, PART), 0) + h * TOK
             spread[h * TOK : (h + 1) * TOK, span] = jnp.where(ids == query, weight, 0.0).astype(jnp.bfloat16)
-    rows = value_ref[...].reshape(GROUP * PART, HEAD)
-    for h in range(HEADS // 2):
-        span = slice(h * 2 * TOK, (h + 1) * 2 * TOK)
-        out_ref[span, :] += jnp.dot(spread[span, :], rows, preferred_element_type=jnp.float32)
-
-
-def mix(codes, weights, values, part):
-    return pl.pallas_call(
-        mix_kernel,
-        grid=(DEVS // GROUP,),
+    out_ref[...] += jnp.dot(spread[...], rows[...], preferred_element_type=jnp.float32)
+
+
+def mix(codes, weights, values, begin):
+    parts = values.shape[1] // PART
+    return pl.pallas_call(
+        functools.partial(mix_kernel, begin=begin),
+        grid=(DEVS // GROUP, parts),
         in_specs=[
-            pl.BlockSpec((GROUP, PART), lambda g: (g, part)),
-            pl.BlockSpec((GROUP, PART), lambda g: (g, part)),
-            pl.BlockSpec((GROUP, PART, HEAD), lambda g: (g, 0, 0)),
-        ],
-        out_specs=pl.BlockSpec((HEADS * TOK, HEAD), lambda g: (0, 0)),
-        out_shape=jax.ShapeDtypeStruct((HEADS * TOK, HEAD), jnp.float32),
-        scratch_shapes=[pltpu.VMEM((HEADS * TOK, GROUP * PART), jnp.bfloat16)],
+            pl.BlockSpec((GROUP, PART), lambda g, p: (g, begin + p)),
+            pl.BlockSpec((GROUP, 128), lambda g, p: (g, CAP // 128), memory_space=pltpu.SMEM),
+            pl.BlockSpec((GROUP, PART), lambda g, p: (g, begin + p)),
+            pl.BlockSpec((GROUP, PART, HEAD), lambda g, p: (g, p, 0)),
+        ],
+        out_specs=pl.BlockSpec((HEADS // 2 * TOK, 2 * HEAD), lambda g, p: (0, 0)),
+        out_shape=jax.ShapeDtypeStruct((HEADS // 2 * TOK, 2 * HEAD), jnp.float32),
+        scratch_shapes=[
+            pltpu.VMEM((HEADS // 2 * TOK, GROUP * PART), jnp.bfloat16),
+            pltpu.VMEM((GROUP * PART, 2 * HEAD), jnp.bfloat16),
+        ],
         compiler_params=pltpu.CompilerParams(vmem_limit_bytes=32 * 1024 * 1024),
-        cost_estimate=cost(15),
+        cost_estimate=cost(12 * parts),
         name="mix",
-    )(codes, weights, values)
+    )(codes, codes, weights, values)
 
 
 def shards(queries, keys, values, mem_keys, mem_values, knn_index, block_slot, gate_bias, w_out):
@@ -392,19 +423,15 @@
     local = jnp.where((here | earlier[None, :])[None], local, -jnp.inf)
     probs = jax.nn.softmax(local, axis=-1).astype(jnp.bfloat16)
     local_out = jnp.einsum("hqk,khd->hqd", probs, value_rows, preferred_element_type=jnp.float32)
-    codes, local_out = lax.optimization_barrier((codes, local_out))
-
-    picked = pick(codes, mem_values)
-    first = send(picked[0])
-    score_one, later = score(wanted, near_queries, line_keys, 0, picked[1])
-    second = send(later)
-    score_two, last = score(wanted, near_queries, line_keys, 1, picked[2], first)
-    scored = join(score_one, score_two, second).reshape(planes, near, CAP)
+    picked, later = pick(codes, mem_values)
+    first = send(picked)
+    scored, later = score(wanted, near_queries, line_keys, later)
+    scored = join(scored, first, local_out).reshape(planes, near, CAP)
     scores = lax.all_to_all(scored, "mem", split_axis=1, concat_axis=1, tiled=True).reshape(DEVS, CAP)
-    third = send(last)
+    last = send(later)
     weights = weigh(places, scores)
-    sums = sum(mix(asked, weights, rows, part) for part, rows in enumerate((first, second, third)))
-    mem_out = sums.reshape(HEADS, TOK, HEAD)
+    sums = mix(asked, weights, first, 0) + mix(asked, weights, last, PARTS - 1)
+    mem_out = jnp.concatenate([sums[:, :HEAD], sums[:, HEAD:]], axis=0).reshape(HEADS, TOK, HEAD)
 
     gate = jax.nn.sigmoid(gate_bias)[:, None, None]
     combined = (gate * mem_out + (1.0 - gate) * local_out).astype(jnp.bfloat16)

time: 400 us -> 339 us (0.85)
  Pallas kernels: 275 us -> 207 us
  waiting for transfers between devices: 16.6 us -> 43.3 us
  local copies, waits for them, and re-layouts: 28.7 us -> 14.9 us
  starting transfers between devices: 53.9 us -> 47.1 us
    pallas_call x6 -> x4, Pallas kernels: 220 us -> 153 us  [the longest x1 72.5 us: score(): pl.pallas_call(score_kernel, grid=(DEVS // GROUP,), in_specs=specs + [pl....]
    all_to_all x1, waiting for transfers between devices: 0.21 us -> 23.1 us  [shards(): lax.all_to_all(wanted, 'seq', split_axis=0, concat_axis=0, tiled=True)]
    unnamed x39 -> x29, local copies, waits for them, and re-layouts: 23.7 us -> 8.85 us
    all_to_all x3 -> x2, waiting for transfers between devices: 0.01 us -> 11.1 us  [the longest x1 11.1 us: shards(): first = send(picked)]
    all_to_all x3 -> x2, starting transfers between devices: 24.5 us -> 16.2 us  [the longest x1 10.6 us: shards(): first = send(picked)]
    all_to_all x1, waiting for transfers between devices: 7.29 us -> 0.01 us  [shards(): lax.all_to_all(asked.reshape(planes, near, CAP + 128), 'mem', split_axis=...]
  transfers between devices with their start and end apart: 11 -> 10, of which waited for: 3 -> 3; matrix products, arithmetic and copies ran while one was open for 3% -> 3% of each run, Pallas kernels for 64% -> 57%
where the time goes in v4:
time: 339 us; the launch traced here: 337 us
  Pallas kernels  207 us (61%)
  starting transfers between devices  47.1 us (14%)
  waiting for transfers between devices  43.3 us (13%)
  local copies, waits for them, and re-layouts  14.9 us (4%)
  between operations  13.8 us (4%)
  matrix products  7.9 us (2%)
    pallas_call x1, Pallas kernels, score(): pl.pallas_call(score_kernel, grid=(DEVS // GROUP,), in_specs=specs + [pl....  72.5 us
    pallas_call x1, Pallas kernels, pick(): pl.pallas_call(pick_kernel, grid=(DEVS // PICK,), in_specs=specs + [pl.Bl...  40.7 us
    pallas_call x2, Pallas kernels, mix(): pl.pallas_call(functools.partial(mix_kernel, begin=begin), grid=(DEVS //...  40.2 us
    pallas_call x1, Pallas kernels, weigh(): pl.pallas_call(weigh_kernel, out_shape=jax.ShapeDtypeStruct((DEVS, CAP),...  28.7 us
    all_to_all x1, waiting for transfers between devices, shards(): lax.all_to_all(wanted, 'seq', split_axis=0, concat_axis=0, tiled=True)  23.1 us
    pallas_call x1, Pallas kernels, route(): pl.pallas_call(route_kernel, out_shape=[jax.ShapeDtypeStruct((DEVS, CAP +...  22.1 us
    all_to_all x1, waiting for transfers between devices, shards(): first = send(picked)  11.1 us
    ppermute x3, starting transfers between devices, shards(): lax.ppermute(own, 'seq', [(i, i + back) for i in range(planes - back)])  11.1 us
  transfers between devices with their start and end apart: 10, of which 3 were waited for; matrix products, arithmetic and copies ran while one was open for 3% of the time, Pallas kernels for 57%

profile of v4, /device:TPU:1, one launch (start us, length us, event | category | flops | bytes accessed | tf_op | source)
XLA Modules:
  0.0 337.2 jit_solution(4097084325874876056)
XLA Ops:
  10.4 22.1 %route.1 = (s32[128,512]{1,0:T(8,128)S(1)}, s32[128,256]{1,0:T(8,128)S(1)}) custom-call(s32[128,256]{1,0:T(8,128)S(1)} %reshape.119.look_ref, s32[8,128]{1,0:T(8,128)S(1)} %bitcast.39), custom_call_target="tpu_custom_call" | custom-call | flops 22000001024 | bytes 22000000 | tf_op jit(solution)/shard_map/route/pallas_call | solution.py:104
  34.1 8.7 %all-to-all-start = ((s32[4,32,512]{2,0,1:T(4,128)}), s32[4,32,512]{2,0,1:T(4,128)S(1)}, u32[]{:S(2)}, u32[]{:S(2)}) async-start(s32[4,32,512]{2,0,1:T(4,128)} %copy.39), calls=%async_computation | async-start | bytes 524288 | tf_op jit(solution)/shard_map/all_to_all | solution.py:408
  43.2 5.7 %collective-permute-start.2 = (bf16[128,2048]{0,1:T(8,128)(2,1)S(1)}, bf16[128,2048]{0,1:T(8,128)(2,1)S(1)}, u32[]{:S(2)}, u32[]{:S(2)}) collective-permute-start(bf16[128,2048]{0,1:T(8,128)(2,1)S(1)} %pad_maximum_fusion.1), channel_id=1, source_target_pairs={{0,96},{1,97},{2,98},{3,99},{4,100},{5,101},{6,102},{7,103},{8,104... | collective-permute-start | bytes 1572872 | tf_op jit(solution)/shard_map/ppermute | solution.py:403
  48.9 2.1 collective-permute-start.1
  51.0 3.3 collective-permute-start
  55.1 3.6 %all-to-all-start.1 = ((s32[4,32,512]{2,1,0:T(8,128)}), s32[4,32,512]{2,1,0:T(8,128)S(1)}, u32[]{:S(2)}, u32[]{:S(2)}) async-start(s32[4,32,512]{2,1,0:T(8,128)} %copy.40), calls=%async_computation.1 | async-start | bytes 524288 | tf_op jit(solution)/shard_map/all_to_all | solution.py:411
  59.6 23.1 %all-to-all-done.1 = s32[4,32,512]{2,1,0:T(8,128)S(1)} async-done(((s32[4,32,512]{2,1,0:T(8,128)}), s32[4,32,512]{2,1,0:T(8,128)S(1)}, u32[]{:S(2)}, u32[]{:S(2)}) %all-to-all-start.1) | async-done | bytes 262176 | tf_op jit(solution)/shard_map/all_to_all | solution.py:411
  82.8 40.7 %pick.1 = (bf16[128,256,128]{2,1,0:T(8,128)(2,1)}, bf16[128,128,128]{2,1,0:T(8,128)(2,1)}) custom-call(s32[128,512]{1,0:T(8,128)S(1)} %bitcast.36, s32[128,512]{1,0:T(8,128)S(1)} %bitcast.37, bf16[512,1024]{1,0:T(8,128)(2,1)S(1)} %copy-done.6), custom_call_target="tpu_custom_call" | custom-call | flops 40000000000 | bytes 40000000 | tf_op jit(solution)/shard_map/pick/pallas_call | solution.py:214
  123.5 10.6 %all-to-all-start.2 = ((bf16[128,256,128]{2,1,0:T(8,128)(2,1)}), bf16[128,256,128]{2,1,0:T(8,128)(2,1)}, u32[]{:S(2)}, u32[]{:S(2)}) async-start(bf16[128,256,128]{2,1,0:T(8,128)(2,1)} %get-tuple-element.15), calls=%async_computation.2 | async-start | bytes 16777216 | tf_op jit(solution)/shard_map/all_to_all | solution.py:427
  136.5 2.2 fusion.32
  138.7 2.0 fusion.5
  141.7 2.2 copy-done
  143.9 2.2 copy-done.5
  146.1 72.5 %score.1 = (f32[128,384]{1,0:T(8,128)S(1)}, bf16[128,128,128]{2,1,0:T(8,128)(2,1)S(1)}) custom-call(s32[128,512]{1,0:T(8,128)} %bitcast.4.code_ref.start_ref, s32[128,512]{1,0:T(8,128)} %bitcast.4.code_ref.start_ref, bf16[2048,1024]{1,0:T(8,128)(2,1)S(1)} %copy-done.5, bf16[32,1024,128]{2,1,0:T(8,128)(2,1)} %bitcast.53, ...), custom_call_target="tpu_custom_call", output_to_operand_aliasing={{1}: (4, {})} | custom-call | flops 74999996416 | bytes 75000000 | tf_op jit(solution)/shard_map/score/pallas_call | solution.py:240
  218.6 2.0 copy-done.1
  221.2 11.1 %all-to-all-done.2._.value_ref = bf16[128,256,128]{2,1,0:T(8,128)(2,1)} async-done(((bf16[128,256,128]{2,1,0:T(8,128)(2,1)}), bf16[128,256,128]{2,1,0:T(8,128)(2,1)}, u32[]{:S(2)}, u32[]{:S(2)}) %all-to-all-start.2) | async-done | bytes 8388640 | tf_op jit(solution)/shard_map/all_to_all | solution.py:427
  234.0 1.7 copy.48
  235.7 7.6 %all-to-all-start.3 = ((f32[4,32,384]{2,0,1:T(4,128)}), f32[4,32,384]{2,0,1:T(4,128)S(1)}, u32[]{:S(2)}, u32[]{:S(2)}) async-start(f32[4,32,384]{2,0,1:T(4,128)} %copy.48), calls=%async_computation.3 | async-start | bytes 393216 | tf_op jit(solution)/shard_map/all_to_all | solution.py:430
  243.3 8.3 %all-to-all-done.3 = f32[4,32,384]{2,0,1:T(4,128)S(1)} async-done(((f32[4,32,384]{2,0,1:T(4,128)}), f32[4,32,384]{2,0,1:T(4,128)S(1)}, u32[]{:S(2)}, u32[]{:S(2)}) %all-to-all-start.3) | async-done | bytes 196640 | tf_op jit(solution)/shard_map/all_to_all | solution.py:430
  251.6 5.6 %all-to-all-start.4 = ((bf16[128,128,128]{2,1,0:T(8,128)(2,1)}), bf16[128,128,128]{2,1,0:T(8,128)(2,1)}, u32[]{:S(2)}, u32[]{:S(2)}) async-start(bf16[128,128,128]{2,1,0:T(8,128)(2,1)} %copy-done.1), calls=%async_computation.4 | async-start | bytes 8388608 | tf_op jit(solution)/shard_map/all_to_all | solution.py:431
  257.2 28.7 %weigh.1.weight_ref = f32[128,384]{1,0:T(8,128)S(1)} custom-call(s32[128,256]{1,0:T(8,128)S(1)} %get-tuple-element.12.place_ref, f32[128,384]{1,0:T(8,128)S(1)} %bitcast.38), custom_call_target="tpu_custom_call" | custom-call | flops 22000001024 | bytes 22000000 | tf_op jit(solution)/shard_map/weigh/pallas_call | solution.py:330
  285.9 26.6 %mix.2 = f32[512,256]{1,0:T(8,128)S(1)} custom-call(s32[128,512]{1,0:T(8,128)S(1)} %copy-done.3, s32[128,512]{1,0:T(8,128)S(1)} %copy-done.3, f32[128,384]{1,0:T(8,128)S(1)} %weigh.1.weight_ref, bf16[128,256,128]{2,1,0:T(8,128)(2,1)} %all-to-all-done.2._.value_ref), custom_call_target="tpu_custom_call" | custom-call | flops 24000000000 | bytes 24000000 | tf_op jit(solution)/shard_map/mix/pallas_call | solution.py:372
  312.6 13.5 %mix.3 = f32[512,256]{1,0:T(8,128)S(1)} custom-call(s32[128,512]{1,0:T(8,128)S(1)} %copy-done.3, s32[128,512]{1,0:T(8,128)S(1)} %copy-done.3, f32[128,384]{1,0:T(8,128)S(1)} %weigh.1.weight_ref, bf16[128,128,128]{2,1,0:T(8,128)(2,1)} %all-to-all-done.4.value_ref), custom_call_target="tpu_custom_call" | custom-call | flops 12000000000 | bytes 12000000 | tf_op jit(solution)/shard_map/mix/pallas_call | solution.py:372
  326.6 3.7 %fusion.1 = bf16[1,128,2048]{2,1,0:T(8,128)(2,1)} fusion(bf16[128,1024]{0,1:T(8,128)(2,1)S(1)} %bitcast.47, bf16[1024,2048]{1,0:T(8,128)(2,1)} %param.17), kind=kOutput, calls=%fused_computation.2 | convolution fusion | flops 537133056 | bytes 4980736 | tf_op jit(solution)/shard_map/dot_general | solution.py:439
  (57 shorter events, 13.7 us)
Async XLA Ops:
  6.5 3.8 %copy-start.7 = (s32[1024]{0:T(1024)S(1)}, s32[1024]{0:T(1024)}, u32[]{:S(2)}) copy-start(s32[1024]{0:T(1024)} %param.15) | copy-start | bytes 12292
  6.5 135.2 %all-gather.3.cloned.1.call-start = ((), (), s32[]{:S(2)}) async-start(), calls=%async_computation.5 | async-start | bytes 5242880 | tf_op jit(solution)/shard_map/all_gather | solution.py:400
  7.3 134.4 %all-gather.5.cloned.1.call-start = ((), (), s32[]{:S(2)}) async-start(), calls=%async_computation.6 | async-start | bytes 8650752 | tf_op jit(solution)/shard_map/all_gather | solution.py:399
  10.3 32.4 %copy-start.9 = (bf16[1,128,1024]{2,1,0:T(8,128)(2,1)S(1)}, bf16[1,128,1024]{2,1,0:T(8,128)(2,1)}, u32[]{:S(2)}) copy-start(bf16[1,128,1024]{2,1,0:T(8,128)(2,1)} %param.11) | copy-start | bytes 786436
  10.3 32.6 %copy-start.10 = (bf16[1,128,1024]{2,1,0:T(8,128)(2,1)S(1)}, bf16[1,128,1024]{2,1,0:T(8,128)(2,1)}, u32[]{:S(2)}) copy-start(bf16[1,128,1024]{2,1,0:T(8,128)(2,1)} %param.10) | copy-start | bytes 786436
  32.5 21.8 %copy-start.8 = (bf16[1,128,1024]{2,1,0:T(8,128)(2,1)S(1)}, bf16[1,128,1024]{2,1,0:T(8,128)(2,1)}, u32[]{:S(2)}) copy-start(bf16[1,128,1024]{2,1,0:T(8,128)(2,1)} %param.9) | copy-start | bytes 786436
  33.3 0.7 copy-start.2
  34.0 48.7 %copy-start.6 = (bf16[512,1024]{1,0:T(8,128)(2,1)S(1)}, bf16[512,1024]{1,0:T(8,128)(2,1)}, u32[]{:S(2)}) copy-start(bf16[512,1024]{1,0:T(8,128)(2,1)} %value_ref.1) | copy-start | bytes 3145732
  34.1 20.3 %all-to-all-start = ((s32[4,32,512]{2,0,1:T(4,128)}), s32[4,32,512]{2,0,1:T(4,128)S(1)}, u32[]{:S(2)}, u32[]{:S(2)}) async-start(s32[4,32,512]{2,0,1:T(4,128)} %copy.39), calls=%async_computation | async-start | bytes 524288 | tf_op jit(solution)/shard_map/all_to_all | solution.py:408
  43.2 90.9 %collective-permute-start.2 = (bf16[128,2048]{0,1:T(8,128)(2,1)S(1)}, bf16[128,2048]{0,1:T(8,128)(2,1)S(1)}, u32[]{:S(2)}, u32[]{:S(2)}) collective-permute-start(bf16[128,2048]{0,1:T(8,128)(2,1)S(1)} %pad_maximum_fusion.1), channel_id=1, source_target_pairs={{0,96},{1,97},{2,98},{3,99},{4,100},{5,101},{6,102},{7,103},{8,104... | collective-permute-start | bytes 1572872 | tf_op jit(solution)/shard_map/ppermute | solution.py:403
  48.9 85.2 %collective-permute-start.1 = (bf16[128,2048]{0,1:T(8,128)(2,1)S(1)}, bf16[128,2048]{0,1:T(8,128)(2,1)}, u32[]{:S(2)}, u32[]{:S(2)}) collective-permute-start(bf16[128,2048]{0,1:T(8,128)(2,1)S(1)} %pad_maximum_fusion.1), channel_id=1, source_target_pairs={{0,64},{32,96},{1,65},{33,97},{2,66},{34,98},{3,67},{35,99},{4,68}... | collective-permute-start | bytes 1572872 | tf_op jit(solution)/shard_map/ppermute | solution.py:403
  51.0 83.1 %collective-permute-start = (bf16[128,2048]{0,1:T(8,128)(2,1)S(1)}, bf16[128,2048]{0,1:T(8,128)(2,1)}, u32[]{:S(2)}, u32[]{:S(2)}) collective-permute-start(bf16[128,2048]{0,1:T(8,128)(2,1)S(1)} %pad_maximum_fusion.1), channel_id=1, source_target_pairs={{0,32},{32,64},{64,96},{1,33},{33,65},{65,97},{2,34},{34,66},{66,9... | collective-permute-start | bytes 1572872 | tf_op jit(solution)/shard_map/ppermute | solution.py:403
  55.1 27.6 %all-to-all-start.1 = ((s32[4,32,512]{2,1,0:T(8,128)}), s32[4,32,512]{2,1,0:T(8,128)S(1)}, u32[]{:S(2)}, u32[]{:S(2)}) async-start(s32[4,32,512]{2,1,0:T(8,128)} %copy.40), calls=%async_computation.1 | async-start | bytes 524288 | tf_op jit(solution)/shard_map/all_to_all | solution.py:411
  123.5 108.8 %all-to-all-start.2 = ((bf16[128,256,128]{2,1,0:T(8,128)(2,1)}), bf16[128,256,128]{2,1,0:T(8,128)(2,1)}, u32[]{:S(2)}, u32[]{:S(2)}) async-start(bf16[128,256,128]{2,1,0:T(8,128)(2,1)} %get-tuple-element.15), calls=%async_computation.2 | async-start | bytes 16777216 | tf_op jit(solution)/shard_map/all_to_all | solution.py:427
  135.7 0.8 copy-start.11
  141.7 2.2 copy-start
  143.9 2.2 copy-start.5
  218.5 2.0 copy-start.1
  220.5 0.7 copy-start.4
  232.3 10.9 %copy-start.12 = (f32[8]{0:T(128)S(1)}, f32[8]{0:T(128)}, u32[]{:S(2)}) copy-start(f32[8]{0:T(128)} %param.16) | copy-start | bytes 100
  235.7 15.9 %all-to-all-start.3 = ((f32[4,32,384]{2,0,1:T(4,128)}), f32[4,32,384]{2,0,1:T(4,128)S(1)}, u32[]{:S(2)}, u32[]{:S(2)}) async-start(f32[4,32,384]{2,0,1:T(4,128)} %copy.48), calls=%async_computation.3 | async-start | bytes 393216 | tf_op jit(solution)/shard_map/all_to_all | solution.py:430
  251.6 60.9 %all-to-all-start.4 = ((bf16[128,128,128]{2,1,0:T(8,128)(2,1)}), bf16[128,128,128]{2,1,0:T(8,128)(2,1)}, u32[]{:S(2)}, u32[]{:S(2)}) async-start(bf16[128,128,128]{2,1,0:T(8,128)(2,1)} %copy-done.1), calls=%async_computation.4 | async-start | bytes 8388608 | tf_op jit(solution)/shard_map/all_to_all | solution.py:431
  257.2 28.7 %copy-start.3 = (s32[128,512]{1,0:T(8,128)S(1)}, s32[128,512]{1,0:T(8,128)}, u32[]{:S(2)}) copy-start(s32[128,512]{1,0:T(8,128)} %copy-done.2) | copy-start | bytes 786436
Sparse Core Ops, SparseCore 0:
  9.0 68.5 all-gather.2
  79.9 56.3 all-gather.4

commit v5 on v4

--- a/solution.py
+++ b/solution.py
@@ -201,27 +201,28 @@
     return specs, scratch
 
 
-def pick_kernel(code_ref, start_ref, value_ref, first_ref, last_ref, wanted, found, hot):
+def pick_kernel(code_ref, start_ref, value_ref, _, first_ref, last_ref, wanted, found, hot):
     pick_rows(code_ref, start_ref, value_ref, wanted, found, hot)
     for i in range(code_ref.shape[0]):
         first_ref[i] = found[i, : CAP - PART, :].astype(jnp.bfloat16)
         last_ref[i] = found[i, CAP - PART : CAP, :].astype(jnp.bfloat16)
 
 
-def pick(codes, values):
+def pick(codes, values, ready):
     specs, scratch = pick_specs(PICK)
     sizes = (CAP - PART, PART)
     return pl.pallas_call(
         pick_kernel,
         grid=(DEVS // PICK,),
-        in_specs=specs + [pl.BlockSpec((MEM_DEV, HEADS * HEAD), lambda g: (0, 0))],
+        in_specs=specs
+        + [pl.BlockSpec((MEM_DEV, HEADS * HEAD), lambda g: (0, 0)), pl.BlockSpec(memory_space=pl.ANY)],
         out_specs=[pl.BlockSpec((PICK, size, HEAD), lambda g: (g, 0, 0)) for size in sizes],
         out_shape=[pltpu.HBM((DEVS, size, HEAD), jnp.bfloat16) for size in sizes],
         scratch_shapes=scratch,
         compiler_params=pltpu.CompilerParams(vmem_limit_bytes=40 * 1024 * 1024),
         cost_estimate=cost(40),
         name="pick",
-    )(codes, codes, values)
+    )(codes, codes, values, ready)
 
 
 def score_kernel(code_ref, start_ref, key_ref, query_ref, _, out_ref, __, wanted, found, hot):
@@ -259,17 +260,17 @@
     )(codes, codes, keys, queries, through)
 
 
-def join_kernel(a_ref, _, __, out_ref):
+def join_kernel(a_ref, _, out_ref):
     out_ref[...] = a_ref[...]
 
 
-def join(scores, *ready):
+def join(scores, ready):
     return pl.pallas_call(
         join_kernel,
-        in_specs=[pl.BlockSpec(memory_space=pltpu.VMEM)] + [pl.BlockSpec(memory_space=pl.ANY)] * len(ready),
+        in_specs=[pl.BlockSpec(memory_space=pltpu.VMEM)] + [pl.BlockSpec(memory_space=pl.ANY)],
         out_shape=jax.ShapeDtypeStruct(scores.shape, scores.dtype),
         name="join",
-    )(scores, *ready)
+    )(scores, ready)
 
 
 def weigh_kernel(place_ref, score_ref, out_ref, parts, near, total, slots, spread):
@@ -423,10 +424,10 @@
     local = jnp.where((here | earlier[None, :])[None], local, -jnp.inf)
     probs = jax.nn.softmax(local, axis=-1).astype(jnp.bfloat16)
     local_out = jnp.einsum("hqk,khd->hqd", probs, value_rows, preferred_element_type=jnp.float32)
-    picked, later = pick(codes, mem_values)
+    picked, later = pick(codes, mem_values, local_out)
     first = send(picked)
     scored, later = score(wanted, near_queries, line_keys, later)
-    scored = join(scored, first, local_out).reshape(planes, near, CAP)
+    scored = join(scored, first).reshape(planes, near, CAP)
     scores = lax.all_to_all(scored, "mem", split_axis=1, concat_axis=1, tiled=True).reshape(DEVS, CAP)
     last = send(later)
     weights = weigh(places, scores)

time: 339 us -> 398 us (1.17)
  waiting for transfers between devices: 43.3 us -> 87.4 us
  starting transfers between devices: 47.1 us -> 62.4 us
    all_gather x1, waiting for transfers between devices: 0.01 us -> 69 us  [shards(): lax.all_gather(turn(queries[0]), 'mem', axis=0, tiled=True)]
    all_to_all x1, waiting for transfers between devices: 23.1 us -> 2 us  [shards(): lax.all_to_all(wanted, 'seq', split_axis=0, concat_axis=0, tiled=True)]
    all_to_all x1, starting transfers between devices: 7.56 us -> 28.7 us  [shards(): lax.all_to_all(scored, 'mem', split_axis=1, concat_axis=1, tiled=True)]
    all_to_all x1, waiting for transfers between devices: 11.1 us -> 0.01 us  [shards(): first = send(picked)]
    all_to_all x1, waiting for transfers between devices: 0.01 us -> 7.3 us  [shards(): lax.all_to_all(asked.reshape(planes, near, CAP + 128), 'mem', split_axis=...]
    all_to_all x1, starting transfers between devices: 10.6 us -> 6.38 us  [shards(): first = send(picked)]
    unnamed x29 -> x35, local copies, waits for them, and re-layouts: 8.85 us -> 11.3 us
  transfers between devices with their start and end apart: 10 -> 10, of which waited for: 3 -> 4; matrix products, arithmetic and copies ran while one was open for 3% -> 3% of each run, Pallas kernels for 57% -> 49%
where the time goes in v5:
time: 398 us; the launch traced here: 396 us
  Pallas kernels  207 us (52%)
  waiting for transfers between devices  87.4 us (22%)
  starting transfers between devices  62.4 us (16%)
  local copies, waits for them, and re-layouts  15.7 us (4%)
  between operations  13.8 us (3%)
  matrix products  8.05 us (2%)
    pallas_call x1, Pallas kernels, score(): pl.pallas_call(score_kernel, grid=(DEVS // GROUP,), in_specs=specs + [pl....  72.5 us
    all_gather x1, waiting for transfers between devices, shards(): lax.all_gather(turn(queries[0]), 'mem', axis=0, tiled=True)  69 us
    pallas_call x1, Pallas kernels, pick(): pl.pallas_call(pick_kernel, grid=(DEVS // PICK,), in_specs=specs + [pl.Bl...  40.7 us
    pallas_call x2, Pallas kernels, mix(): pl.pallas_call(functools.partial(mix_kernel, begin=begin), grid=(DEVS //...  40.2 us
    all_to_all x1, starting transfers between devices, shards(): lax.all_to_all(scored, 'mem', split_axis=1, concat_axis=1, tiled=True)  28.7 us
    pallas_call x1, Pallas kernels, weigh(): pl.pallas_call(weigh_kernel, out_shape=jax.ShapeDtypeStruct((DEVS, CAP),...  28.7 us
    pallas_call x1, Pallas kernels, route(): pl.pallas_call(route_kernel, out_shape=[jax.ShapeDtypeStruct((DEVS, CAP +...  22.1 us
    unnamed x35, local copies, waits for them, and re-layouts  11.3 us
  transfers between devices with their start and end apart: 10, of which 4 were waited for; matrix products, arithmetic and copies ran while one was open for 3% of the time, Pallas kernels for 49%

profile of v5, /device:TPU:1, one launch (start us, length us, event | category | flops | bytes accessed | tf_op | source)
XLA Modules:
  0.0 396.2 jit_solution(1682737458143180684)
XLA Ops:
  10.4 6.5 %collective-permute-start.2 = (bf16[128,2048]{0,1:T(8,128)(2,1)S(1)}, bf16[128,2048]{0,1:T(8,128)(2,1)S(1)}, u32[]{:S(2)}, u32[]{:S(2)}) collective-permute-start(bf16[128,2048]{0,1:T(8,128)(2,1)S(1)} %pad_maximum_fusion.1), channel_id=1, source_target_pairs={{0,96},{1,97},{2,98},{3,99},{4,100},{5,101},{6,102},{7,103},{8,104... | collective-permute-start | bytes 1572872 | tf_op jit(solution)/shard_map/ppermute | solution.py:404
  18.3 2.5 collective-permute-start
  21.2 22.1 %route.1 = (s32[128,512]{1,0:T(8,128)S(1)}, s32[128,256]{1,0:T(8,128)S(1)}) custom-call(s32[128,256]{1,0:T(8,128)S(1)} %reshape.119.look_ref, s32[8,128]{1,0:T(8,128)S(1)} %bitcast.39), custom_call_target="tpu_custom_call" | custom-call | flops 22000001024 | bytes 22000000 | tf_op jit(solution)/shard_map/route/pallas_call | solution.py:104
  44.9 8.3 %all-to-all-start = ((s32[4,32,512]{2,0,1:T(4,128)}), s32[4,32,512]{2,0,1:T(4,128)S(1)}, u32[]{:S(2)}, u32[]{:S(2)}) async-start(s32[4,32,512]{2,0,1:T(4,128)} %copy.39), calls=%async_computation | async-start | bytes 524288 | tf_op jit(solution)/shard_map/all_to_all | solution.py:409
  54.9 7.3 %all-to-all-done = s32[4,32,512]{2,0,1:T(4,128)S(1)} async-done(((s32[4,32,512]{2,0,1:T(4,128)}), s32[4,32,512]{2,0,1:T(4,128)S(1)}, u32[]{:S(2)}, u32[]{:S(2)}) %all-to-all-start) | async-done | bytes 262176 | tf_op jit(solution)/shard_map/all_to_all | solution.py:409
  63.0 3.6 all-to-all-start.1
  67.8 2.2 fusion.32
  70.0 2.1 fusion.5
  72.4 2.0 all-to-all-done.1
  74.4 40.7 %pick.1 = (bf16[128,256,128]{2,1,0:T(8,128)(2,1)}, bf16[128,128,128]{2,1,0:T(8,128)(2,1)}) custom-call(s32[128,512]{1,0:T(8,128)S(1)} %bitcast.36, s32[128,512]{1,0:T(8,128)S(1)} %bitcast.37, bf16[512,1024]{1,0:T(8,128)(2,1)S(1)} %copy-done.6, f32[8,128,128]{2,1,0:T(8,128)S(1)} %copy.47._), custom_call_target="tpu_custom_call" | custom-call | flops 40000000000 | bytes 40000000 | tf_op jit(solution)/shard_map/pick/pallas_call | solution.py:214
  115.1 6.4 %all-to-all-start.2 = ((bf16[128,256,128]{2,1,0:T(8,128)(2,1)}), bf16[128,256,128]{2,1,0:T(8,128)(2,1)}, u32[]{:S(2)}, u32[]{:S(2)}) async-start(bf16[128,256,128]{2,1,0:T(8,128)(2,1)} %get-tuple-element.15), calls=%async_computation.2 | async-start | bytes 16777216 | tf_op jit(solution)/shard_map/all_to_all | solution.py:428
  121.5 69.0 %all-gather.5.cloned.1.call-done = bf16[32768,128]{1,0:T(8,128)(2,1)} async-done(((bf16[1024,128]{1,0:T(8,128)(2,1)}), bf16[32768,128]{1,0:T(8,128)(2,1)}) %all-gather.5.cloned.1.call-update) | async-done | bytes 8388624 | tf_op jit(solution)/shard_map/all_gather | solution.py:400
  190.5 2.2 copy-done
  192.7 2.2 copy-done.5
  194.9 72.5 %score.1 = (f32[128,384]{1,0:T(8,128)S(1)}, bf16[128,128,128]{2,1,0:T(8,128)(2,1)S(1)}) custom-call(s32[128,512]{1,0:T(8,128)} %bitcast.4.code_ref.start_ref, s32[128,512]{1,0:T(8,128)} %bitcast.4.code_ref.start_ref, bf16[2048,1024]{1,0:T(8,128)(2,1)S(1)} %copy-done.5, bf16[32,1024,128]{2,1,0:T(8,128)(2,1)} %bitcast.53, ...), custom_call_target="tpu_custom_call", output_to_operand_aliasing={{1}: (4, {})} | custom-call | flops 74999996416 | bytes 75000000 | tf_op jit(solution)/shard_map/score/pallas_call | solution.py:241
  267.4 2.0 copy-done.1
  271.7 1.7 copy.48
  273.4 28.7 %all-to-all-start.3 = ((f32[4,32,384]{2,0,1:T(4,128)}), f32[4,32,384]{2,0,1:T(4,128)S(1)}, u32[]{:S(2)}, u32[]{:S(2)}) async-start(f32[4,32,384]{2,0,1:T(4,128)} %copy.48), calls=%async_computation.3 | async-start | bytes 393216 | tf_op jit(solution)/shard_map/all_to_all | solution.py:431
  302.1 8.3 %all-to-all-done.3 = f32[4,32,384]{2,0,1:T(4,128)S(1)} async-done(((f32[4,32,384]{2,0,1:T(4,128)}), f32[4,32,384]{2,0,1:T(4,128)S(1)}, u32[]{:S(2)}, u32[]{:S(2)}) %all-to-all-start.3) | async-done | bytes 196640 | tf_op jit(solution)/shard_map/all_to_all | solution.py:431
  310.4 5.1 %all-to-all-start.4 = ((bf16[128,128,128]{2,1,0:T(8,128)(2,1)}), bf16[128,128,128]{2,1,0:T(8,128)(2,1)}, u32[]{:S(2)}, u32[]{:S(2)}) async-start(bf16[128,128,128]{2,1,0:T(8,128)(2,1)} %copy-done.1), calls=%async_computation.4 | async-start | bytes 8388608 | tf_op jit(solution)/shard_map/all_to_all | solution.py:432
  315.6 28.7 %weigh.1.weight_ref = f32[128,384]{1,0:T(8,128)S(1)} custom-call(s32[128,256]{1,0:T(8,128)S(1)} %get-tuple-element.12.place_ref, f32[128,384]{1,0:T(8,128)S(1)} %bitcast.38), custom_call_target="tpu_custom_call" | custom-call | flops 22000001024 | bytes 22000000 | tf_op jit(solution)/shard_map/weigh/pallas_call | solution.py:331
  344.3 26.6 %mix.2 = f32[512,256]{1,0:T(8,128)S(1)} custom-call(s32[128,512]{1,0:T(8,128)S(1)} %copy-done.3, s32[128,512]{1,0:T(8,128)S(1)} %copy-done.3, f32[128,384]{1,0:T(8,128)S(1)} %weigh.1.weight_ref, bf16[128,256,128]{2,1,0:T(8,128)(2,1)} %all-to-all-done.2._.value_ref), custom_call_target="tpu_custom_call" | custom-call | flops 24000000000 | bytes 24000000 | tf_op jit(solution)/shard_map/mix/pallas_call | solution.py:373
  370.9 13.5 %mix.3 = f32[512,256]{1,0:T(8,128)S(1)} custom-call(s32[128,512]{1,0:T(8,128)S(1)} %copy-done.3, s32[128,512]{1,0:T(8,128)S(1)} %copy-done.3, f32[128,384]{1,0:T(8,128)S(1)} %weigh.1.weight_ref, bf16[128,128,128]{2,1,0:T(8,128)(2,1)} %all-to-all-done.4.value_ref), custom_call_target="tpu_custom_call" | custom-call | flops 12000000000 | bytes 12000000 | tf_op jit(solution)/shard_map/mix/pallas_call | solution.py:373
  385.7 3.7 fusion.1
  (63 shorter events, 14.5 us)
Async XLA Ops:
  6.5 3.6 copy-start.11
  6.5 14.2 %copy-start.13 = (s32[1,128,8,32]{1,3,2,0:T(8,128)S(1)}, s32[1,128,8,32]{1,3,2,0:T(8,128)}, u32[]{:S(2)}) copy-start(s32[1,128,8,32]{1,3,2,0:T(8,128)} %param.14) | copy-start | bytes 393220
  6.5 115.0 %all-gather.3.cloned.1.call-start = ((), (), s32[]{:S(2)}) async-start(), calls=%async_computation.5 | async-start | bytes 5242880 | tf_op jit(solution)/shard_map/all_gather | solution.py:401
  7.3 183.2 %all-gather.5.cloned.1.call-start = ((), (), s32[]{:S(2)}) async-start(), calls=%async_computation.6 | async-start | bytes 8650752 | tf_op jit(solution)/shard_map/all_gather | solution.py:400
  7.3 13.9 %copy-start.7 = (s32[1024]{0:T(1024)S(1)}, s32[1024]{0:T(1024)}, u32[]{:S(2)}) copy-start(s32[1024]{0:T(1024)} %param.15) | copy-start | bytes 12292
  10.4 56.2 %collective-permute-start.2 = (bf16[128,2048]{0,1:T(8,128)(2,1)S(1)}, bf16[128,2048]{0,1:T(8,128)(2,1)S(1)}, u32[]{:S(2)}, u32[]{:S(2)}) collective-permute-start(bf16[128,2048]{0,1:T(8,128)(2,1)S(1)} %pad_maximum_fusion.1), channel_id=1, source_target_pairs={{0,96},{1,97},{2,98},{3,99},{4,100},{5,101},{6,102},{7,103},{8,104... | collective-permute-start | bytes 1572872 | tf_op jit(solution)/shard_map/ppermute | solution.py:404
  16.9 49.7 %collective-permute-start.1 = (bf16[128,2048]{0,1:T(8,128)(2,1)S(1)}, bf16[128,2048]{0,1:T(8,128)(2,1)S(1)}, u32[]{:S(2)}, u32[]{:S(2)}) collective-permute-start(bf16[128,2048]{0,1:T(8,128)(2,1)S(1)} %pad_maximum_fusion.1), channel_id=1, source_target_pairs={{0,64},{32,96},{1,65},{33,97},{2,66},{34,98},{3,67},{35,99},{4,68}... | collective-permute-start | bytes 1572872 | tf_op jit(solution)/shard_map/ppermute | solution.py:404
  18.3 48.3 %collective-permute-start = (bf16[128,2048]{0,1:T(8,128)(2,1)S(1)}, bf16[128,2048]{0,1:T(8,128)(2,1)S(1)}, u32[]{:S(2)}, u32[]{:S(2)}) collective-permute-start(bf16[128,2048]{0,1:T(8,128)(2,1)S(1)} %pad_maximum_fusion.1), channel_id=1, source_target_pairs={{0,32},{32,64},{64,96},{1,33},{33,65},{65,97},{2,34},{34,66},{66,9... | collective-permute-start | bytes 1572872 | tf_op jit(solution)/shard_map/ppermute | solution.py:404
  21.2 32.1 %copy-start.10 = (bf16[1,128,1024]{2,1,0:T(8,128)(2,1)S(1)}, bf16[1,128,1024]{2,1,0:T(8,128)(2,1)}, u32[]{:S(2)}) copy-start(bf16[1,128,1024]{2,1,0:T(8,128)(2,1)} %param.9) | copy-start | bytes 786436
  44.9 17.3 %all-to-all-start = ((s32[4,32,512]{2,0,1:T(4,128)}), s32[4,32,512]{2,0,1:T(4,128)S(1)}, u32[]{:S(2)}, u32[]{:S(2)}) async-start(s32[4,32,512]{2,0,1:T(4,128)} %copy.39), calls=%async_computation | async-start | bytes 524288 | tf_op jit(solution)/shard_map/all_to_all | solution.py:409
  63.0 11.4 %all-to-all-start.1 = ((s32[4,32,512]{2,1,0:T(8,128)}), s32[4,32,512]{2,1,0:T(8,128)S(1)}, u32[]{:S(2)}, u32[]{:S(2)}) async-start(s32[4,32,512]{2,1,0:T(8,128)} %copy.40), calls=%async_computation.1 | async-start | bytes 524288 | tf_op jit(solution)/shard_map/all_to_all | solution.py:412
  66.8 1.0 copy-start.12
  66.9 0.9 copy-start.14
  70.0 4.3 %copy-start.6 = (bf16[512,1024]{1,0:T(8,128)(2,1)S(1)}, bf16[512,1024]{1,0:T(8,128)(2,1)}, u32[]{:S(2)}) copy-start(bf16[512,1024]{1,0:T(8,128)(2,1)} %value_ref.1) | copy-start | bytes 3145732
  72.1 43.0 %copy-start.8 = (f32[8,128,128]{1,2,0:T(8,128)}, f32[8,128,128]{1,2,0:T(8,128)S(1)}, u32[]{:S(2)}) copy-start(f32[8,128,128]{1,2,0:T(8,128)S(1)} %fusion.5) | copy-start | bytes 1572868
  115.1 154.9 %all-to-all-start.2 = ((bf16[128,256,128]{2,1,0:T(8,128)(2,1)}), bf16[128,256,128]{2,1,0:T(8,128)(2,1)}, u32[]{:S(2)}, u32[]{:S(2)}) async-start(bf16[128,256,128]{2,1,0:T(8,128)(2,1)} %get-tuple-element.15), calls=%async_computation.2 | async-start | bytes 16777216 | tf_op jit(solution)/shard_map/all_to_all | solution.py:428
  190.5 2.2 copy-start
  192.7 2.2 copy-start.5
  267.3 2.0 copy-start.1
  270.0 32.1 %copy-start.15 = (f32[8]{0:T(128)S(1)}, f32[8]{0:T(128)}, u32[]{:S(2)}) copy-start(f32[8]{0:T(128)} %param.16) | copy-start | bytes 100
  273.4 37.0 %all-to-all-start.3 = ((f32[4,32,384]{2,0,1:T(4,128)}), f32[4,32,384]{2,0,1:T(4,128)S(1)}, u32[]{:S(2)}, u32[]{:S(2)}) async-start(f32[4,32,384]{2,0,1:T(4,128)} %copy.48), calls=%async_computation.3 | async-start | bytes 393216 | tf_op jit(solution)/shard_map/all_to_all | solution.py:431
  310.4 60.5 %all-to-all-start.4 = ((bf16[128,128,128]{2,1,0:T(8,128)(2,1)}), bf16[128,128,128]{2,1,0:T(8,128)(2,1)}, u32[]{:S(2)}, u32[]{:S(2)}) async-start(bf16[128,128,128]{2,1,0:T(8,128)(2,1)} %copy-done.1), calls=%async_computation.4 | async-start | bytes 8388608 | tf_op jit(solution)/shard_map/all_to_all | solution.py:432
  315.6 28.7 %copy-start.3 = (s32[128,512]{1,0:T(8,128)S(1)}, s32[128,512]{1,0:T(8,128)}, u32[]{:S(2)}) copy-start(s32[128,512]{1,0:T(8,128)} %copy-done.2) | copy-start | bytes 786436
  384.5 1.0 copy-start.9
  (2 other events, 1.4 us)
Sparse Core Ops, SparseCore 0:
  9.0 68.7 all-gather.2
  80.1 110.3 all-gather.4

commit v6 on v4

--- a/solution.py
+++ b/solution.py
@@ -201,27 +201,28 @@
     return specs, scratch
 
 
-def pick_kernel(code_ref, start_ref, value_ref, first_ref, last_ref, wanted, found, hot):
+def pick_kernel(code_ref, start_ref, value_ref, _, first_ref, last_ref, wanted, found, hot):
     pick_rows(code_ref, start_ref, value_ref, wanted, found, hot)
     for i in range(code_ref.shape[0]):
         first_ref[i] = found[i, : CAP - PART, :].astype(jnp.bfloat16)
         last_ref[i] = found[i, CAP - PART : CAP, :].astype(jnp.bfloat16)
 
 
-def pick(codes, values):
+def pick(codes, values, ready):
     specs, scratch = pick_specs(PICK)
     sizes = (CAP - PART, PART)
     return pl.pallas_call(
         pick_kernel,
         grid=(DEVS // PICK,),
-        in_specs=specs + [pl.BlockSpec((MEM_DEV, HEADS * HEAD), lambda g: (0, 0))],
+        in_specs=specs
+        + [pl.BlockSpec((MEM_DEV, HEADS * HEAD), lambda g: (0, 0)), pl.BlockSpec(memory_space=pl.ANY)],
         out_specs=[pl.BlockSpec((PICK, size, HEAD), lambda g: (g, 0, 0)) for size in sizes],
         out_shape=[pltpu.HBM((DEVS, size, HEAD), jnp.bfloat16) for size in sizes],
         scratch_shapes=scratch,
         compiler_params=pltpu.CompilerParams(vmem_limit_bytes=40 * 1024 * 1024),
         cost_estimate=cost(40),
         name="pick",
-    )(codes, codes, values)
+    )(codes, codes, values, ready)
 
 
 def score_kernel(code_ref, start_ref, key_ref, query_ref, _, out_ref, __, wanted, found, hot):
@@ -397,7 +398,18 @@
     planes = lax.axis_size("seq")
     near = lax.axis_size("mem")
     near_queries = lax.all_gather(turn(queries[0]), "mem", axis=0, tiled=True).reshape(near, HEADS * TOK, HEAD)
-    line_keys = lax.all_gather(mem_keys, "seq", axis=0, tiled=True)
+    up = [(i, (i + 1) % planes) for i in range(planes)]
+    down = [(i, (i - 1) % planes) for i in range(planes)]
+    middle = mem_keys.shape[0] // 2
+    below = lax.ppermute(mem_keys, "seq", up)
+    above = lax.ppermute(mem_keys, "seq", down)
+    far = jnp.concatenate(
+        [lax.ppermute(below[:middle], "seq", up), lax.ppermute(above[middle:], "seq", down)], axis=0
+    )
+    place = lax.axis_index("seq")
+    line_keys = jnp.zeros((planes * MEM_DEV, HEADS * HEAD), mem_keys.dtype)
+    for back, rows in enumerate((mem_keys, below, far, above)):
+        line_keys = lax.dynamic_update_slice_in_dim(line_keys, rows, (place - back) % planes * MEM_DEV, axis=0)
     own = jnp.concatenate([keys[0], values[0]], axis=1)
     blocks = [own] + [
         lax.ppermute(own, "seq", [(i, i + back) for i in range(planes - back)]) for back in range(1, planes)
@@ -423,7 +435,7 @@
     local = jnp.where((here | earlier[None, :])[None], local, -jnp.inf)
     probs = jax.nn.softmax(local, axis=-1).astype(jnp.bfloat16)
     local_out = jnp.einsum("hqk,khd->hqd", probs, value_rows, preferred_element_type=jnp.float32)
-    picked, later = pick(codes, mem_values)
+    picked, later = pick(codes, mem_values, line_keys)
     first = send(picked)
     scored, later = score(wanted, near_queries, line_keys, later)
     scored = join(scored, first, local_out).reshape(planes, near, CAP)

time: 339 us -> 341 us (level)
  waiting for transfers between devices: 43.3 us -> 24.7 us
  starting transfers between devices: 47.1 us -> 55.8 us
  local copies, waits for them, and re-layouts: 14.9 us -> 23 us
    all_to_all x1, waiting for transfers between devices: 23.1 us -> 0.01 us  [shards(): lax.all_to_all(wanted, 'seq', split_axis=0, concat_axis=0, tiled=True)]
    ppermute x0 -> x4, starting transfers between devices: none -> 7.41 us  [the longest x1 2.67 us: shards(): lax.ppermute(above[middle:], 'seq', down)]
    unnamed x29 -> x35, local copies, waits for them, and re-layouts: 8.85 us -> 8.66 us
  transfers between devices with their start and end apart: 10 -> 13, of which waited for: 3 -> 3; matrix products, arithmetic and copies ran while one was open for 3% -> 7% of each run, Pallas kernels for 57% -> 56%
where the time goes in v6:
time: 341 us; the launch traced here: 339 us
  Pallas kernels  208 us (61%)
  starting transfers between devices  55.8 us (16%)
  waiting for transfers between devices  24.7 us (7%)
  local copies, waits for them, and re-layouts  23 us (7%)
  between operations  13.8 us (4%)
  matrix products  7.91 us (2%)
  other arithmetic  5.91 us (2%)
    pallas_call x1, Pallas kernels, score(): pl.pallas_call(score_kernel, grid=(DEVS // GROUP,), in_specs=specs + [pl....  73 us
    pallas_call x1, Pallas kernels, pick(): pl.pallas_call(pick_kernel, grid=(DEVS // PICK,), in_specs=specs + [pl.Bl...  40.7 us
    pallas_call x2, Pallas kernels, mix(): pl.pallas_call(functools.partial(mix_kernel, begin=begin), grid=(DEVS //...  40.2 us
    pallas_call x1, Pallas kernels, weigh(): pl.pallas_call(weigh_kernel, out_shape=jax.ShapeDtypeStruct((DEVS, CAP),...  28.7 us
    pallas_call x1, Pallas kernels, route(): pl.pallas_call(route_kernel, out_shape=[jax.ShapeDtypeStruct((DEVS, CAP +...  22.1 us
    all_to_all x1, starting transfers between devices, shards(): first = send(picked)  13.4 us
    all_to_all x1, waiting for transfers between devices, shards(): first = send(picked)  13.3 us
    ppermute x3, starting transfers between devices, shards(): lax.ppermute(own, 'seq', [(i, i + back) for i in range(planes - back)])  9.31 us
  transfers between devices with their start and end apart: 13, of which 3 were waited for; matrix products, arithmetic and copies ran while one was open for 7% of the time, Pallas kernels for 56%

profile of v6, /device:TPU:1, one launch (start us, length us, event | category | flops | bytes accessed | tf_op | source)
XLA Modules:
  0.0 339.2 jit_solution(11862952232116031142)
XLA Ops:
  8.3 2.5 collective-permute-start
  10.8 2.2 collective-permute-start.2
  16.3 2.1 collective-permute-start.4
  18.4 5.1 %collective-permute-start.5 = (bf16[128,2048]{0,1:T(8,128)(2,1)}, bf16[128,2048]{0,1:T(8,128)(2,1)}, u32[]{:S(2)}, u32[]{:S(2)}) collective-permute-start(bf16[128,2048]{0,1:T(8,128)(2,1)} %pad_maximum_fusion.1), channel_id=1, source_target_pairs={{0,64},{32,96},{1,65},{33,97},{2,66},{34,98},{3,67},{35,99},{4,68}... | collective-permute-start | bytes 1572872 | tf_op jit(solution)/shard_map/ppermute | solution.py:415
  26.9 22.1 %route.1 = (s32[128,512]{1,0:T(8,128)S(1)}, s32[128,256]{1,0:T(8,128)S(1)}) custom-call(s32[128,256]{1,0:T(8,128)S(1)} %reshape.119.look_ref, s32[8,128]{1,0:T(8,128)S(1)} %bitcast.39), custom_call_target="tpu_custom_call" | custom-call | flops 22000001024 | bytes 22000000 | tf_op jit(solution)/shard_map/route/pallas_call | solution.py:104
  50.6 8.9 %all-to-all-start = ((s32[4,32,512]{2,0,1:T(4,128)}), s32[4,32,512]{2,0,1:T(4,128)}, u32[]{:S(2)}, u32[]{:S(2)}) async-start(s32[4,32,512]{2,0,1:T(4,128)} %copy.39), calls=%async_computation | async-start | bytes 524288 | tf_op jit(solution)/shard_map/all_to_all | solution.py:420
  59.6 2.5 broadcast_in_dim.16
  64.8 2.7 collective-permute-start.3
  70.9 3.6 %all-to-all-start.1 = ((s32[4,32,512]{2,1,0:T(8,128)}), s32[4,32,512]{2,1,0:T(8,128)S(1)}, u32[]{:S(2)}, u32[]{:S(2)}) async-start(s32[4,32,512]{2,1,0:T(8,128)} %copy.40), calls=%async_computation.1 | async-start | bytes 524288 | tf_op jit(solution)/shard_map/all_to_all | solution.py:423
  75.6 3.0 collective-permute-done.1
  78.7 2.3 maximum_dynamic-update-slice_fusion
  82.0 40.7 %pick.1 = (bf16[128,256,128]{2,1,0:T(8,128)(2,1)}, bf16[128,128,128]{2,1,0:T(8,128)(2,1)}) custom-call(s32[128,512]{1,0:T(8,128)S(1)} %bitcast.36, s32[128,512]{1,0:T(8,128)S(1)} %bitcast.37, bf16[512,1024]{1,0:T(8,128)(2,1)S(1)} %copy-done.5, bf16[2048,1024]{1,0:T(8,128)(2,1)} %constant_dynamic-update-slice_fusion._.key_ref), custom_call_target="tpu_custom_call" | custom-call | flops 40000000000 | bytes 40000000 | tf_op jit(solution)/shard_map/pick/pallas_call | solution.py:214
  122.7 13.4 %all-to-all-start.2 = ((bf16[128,256,128]{2,1,0:T(8,128)(2,1)}), bf16[128,256,128]{2,1,0:T(8,128)(2,1)}, u32[]{:S(2)}, u32[]{:S(2)}) async-start(bf16[128,256,128]{2,1,0:T(8,128)(2,1)} %get-tuple-element.15), calls=%async_computation.2 | async-start | bytes 16777216 | tf_op jit(solution)/shard_map/all_to_all | solution.py:439
  138.0 2.2 fusion.32
  143.2 2.2 copy-done
  145.4 73.0 %score.1 = (f32[128,384]{1,0:T(8,128)S(1)}, bf16[128,128,128]{2,1,0:T(8,128)(2,1)S(1)}) custom-call(s32[128,512]{1,0:T(8,128)} %bitcast.4.code_ref.start_ref, s32[128,512]{1,0:T(8,128)} %bitcast.4.code_ref.start_ref, bf16[2048,1024]{1,0:T(8,128)(2,1)} %constant_dynamic-update-slice_fusion._.key_ref, ...), custom_call_target="tpu_custom_call", output_to_operand_aliasing={{1}: (4, {})} | custom-call | flops 74999996416 | bytes 75000000 | tf_op jit(solution)/shard_map/score/pallas_call | solution.py:241
  221.0 13.3 %all-to-all-done.2._.value_ref = bf16[128,256,128]{2,1,0:T(8,128)(2,1)} async-done(((bf16[128,256,128]{2,1,0:T(8,128)(2,1)}), bf16[128,256,128]{2,1,0:T(8,128)(2,1)}, u32[]{:S(2)}, u32[]{:S(2)}) %all-to-all-start.2) | async-done | bytes 8388640 | tf_op jit(solution)/shard_map/all_to_all | solution.py:439
  237.7 7.6 %all-to-all-start.3 = ((f32[4,32,384]{2,0,1:T(4,128)}), f32[4,32,384]{2,0,1:T(4,128)S(1)}, u32[]{:S(2)}, u32[]{:S(2)}) async-start(f32[4,32,384]{2,0,1:T(4,128)} %copy.48), calls=%async_computation.3 | async-start | bytes 393216 | tf_op jit(solution)/shard_map/all_to_all | solution.py:442
  245.3 8.3 %all-to-all-done.3 = f32[4,32,384]{2,0,1:T(4,128)S(1)} async-done(((f32[4,32,384]{2,0,1:T(4,128)}), f32[4,32,384]{2,0,1:T(4,128)S(1)}, u32[]{:S(2)}, u32[]{:S(2)}) %all-to-all-start.3) | async-done | bytes 196640 | tf_op jit(solution)/shard_map/all_to_all | solution.py:442
  253.6 5.6 %all-to-all-start.4 = ((bf16[128,128,128]{2,1,0:T(8,128)(2,1)}), bf16[128,128,128]{2,1,0:T(8,128)(2,1)}, u32[]{:S(2)}, u32[]{:S(2)}) async-start(bf16[128,128,128]{2,1,0:T(8,128)(2,1)} %copy-done.1), calls=%async_computation.4 | async-start | bytes 8388608 | tf_op jit(solution)/shard_map/all_to_all | solution.py:443
  259.2 28.7 %weigh.1.weight_ref = f32[128,384]{1,0:T(8,128)S(1)} custom-call(s32[128,256]{1,0:T(8,128)S(1)} %get-tuple-element.12.place_ref, f32[128,384]{1,0:T(8,128)S(1)} %bitcast.38), custom_call_target="tpu_custom_call" | custom-call | flops 22000001024 | bytes 22000000 | tf_op jit(solution)/shard_map/weigh/pallas_call | solution.py:331
  287.9 26.6 %mix.2 = f32[512,256]{1,0:T(8,128)S(1)} custom-call(s32[128,512]{1,0:T(8,128)S(1)} %copy-done.3, s32[128,512]{1,0:T(8,128)S(1)} %copy-done.3, f32[128,384]{1,0:T(8,128)S(1)} %weigh.1.weight_ref, bf16[128,256,128]{2,1,0:T(8,128)(2,1)} %all-to-all-done.2._.value_ref), custom_call_target="tpu_custom_call" | custom-call | flops 24000000000 | bytes 24000000 | tf_op jit(solution)/shard_map/mix/pallas_call | solution.py:373
  314.5 13.5 %mix.3 = f32[512,256]{1,0:T(8,128)S(1)} custom-call(s32[128,512]{1,0:T(8,128)S(1)} %copy-done.3, s32[128,512]{1,0:T(8,128)S(1)} %copy-done.3, f32[128,384]{1,0:T(8,128)S(1)} %weigh.1.weight_ref, bf16[128,128,128]{2,1,0:T(8,128)(2,1)} %all-to-all-done.4.value_ref), custom_call_target="tpu_custom_call" | custom-call | flops 12000000000 | bytes 12000000 | tf_op jit(solution)/shard_map/mix/pallas_call | solution.py:373
  328.6 3.7 %fusion.1 = bf16[1,128,2048]{2,1,0:T(8,128)(2,1)} fusion(bf16[128,1024]{0,1:T(8,128)(2,1)S(1)} %bitcast.47, bf16[1024,2048]{1,0:T(8,128)(2,1)} %param.17), kind=kOutput, calls=%fused_computation.2 | convolution fusion | flops 537133056 | bytes 4980736 | tf_op jit(solution)/shard_map/dot_general | solution.py:451
  (75 shorter events, 29.5 us)
Async XLA Ops:
  6.5 20.3 %copy-start.6 = (s32[1024]{0:T(1024)S(1)}, s32[1024]{0:T(1024)}, u32[]{:S(2)}) copy-start(s32[1024]{0:T(1024)} %param.15) | copy-start | bytes 12292
  6.5 136.6 %all-gather.2.cloned.1.call-start = ((), (), s32[]{:S(2)}) async-start(), calls=%async_computation.5 | async-start | bytes 8650752 | tf_op jit(solution)/shard_map/all_gather | solution.py:400
  8.3 54.8 %collective-permute-start = (bf16[512,1024]{1,0:T(8,128)(2,1)}, bf16[512,1024]{1,0:T(8,128)(2,1)S(1)}, u32[]{:S(2)}, u32[]{:S(2)}) collective-permute-start(bf16[512,1024]{1,0:T(8,128)(2,1)} %param.12), channel_id=1, source_target_pairs={{0,32},{32,64},{64,96},{96,0},{1,33},{33,65},{65,97},{97,1},{2,34}... | collective-permute-start | bytes 3145736 | tf_op jit(solution)/shard_map/ppermute | solution.py:404
  10.8 53.1 %collective-permute-start.2 = (bf16[512,1024]{1,0:T(8,128)(2,1)}, bf16[512,1024]{1,0:T(8,128)(2,1)S(1)}, u32[]{:S(2)}, u32[]{:S(2)}) collective-permute-start(bf16[512,1024]{1,0:T(8,128)(2,1)} %param.12), channel_id=1, source_target_pairs={{0,96},{32,0},{64,32},{96,64},{1,97},{33,1},{65,33},{97,65},{2,98}... | collective-permute-start | bytes 3145736 | tf_op jit(solution)/shard_map/ppermute | solution.py:405
  14.1 11.4 %copy-start.7 = (bf16[1,128,1024]{1,2,0:T(8,128)(2,1)}, bf16[1,128,1024]{1,2,0:T(8,128)(2,1)S(1)}, u32[]{:S(2)}) copy-start(bf16[1,128,1024]{1,2,0:T(8,128)(2,1)S(1)} %copy.42) | copy-start | bytes 786436
  15.4 33.6 %copy-start.9 = (bf16[1,128,1024]{1,2,0:T(8,128)(2,1)}, bf16[1,128,1024]{1,2,0:T(8,128)(2,1)S(1)}, u32[]{:S(2)}) copy-start(bf16[1,128,1024]{1,2,0:T(8,128)(2,1)S(1)} %copy.43) | copy-start | bytes 786436
  16.3 119.9 %collective-permute-start.4 = (bf16[128,2048]{0,1:T(8,128)(2,1)}, bf16[128,2048]{0,1:T(8,128)(2,1)}, u32[]{:S(2)}, u32[]{:S(2)}) collective-permute-start(bf16[128,2048]{0,1:T(8,128)(2,1)} %pad_maximum_fusion.1), channel_id=1, source_target_pairs={{0,32},{32,64},{64,96},{1,33},{33,65},{65,97},{2,34},{34,66},{66,9... | collective-permute-start | bytes 1572872 | tf_op jit(solution)/shard_map/ppermute | solution.py:415
  18.4 117.8 %collective-permute-start.5 = (bf16[128,2048]{0,1:T(8,128)(2,1)}, bf16[128,2048]{0,1:T(8,128)(2,1)}, u32[]{:S(2)}, u32[]{:S(2)}) collective-permute-start(bf16[128,2048]{0,1:T(8,128)(2,1)} %pad_maximum_fusion.1), channel_id=1, source_target_pairs={{0,64},{32,96},{1,65},{33,97},{2,66},{34,98},{3,67},{35,99},{4,68}... | collective-permute-start | bytes 1572872 | tf_op jit(solution)/shard_map/ppermute | solution.py:415
  23.5 112.7 %collective-permute-start.6 = (bf16[128,2048]{0,1:T(8,128)(2,1)}, bf16[128,2048]{0,1:T(8,128)(2,1)}, u32[]{:S(2)}, u32[]{:S(2)}) collective-permute-start(bf16[128,2048]{0,1:T(8,128)(2,1)} %pad_maximum_fusion.1), channel_id=1, source_target_pairs={{0,96},{1,97},{2,98},{3,99},{4,100},{5,101},{6,102},{7,103},{8,104... | collective-permute-start | bytes 1572872 | tf_op jit(solution)/shard_map/ppermute | solution.py:415
  49.0 13.1 %copy-start.11 = (bf16[512,1024]{1,0:T(8,128)(2,1)S(1)}, bf16[512,1024]{1,0:T(8,128)(2,1)}, u32[]{:S(2)}) copy-start(bf16[512,1024]{1,0:T(8,128)(2,1)} %param.12) | copy-start | bytes 3145732
  50.6 18.6 %all-to-all-start = ((s32[4,32,512]{2,0,1:T(4,128)}), s32[4,32,512]{2,0,1:T(4,128)}, u32[]{:S(2)}, u32[]{:S(2)}) async-start(s32[4,32,512]{2,0,1:T(4,128)} %copy.39), calls=%async_computation | async-start | bytes 524288 | tf_op jit(solution)/shard_map/all_to_all | solution.py:420
  59.6 8.0 %copy-start.12 = (bf16[1,128,1024]{2,1,0:T(8,128)(2,1)S(1)}, bf16[1,128,1024]{2,1,0:T(8,128)(2,1)}, u32[]{:S(2)}) copy-start(bf16[1,128,1024]{2,1,0:T(8,128)(2,1)} %param.9) | copy-start | bytes 786436
  63.9 14.7 %collective-permute-start.1 = (bf16[256,1024]{1,0:T(8,128)(2,1)}, bf16[256,1024]{1,0:T(8,128)(2,1)}, u32[]{:S(2)}, u32[]{:S(2)}) collective-permute-start(bf16[256,1024]{1,0:T(8,128)(2,1)} %slice.24), channel_id=1, source_target_pairs={{0,32},{32,64},{64,96},{96,0},{1,33},{33,65},{65,97},{97,1},{2,34}... | collective-permute-start | bytes 1572872 | tf_op jit(solution)/shard_map/ppermute | solution.py:407
  64.8 17.2 %copy-start.5 = (bf16[512,1024]{1,0:T(8,128)(2,1)S(1)}, bf16[512,1024]{1,0:T(8,128)(2,1)}, u32[]{:S(2)}) copy-start(bf16[512,1024]{1,0:T(8,128)(2,1)} %value_ref.1) | copy-start | bytes 3145732
  64.8 13.9 %collective-permute-start.3 = (bf16[256,1024]{1,0:T(8,128)(2,1)}, bf16[256,1024]{1,0:T(8,128)(2,1)}, u32[]{:S(2)}, u32[]{:S(2)}) collective-permute-start(bf16[256,1024]{1,0:T(8,128)(2,1)} %slice.25), channel_id=1, source_target_pairs={{0,96},{32,0},{64,32},{96,64},{1,97},{33,1},{65,33},{97,65},{2,98}... | collective-permute-start | bytes 1572872 | tf_op jit(solution)/shard_map/ppermute | solution.py:407
  70.9 11.0 %all-to-all-start.1 = ((s32[4,32,512]{2,1,0:T(8,128)}), s32[4,32,512]{2,1,0:T(8,128)S(1)}, u32[]{:S(2)}, u32[]{:S(2)}) async-start(s32[4,32,512]{2,1,0:T(8,128)} %copy.40), calls=%async_computation.1 | async-start | bytes 524288 | tf_op jit(solution)/shard_map/all_to_all | solution.py:423
  122.7 13.5 %copy-start.8 = (bf16[1,128,1024]{1,2,0:T(8,128)(2,1)S(1)}, bf16[1,128,1024]{1,2,0:T(8,128)(2,1)}, u32[]{:S(2)}) copy-start(bf16[1,128,1024]{1,2,0:T(8,128)(2,1)} %copy-done.7) | copy-start | bytes 786436
  122.7 13.5 %copy-start.10 = (bf16[1,128,1024]{1,2,0:T(8,128)(2,1)S(1)}, bf16[1,128,1024]{1,2,0:T(8,128)(2,1)}, u32[]{:S(2)}) copy-start(bf16[1,128,1024]{1,2,0:T(8,128)(2,1)} %copy-done.9) | copy-start | bytes 786436
  122.7 111.6 %all-to-all-start.2 = ((bf16[128,256,128]{2,1,0:T(8,128)(2,1)}), bf16[128,256,128]{2,1,0:T(8,128)(2,1)}, u32[]{:S(2)}, u32[]{:S(2)}) async-start(bf16[128,256,128]{2,1,0:T(8,128)(2,1)} %get-tuple-element.15), calls=%async_computation.2 | async-start | bytes 16777216 | tf_op jit(solution)/shard_map/all_to_all | solution.py:439
  143.2 2.2 copy-start
  234.3 10.9 %copy-start.15 = (f32[8]{0:T(128)S(1)}, f32[8]{0:T(128)}, u32[]{:S(2)}) copy-start(f32[8]{0:T(128)} %param.16) | copy-start | bytes 100
  237.7 15.9 %all-to-all-start.3 = ((f32[4,32,384]{2,0,1:T(4,128)}), f32[4,32,384]{2,0,1:T(4,128)S(1)}, u32[]{:S(2)}, u32[]{:S(2)}) async-start(f32[4,32,384]{2,0,1:T(4,128)} %copy.48), calls=%async_computation.3 | async-start | bytes 393216 | tf_op jit(solution)/shard_map/all_to_all | solution.py:442
  253.6 60.9 %all-to-all-start.4 = ((bf16[128,128,128]{2,1,0:T(8,128)(2,1)}), bf16[128,128,128]{2,1,0:T(8,128)(2,1)}, u32[]{:S(2)}, u32[]{:S(2)}) async-start(bf16[128,128,128]{2,1,0:T(8,128)(2,1)} %copy-done.1), calls=%async_computation.4 | async-start | bytes 8388608 | tf_op jit(solution)/shard_map/all_to_all | solution.py:443
  259.2 28.7 %copy-start.3 = (s32[128,512]{1,0:T(8,128)S(1)}, s32[128,512]{1,0:T(8,128)}, u32[]{:S(2)}) copy-start(s32[128,512]{1,0:T(8,128)} %copy-done.2) | copy-start | bytes 786436
  (5 other events, 7.0 us)
Sparse Core Ops, SparseCore 0:
  9.6 58.1 all-gather.1

commit v7 on v6

--- a/solution.py
+++ b/solution.py
@@ -260,6 +260,22 @@
     )(codes, codes, keys, queries, through)
 
 
+def after_kernel(*refs):
+    pass
+
+
+def after(ready, *arrays):
+    count = len(arrays)
+    return pl.pallas_call(
+        after_kernel,
+        in_specs=[pl.BlockSpec(memory_space=pl.ANY)] * (count + 1),
+        out_specs=[pl.BlockSpec(memory_space=pl.ANY)] * count,
+        out_shape=[jax.ShapeDtypeStruct(one.shape, one.dtype) for one in arrays],
+        input_output_aliases={i + 1: i for i in range(count)},
+        name="after",
+    )(ready, *arrays)
+
+
 def join_kernel(a_ref, _, __, out_ref):
     out_ref[...] = a_ref[...]
 
@@ -403,6 +419,12 @@
     middle = mem_keys.shape[0] // 2
     below = lax.ppermute(mem_keys, "seq", up)
     above = lax.ppermute(mem_keys, "seq", down)
+    own = jnp.concatenate([keys[0], values[0]], axis=1)
+    seen = lax.all_gather(own, "seq", axis=0, tiled=True)
+
+    lookups = knn_index[0].transpose(1, 0, 2).reshape(TOK * HEADS * TOPK // ROWS, ROWS)
+    asked, places = route(lookups, block_slot)
+    below, above = after(asked, below, above)
     far = jnp.concatenate(
         [lax.ppermute(below[:middle], "seq", up), lax.ppermute(above[middle:], "seq", down)], axis=0
     )
@@ -410,13 +432,6 @@
     line_keys = jnp.zeros((planes * MEM_DEV, HEADS * HEAD), mem_keys.dtype)
     for back, rows in enumerate((mem_keys, below, far, above)):
         line_keys = lax.dynamic_update_slice_in_dim(line_keys, rows, (place - back) % planes * MEM_DEV, axis=0)
-    own = jnp.concatenate([keys[0], values[0]], axis=1)
-    blocks = [own] + [
-        lax.ppermute(own, "seq", [(i, i + back) for i in range(planes - back)]) for back in range(1, planes)
-    ]
-
-    lookups = knn_index[0].transpose(1, 0, 2).reshape(TOK * HEADS * TOPK // ROWS, ROWS)
-    asked, places = route(lookups, block_slot)
     wanted = lax.all_to_all(
         asked.reshape(planes, near, CAP + 128), "mem", split_axis=1, concat_axis=1, tiled=True
     )
@@ -424,15 +439,12 @@
     wanted = wanted.reshape(DEVS, CAP + 128)
 
     query = queries[0].reshape(TOK, HEADS, HEAD)
-    seen = jnp.concatenate(blocks, axis=0)
     key_rows = seen[:, : HEADS * HEAD].reshape(-1, HEADS, HEAD)
     value_rows = seen[:, HEADS * HEAD :].reshape(-1, HEADS, HEAD)
     local = jnp.einsum("qhd,khd->hqk", query, key_rows, preferred_element_type=jnp.float32) * HEAD ** (-0.5)
-    back = jnp.arange(seen.shape[0], dtype=jnp.int32) // TOK
-    within = jnp.arange(seen.shape[0], dtype=jnp.int32) % TOK
-    here = (back == 0)[None, :] & (within[None, :] <= jnp.arange(TOK, dtype=jnp.int32)[:, None])
-    earlier = (back > 0) & (back <= lax.axis_index("seq"))
-    local = jnp.where((here | earlier[None, :])[None], local, -jnp.inf)
+    query_pos = lax.axis_index("seq") * TOK + jnp.arange(TOK, dtype=jnp.int32)
+    key_pos = jnp.arange(seen.shape[0], dtype=jnp.int32)
+    local = jnp.where(key_pos[None, None, :] <= query_pos[None, :, None], local, -jnp.inf)
     probs = jax.nn.softmax(local, axis=-1).astype(jnp.bfloat16)
     local_out = jnp.einsum("hqk,khd->hqd", probs, value_rows, preferred_element_type=jnp.float32)
     picked, later = pick(codes, mem_values, line_keys)

time: 341 us -> 339 us (level)
  starting transfers between devices: 55.8 us -> 40.2 us
  waiting for transfers between devices: 24.7 us -> 38.1 us
    ppermute x3 -> x0, starting transfers between devices: 9.31 us -> none  [shards(): lax.ppermute(own, 'seq', [(i, i + back) for i in range(planes - back)])]
    ppermute x1, waiting for transfers between devices: 0.01 us -> 8.76 us  [shards(): below = lax.ppermute(mem_keys, 'seq', up)]
    all_to_all x1, starting transfers between devices: 13.4 us -> 5.84 us  [shards(): first = send(picked)]
    all_to_all x1, waiting for transfers between devices: 0.01 us -> 5.33 us  [shards(): lax.all_to_all(asked.reshape(planes, near, CAP + 128), 'mem', split_axis=...]
    unnamed x35 -> x31, local copies, waits for them, and re-layouts: 8.66 us -> 9.24 us
  transfers between devices with their start and end apart: 13 -> 11, of which waited for: 3 -> 5; matrix products, arithmetic and copies ran while one was open for 7% -> 6% of each run, Pallas kernels for 56% -> 57%
where the time goes in v7:
time: 339 us; the launch traced here: 338 us
  Pallas kernels  208 us (61%)
  starting transfers between devices  40.2 us (12%)
  waiting for transfers between devices  38.1 us (11%)
  local copies, waits for them, and re-layouts  26.4 us (8%)
  between operations  13.8 us (4%)
  matrix products  7.92 us (2%)
    pallas_call x1, Pallas kernels, score(): pl.pallas_call(score_kernel, grid=(DEVS // GROUP,), in_specs=specs + [pl....  73 us
    pallas_call x1, Pallas kernels, pick(): pl.pallas_call(pick_kernel, grid=(DEVS // PICK,), in_specs=specs + [pl.Bl...  40.7 us
    pallas_call x2, Pallas kernels, mix(): pl.pallas_call(functools.partial(mix_kernel, begin=begin), grid=(DEVS //...  40.2 us
    pallas_call x1, Pallas kernels, weigh(): pl.pallas_call(weigh_kernel, out_shape=jax.ShapeDtypeStruct((DEVS, CAP),...  28.7 us
    pallas_call x1, Pallas kernels, route(): pl.pallas_call(route_kernel, out_shape=[jax.ShapeDtypeStruct((DEVS, CAP +...  22.1 us
    all_to_all x1, waiting for transfers between devices, shards(): first = send(picked)  13.5 us
    all_to_all x1, starting transfers between devices, shards(): lax.all_to_all(asked.reshape(planes, near, CAP + 128), 'mem', split_axis=...  10.2 us
    unnamed x31, local copies, waits for them, and re-layouts  9.24 us
  transfers between devices with their start and end apart: 11, of which 5 were waited for; matrix products, arithmetic and copies ran while one was open for 6% of the time, Pallas kernels for 57%

profile of v7, /device:TPU:1, one launch (start us, length us, event | category | flops | bytes accessed | tf_op | source)
XLA Modules:
  0.0 337.5 jit_solution(12988387992216328689)
XLA Ops:
  11.4 2.5 collective-permute-start
  14.0 2.2 collective-permute-start.1
  17.5 22.1 %route.1 = (s32[128,512]{1,0:T(8,128)S(1)}, s32[128,256]{1,0:T(8,128)S(1)}) custom-call(s32[128,256]{1,0:T(8,128)S(1)} %reshape.68.look_ref, s32[8,128]{1,0:T(8,128)S(1)} %bitcast.39), custom_call_target="tpu_custom_call" | custom-call | flops 22000001024 | bytes 22000000 | tf_op jit(solution)/shard_map/route/pallas_call | solution.py:104
  40.3 8.8 %collective-permute-done.refs_1_ = bf16[512,1024]{1,0:T(8,128)(2,1)S(1)} collective-permute-done((bf16[512,1024]{1,0:T(8,128)(2,1)}, bf16[512,1024]{1,0:T(8,128)(2,1)S(1)}, u32[]{:S(2)}, u32[]{:S(2)}) %collective-permute-start) | collective-permute-done | bytes 1048608 | tf_op jit(solution)/shard_map/ppermute | solution.py:420
  54.3 2.7 collective-permute-start.3
  57.8 10.2 %all-to-all-start = ((s32[4,32,512]{2,0,1:T(4,128)}), s32[4,32,512]{2,0,1:T(4,128)S(1)}, u32[]{:S(2)}, u32[]{:S(2)}) async-start(s32[4,32,512]{2,0,1:T(4,128)} %copy.41), calls=%async_computation | async-start | bytes 524288 | tf_op jit(solution)/shard_map/all_to_all | solution.py:435
  68.2 2.5 broadcast_in_dim.23
  71.7 5.3 %all-to-all-done = s32[4,32,512]{2,0,1:T(4,128)S(1)} async-done(((s32[4,32,512]{2,0,1:T(4,128)}), s32[4,32,512]{2,0,1:T(4,128)S(1)}, u32[]{:S(2)}, u32[]{:S(2)}) %all-to-all-start) | async-done | bytes 262176 | tf_op jit(solution)/shard_map/all_to_all | solution.py:435
  77.9 3.6 %all-to-all-start.1 = ((s32[4,32,512]{2,1,0:T(8,128)}), s32[4,32,512]{2,1,0:T(8,128)S(1)}, u32[]{:S(2)}, u32[]{:S(2)}) async-start(s32[4,32,512]{2,1,0:T(8,128)} %copy.42), calls=%async_computation.1 | async-start | bytes 524288 | tf_op jit(solution)/shard_map/all_to_all | solution.py:438
  82.6 2.1 maximum_dynamic-update-slice_fusion
  85.7 2.1 all-to-all-done.1
  87.9 40.7 %pick.1 = (bf16[128,256,128]{2,1,0:T(8,128)(2,1)}, bf16[128,128,128]{2,1,0:T(8,128)(2,1)}) custom-call(s32[128,512]{1,0:T(8,128)S(1)} %bitcast.36, s32[128,512]{1,0:T(8,128)S(1)} %bitcast.37, bf16[512,1024]{1,0:T(8,128)(2,1)S(1)} %copy-done.5, bf16[2048,1024]{1,0:T(8,128)(2,1)} %constant_dynamic-update-slice_fusion._.key_ref), custom_call_target="tpu_custom_call" | custom-call | flops 40000000000 | bytes 40000000 | tf_op jit(solution)/shard_map/pick/pallas_call | solution.py:214
  128.5 5.8 %all-to-all-start.2 = ((bf16[128,256,128]{2,1,0:T(8,128)(2,1)}), bf16[128,256,128]{2,1,0:T(8,128)(2,1)}, u32[]{:S(2)}, u32[]{:S(2)}) async-start(bf16[128,256,128]{2,1,0:T(8,128)(2,1)} %get-tuple-element.19), calls=%async_computation.2 | async-start | bytes 16777216 | tf_op jit(solution)/shard_map/all_to_all | solution.py:451
  136.2 2.2 fusion.19
  141.4 2.2 copy-done
  143.6 73.0 %score.1 = (f32[128,384]{1,0:T(8,128)S(1)}, bf16[128,128,128]{2,1,0:T(8,128)(2,1)S(1)}) custom-call(s32[128,512]{1,0:T(8,128)} %bitcast.4.code_ref.start_ref, s32[128,512]{1,0:T(8,128)} %bitcast.4.code_ref.start_ref, bf16[2048,1024]{1,0:T(8,128)(2,1)} %constant_dynamic-update-slice_fusion._.key_ref, ...), custom_call_target="tpu_custom_call", output_to_operand_aliasing={{1}: (4, {})} | custom-call | flops 74999996416 | bytes 75000000 | tf_op jit(solution)/shard_map/score/pallas_call | solution.py:241
  219.2 13.5 %all-to-all-done.2._.value_ref = bf16[128,256,128]{2,1,0:T(8,128)(2,1)} async-done(((bf16[128,256,128]{2,1,0:T(8,128)(2,1)}), bf16[128,256,128]{2,1,0:T(8,128)(2,1)}, u32[]{:S(2)}, u32[]{:S(2)}) %all-to-all-start.2) | async-done | bytes 8388640 | tf_op jit(solution)/shard_map/all_to_all | solution.py:451
  236.1 7.6 %all-to-all-start.3 = ((f32[4,32,384]{2,0,1:T(4,128)}), f32[4,32,384]{2,0,1:T(4,128)S(1)}, u32[]{:S(2)}, u32[]{:S(2)}) async-start(f32[4,32,384]{2,0,1:T(4,128)} %copy.50), calls=%async_computation.3 | async-start | bytes 393216 | tf_op jit(solution)/shard_map/all_to_all | solution.py:454
  243.7 8.3 %all-to-all-done.3 = f32[4,32,384]{2,0,1:T(4,128)S(1)} async-done(((f32[4,32,384]{2,0,1:T(4,128)}), f32[4,32,384]{2,0,1:T(4,128)S(1)}, u32[]{:S(2)}, u32[]{:S(2)}) %all-to-all-start.3) | async-done | bytes 196640 | tf_op jit(solution)/shard_map/all_to_all | solution.py:454
  252.0 5.6 %all-to-all-start.4 = ((bf16[128,128,128]{2,1,0:T(8,128)(2,1)}), bf16[128,128,128]{2,1,0:T(8,128)(2,1)}, u32[]{:S(2)}, u32[]{:S(2)}) async-start(bf16[128,128,128]{2,1,0:T(8,128)(2,1)} %copy-done.1), calls=%async_computation.4 | async-start | bytes 8388608 | tf_op jit(solution)/shard_map/all_to_all | solution.py:455
  257.6 28.7 %weigh.1.weight_ref = f32[128,384]{1,0:T(8,128)S(1)} custom-call(s32[128,256]{1,0:T(8,128)S(1)} %get-tuple-element.14.place_ref, f32[128,384]{1,0:T(8,128)S(1)} %bitcast.38), custom_call_target="tpu_custom_call" | custom-call | flops 22000001024 | bytes 22000000 | tf_op jit(solution)/shard_map/weigh/pallas_call | solution.py:347
  286.3 26.6 %mix.2 = f32[512,256]{1,0:T(8,128)S(1)} custom-call(s32[128,512]{1,0:T(8,128)S(1)} %copy-done.3, s32[128,512]{1,0:T(8,128)S(1)} %copy-done.3, f32[128,384]{1,0:T(8,128)S(1)} %weigh.1.weight_ref, bf16[128,256,128]{2,1,0:T(8,128)(2,1)} %all-to-all-done.2._.value_ref), custom_call_target="tpu_custom_call" | custom-call | flops 24000000000 | bytes 24000000 | tf_op jit(solution)/shard_map/mix/pallas_call | solution.py:389
  312.9 13.5 %mix.3 = f32[512,256]{1,0:T(8,128)S(1)} custom-call(s32[128,512]{1,0:T(8,128)S(1)} %copy-done.3, s32[128,512]{1,0:T(8,128)S(1)} %copy-done.3, f32[128,384]{1,0:T(8,128)S(1)} %weigh.1.weight_ref, bf16[128,128,128]{2,1,0:T(8,128)(2,1)} %all-to-all-done.4.value_ref), custom_call_target="tpu_custom_call" | custom-call | flops 12000000000 | bytes 12000000 | tf_op jit(solution)/shard_map/mix/pallas_call | solution.py:389
  327.0 3.7 %fusion.1 = bf16[1,128,2048]{2,1,0:T(8,128)(2,1)} fusion(bf16[128,1024]{0,1:T(8,128)(2,1)S(1)} %bitcast.43, bf16[1024,2048]{1,0:T(8,128)(2,1)} %param.17), kind=kOutput, calls=%fused_computation.2 | convolution fusion | flops 537133056 | bytes 4980736 | tf_op jit(solution)/shard_map/dot_general | solution.py:463
  (67 shorter events, 28.3 us)
Async XLA Ops:
  6.5 11.0 %copy-start.6 = (s32[1024]{0:T(1024)S(1)}, s32[1024]{0:T(1024)}, u32[]{:S(2)}) copy-start(s32[1024]{0:T(1024)} %param.15) | copy-start | bytes 12292
  6.5 128.0 %all-gather.5.cloned.1.call-start = ((), (), s32[]{:S(2)}) async-start(), calls=%async_computation.6 | async-start | bytes 2621440 | tf_op jit(solution)/shard_map/all_gather | solution.py:423
  9.7 131.7 %all-gather.3.cloned.1.call-start = ((), (), s32[]{:S(2)}) async-start(), calls=%async_computation.5 | async-start | bytes 8650752 | tf_op jit(solution)/shard_map/all_gather | solution.py:416
  11.4 37.6 %collective-permute-start = (bf16[512,1024]{1,0:T(8,128)(2,1)}, bf16[512,1024]{1,0:T(8,128)(2,1)S(1)}, u32[]{:S(2)}, u32[]{:S(2)}) collective-permute-start(bf16[512,1024]{1,0:T(8,128)(2,1)} %param.12), channel_id=1, source_target_pairs={{0,32},{32,64},{64,96},{96,0},{1,33},{33,65},{65,97},{97,1},{2,34}... | collective-permute-start | bytes 3145736 | tf_op jit(solution)/shard_map/ppermute | solution.py:420
  14.0 35.1 %collective-permute-start.1 = (bf16[512,1024]{1,0:T(8,128)(2,1)}, bf16[512,1024]{1,0:T(8,128)(2,1)S(1)}, u32[]{:S(2)}, u32[]{:S(2)}) collective-permute-start(bf16[512,1024]{1,0:T(8,128)(2,1)} %param.12), channel_id=1, source_target_pairs={{0,96},{32,0},{64,32},{96,64},{1,97},{33,1},{65,33},{97,65},{2,98}... | collective-permute-start | bytes 3145736 | tf_op jit(solution)/shard_map/ppermute | solution.py:421
  39.6 0.7 copy-start.2
  49.1 1.0 copy-start.7
  49.1 7.9 %copy-start.3 = (s32[128,512]{1,0:T(8,128)S(1)}, s32[128,512]{1,0:T(8,128)}, u32[]{:S(2)}) copy-start(s32[128,512]{1,0:T(8,128)} %copy-done.2) | copy-start | bytes 786436
  49.1 1.4 copy-start.9
  50.5 20.2 %copy-start.11 = (bf16[512,1024]{1,0:T(8,128)(2,1)S(1)}, bf16[512,1024]{1,0:T(8,128)(2,1)}, u32[]{:S(2)}) copy-start(bf16[512,1024]{1,0:T(8,128)(2,1)} %param.12) | copy-start | bytes 3145732
  52.4 30.2 %collective-permute-start.2 = (bf16[256,1024]{1,0:T(8,128)(2,1)}, bf16[256,1024]{1,0:T(8,128)(2,1)S(1)}, u32[]{:S(2)}, u32[]{:S(2)}) collective-permute-start(bf16[256,1024]{1,0:T(8,128)(2,1)} %slice.18), channel_id=1, source_target_pairs={{0,32},{32,64},{64,96},{96,0},{1,33},{33,65},{65,97},{97,1},{2,34}... | collective-permute-start | bytes 1572872 | tf_op jit(solution)/shard_map/ppermute | solution.py:429
  54.3 28.3 %collective-permute-start.3 = (bf16[256,1024]{1,0:T(8,128)(2,1)}, bf16[256,1024]{1,0:T(8,128)(2,1)}, u32[]{:S(2)}, u32[]{:S(2)}) collective-permute-start(bf16[256,1024]{1,0:T(8,128)(2,1)} %slice.19), channel_id=1, source_target_pairs={{0,96},{32,0},{64,32},{96,64},{1,97},{33,1},{65,33},{97,65},{2,98}... | collective-permute-start | bytes 1572872 | tf_op jit(solution)/shard_map/ppermute | solution.py:429
  57.0 24.5 %copy-start.8 = (bf16[512,1024]{1,0:T(8,128)(2,1)S(1)}, bf16[512,1024]{1,0:T(8,128)(2,1)}, u32[]{:S(2)}) copy-start(bf16[512,1024]{1,0:T(8,128)(2,1)} %get-tuple-element.15) | copy-start | bytes 3145732
  57.8 19.2 %all-to-all-start = ((s32[4,32,512]{2,0,1:T(4,128)}), s32[4,32,512]{2,0,1:T(4,128)S(1)}, u32[]{:S(2)}, u32[]{:S(2)}) async-start(s32[4,32,512]{2,0,1:T(4,128)} %copy.41), calls=%async_computation | async-start | bytes 524288 | tf_op jit(solution)/shard_map/all_to_all | solution.py:435
  71.7 16.1 %copy-start.5 = (bf16[512,1024]{1,0:T(8,128)(2,1)S(1)}, bf16[512,1024]{1,0:T(8,128)(2,1)}, u32[]{:S(2)}) copy-start(bf16[512,1024]{1,0:T(8,128)(2,1)} %value_ref.1) | copy-start | bytes 3145732
  77.9 10.0 %all-to-all-start.1 = ((s32[4,32,512]{2,1,0:T(8,128)}), s32[4,32,512]{2,1,0:T(8,128)S(1)}, u32[]{:S(2)}, u32[]{:S(2)}) async-start(s32[4,32,512]{2,1,0:T(8,128)} %copy.42), calls=%async_computation.1 | async-start | bytes 524288 | tf_op jit(solution)/shard_map/all_to_all | solution.py:438
  81.5 3.2 copy-start.10
  128.5 5.9 %copy-start.12 = (bf16[1,128,1024]{2,1,0:T(8,128)(2,1)S(1)}, bf16[1,128,1024]{2,1,0:T(8,128)(2,1)}, u32[]{:S(2)}) copy-start(bf16[1,128,1024]{2,1,0:T(8,128)(2,1)} %param.9) | copy-start | bytes 786436
  128.5 104.2 %all-to-all-start.2 = ((bf16[128,256,128]{2,1,0:T(8,128)(2,1)}), bf16[128,256,128]{2,1,0:T(8,128)(2,1)}, u32[]{:S(2)}, u32[]{:S(2)}) async-start(bf16[128,256,128]{2,1,0:T(8,128)(2,1)} %get-tuple-element.19), calls=%async_computation.2 | async-start | bytes 16777216 | tf_op jit(solution)/shard_map/all_to_all | solution.py:451
  141.4 2.2 copy-start
  216.6 2.0 copy-start.1
  232.7 10.9 %copy-start.13 = (f32[8]{0:T(128)S(1)}, f32[8]{0:T(128)}, u32[]{:S(2)}) copy-start(f32[8]{0:T(128)} %param.16) | copy-start | bytes 100
  236.1 15.9 %all-to-all-start.3 = ((f32[4,32,384]{2,0,1:T(4,128)}), f32[4,32,384]{2,0,1:T(4,128)S(1)}, u32[]{:S(2)}, u32[]{:S(2)}) async-start(f32[4,32,384]{2,0,1:T(4,128)} %copy.50), calls=%async_computation.3 | async-start | bytes 393216 | tf_op jit(solution)/shard_map/all_to_all | solution.py:454
  252.0 60.9 %all-to-all-start.4 = ((bf16[128,128,128]{2,1,0:T(8,128)(2,1)}), bf16[128,128,128]{2,1,0:T(8,128)(2,1)}, u32[]{:S(2)}, u32[]{:S(2)}) async-start(bf16[128,128,128]{2,1,0:T(8,128)(2,1)} %copy-done.1), calls=%async_computation.4 | async-start | bytes 8388608 | tf_op jit(solution)/shard_map/all_to_all | solution.py:455
  (1 other events, 0.7 us)
Sparse Core Ops, SparseCore 0:
  9.8 50.5 all-gather.4
  62.7 54.5 all-gather.2
